TPU v7x, 32 devices: a whole 2x2x4 slice. The times are simulated.
32 devices in a mesh: group: 4 (over x, core), dp: 8 (over z, y).
Axes of the slice: x: 2, y: 2, z: 4, core: 2. Of those that a mesh axis runs over, the one named last changes fastest.
Arguments:
- query_hidden: bfloat16 [256, 32, 768], P(('dp', 'group')), may hold values from -6 to 6
- passage_hidden: bfloat16 [512, 128, 768], P(('dp', 'group')), may hold values from -6 to 6
- projection: bfloat16 [768, 128], replicated, may hold values from -0.21875 to 0.21875
- positive: int32 [256], P(('dp', 'group')), may hold values from 0 to 63
- hard_ids: int32 [256, 32], P(('dp', 'group')), may hold values from -1 to 63, as said below
- passage_len: int32 [512], P(('dp', 'group')), may hold values from 16 to 128, as said below
Outputs:
- losses: float32 [256], P(('dp', 'group'))
- grad_proj: float32 [768, 128], replicated
- grad_query: bfloat16 [256, 32, 768], P(('dp', 'group'))
- grad_passage: bfloat16 [512, 128, 768], P(('dp', 'group'))
Inputs may be any that keep to these rules, and one draw needn't show every extreme that they name: A passage's first passage_len tokens are live, the rest padding. `hard_ids`: A query's filled slots come first, from 8 to 32 of them; the rest hold -1. Slots may repeat a passage or name the positive.
All inputs are finite; a program needn't handle non-finite values.
Results may differ from a plain program's by a relative error of at most 0.017.
Values may be sent and summed in bfloat16 or wider, within the bound.
No kernel may reach another device: no remote copies, remote signals or barrier semaphores. Data moves between devices by JAX's collectives and lax.ppermute only.
A program may use at most 64 MiB of HBM per device.

v0:
```python
import jax
import jax.numpy as jnp
from jax import lax
from jax.sharding import PartitionSpec as P

smooth_temp = 0.1
norm_eps = 1e-06


def normalize(projected):
    return projected * lax.rsqrt(jnp.sum(projected * projected, axis=-1, keepdims=True) + norm_eps)


def contract_last(left, right):
    return lax.dot_general(
        left, right, (((1,), (1,)), ((), ())), preferred_element_type=jnp.float32
    )


def contract_first(left, right):
    return lax.dot_general(
        left, right, (((0,), (0,)), ((), ())), preferred_element_type=jnp.float32
    )


def smooth_scores(query_rows, passage_rows, usable):
    similar = contract_last(query_rows, passage_rows)
    similar = similar.reshape(similar.shape[0], usable.shape[0], usable.shape[1])
    summed = jnp.sum(jnp.where(usable[None], jnp.exp(similar / smooth_temp), 0.0), axis=-1)
    return smooth_temp * jnp.log(summed)


def token_grads(query_rows, passage_rows, usable, smooth, weights):
    similar = contract_last(query_rows, passage_rows)
    similar = similar.reshape(similar.shape[0], usable.shape[0], usable.shape[1])
    shares = jnp.where(
        usable[None], jnp.exp(similar / smooth_temp - smooth[:, :, None] / smooth_temp), 0.0
    )
    coefficient = (weights[:, :, None] * shares).astype(jnp.bfloat16)
    coefficient = coefficient.reshape(query_rows.shape[0], passage_rows.shape[0])
    query_part = jnp.dot(coefficient, passage_rows, preferred_element_type=jnp.float32)
    passage_part = contract_first(coefficient, query_rows)
    return (query_part, passage_part)


def hard_counts(hard_ids, pool_size):
    columns = jnp.arange(pool_size, dtype=jnp.int32)
    return jnp.sum((hard_ids[:, :, None] == columns[None, None, :]).astype(jnp.float32), axis=1)


def finish_loss(scores, positive, hard_ids, total_slots):
    counts = hard_counts(hard_ids, scores.shape[1])
    boost = scores.shape[1] / hard_ids.shape[1]
    hard_total = lax.psum(jnp.sum(counts * jnp.exp(scores)), ("group", "dp"))
    hard_mean = hard_total / total_slots
    columns = jnp.arange(scores.shape[1], dtype=jnp.int32)
    chosen = positive[:, None] == columns[None, :]
    pos_score = jnp.sum(jnp.where(chosen, scores, 0.0), axis=1, keepdims=True)
    reweight = 1.0 + jnp.where(chosen, 0.0, boost * counts * jnp.exp(scores - jnp.log(hard_mean)))
    weighted = reweight * jnp.exp(scores - pos_score)
    partition = jnp.sum(weighted, axis=1, keepdims=True)
    losses = jnp.log(partition[:, 0])
    score_grad = weighted / partition - chosen.astype(jnp.float32)
    return (losses, score_grad)


def local(query_hidden, passage_hidden, projection, positive, hard_ids, passage_len):
    query_count = query_hidden.shape[0]
    query_len = query_hidden.shape[1]
    hidden_width = query_hidden.shape[2]
    passage_count = passage_hidden.shape[0]
    passage_tokens = passage_hidden.shape[1]
    embed_width = projection.shape[1]
    groups = lax.axis_size("group")
    total_slots = query_count * groups * lax.axis_size("dp") * hard_ids.shape[1]
    block_rows = query_count * query_len
    query_flat = query_hidden.reshape(block_rows, hidden_width)
    passage_flat = passage_hidden.reshape(passage_count * passage_tokens, hidden_width)
    query_pre = jnp.dot(query_flat, projection, preferred_element_type=jnp.float32)
    passage_pre = jnp.dot(passage_flat, projection, preferred_element_type=jnp.float32)
    query_embed = normalize(query_pre).astype(jnp.bfloat16)
    passage_embed = normalize(passage_pre).astype(jnp.bfloat16)
    token_index = jnp.arange(passage_tokens, dtype=jnp.int32)
    gathered = lax.all_gather(query_embed, "group", axis=0, tiled=True)
    query_blocks = gathered.reshape(groups, block_rows, embed_width)
    usable = token_index[None, :] < passage_len[:, None]
    smooth_blocks = lax.map(
        lambda query_block: smooth_scores(query_block, passage_embed, usable), query_blocks
    )
    local_scores = jnp.sum(
        smooth_blocks.reshape(groups * query_count, query_len, passage_count), axis=1
    )
    scores = lax.all_to_all(local_scores, "group", split_axis=0, concat_axis=1, tiled=True)
    losses, score_grad = finish_loss(scores, positive, hard_ids, total_slots)
    returned = lax.all_to_all(score_grad, "group", split_axis=1, concat_axis=0, tiled=True)
    weight_blocks = jnp.repeat(returned, query_len, axis=0).reshape(
        groups, block_rows, passage_count
    )

    def backward_block(running, members):
        query_part, passage_part = token_grads(
            members[0], passage_embed, usable, members[1], members[2]
        )
        rounded = lax.optimization_barrier(passage_part.astype(jnp.bfloat16))
        return (running + rounded.astype(jnp.float32), query_part)

    initial = jnp.zeros((passage_count * passage_tokens, embed_width), jnp.float32)
    passage_grad, query_parts = lax.scan(
        backward_block, initial, (query_blocks, smooth_blocks, weight_blocks)
    )
    query_grad = lax.psum_scatter(
        query_parts.reshape(groups * block_rows, embed_width).astype(jnp.bfloat16),
        "group",
        scatter_dimension=0,
        tiled=True,
    ).astype(jnp.float32)
    query_back = jax.vjp(normalize, query_pre)[1](query_grad)[0].astype(jnp.bfloat16)
    passage_back = jax.vjp(normalize, passage_pre)[1](passage_grad)[0].astype(jnp.bfloat16)
    grad_query = (
        contract_last(query_back, projection)
        .astype(jnp.bfloat16)
        .reshape(query_count, query_len, hidden_width)
    )
    grad_passage = (
        contract_last(passage_back, projection)
        .astype(jnp.bfloat16)
        .reshape(passage_count, passage_tokens, hidden_width)
    )
    local_weight = contract_first(query_flat, query_back) + contract_first(
        passage_flat, passage_back
    )
    grad_proj = lax.psum(local_weight, ("group", "dp"))
    return (losses, grad_proj, grad_query, grad_passage)


def solution(mesh):
    in_specs = (
        P(("dp", "group"), None, None),
        P(("dp", "group"), None, None),
        P(),
        P(("dp", "group")),
        P(("dp", "group"), None),
        P(("dp", "group")),
    )
    out_specs = (
        P(("dp", "group")),
        P(),
        P(("dp", "group"), None, None),
        P(("dp", "group"), None, None),
    )
    return jax.shard_map(local, mesh=mesh, in_specs=in_specs, out_specs=out_specs, check_vma=False)
```

profile of v0, /device:TPU:1, one launch (start us, length us, event | category | flops | bytes accessed | tf_op | source)
XLA Modules:
  0.0 278.2 jit_solution(1150926679223699270)
XLA Ops:
  8.7 7.6 %all_gather.3 = bf16[1024,128]{0,1:T(8,128)(2,1)} all-gather(bf16[256,128]{0,1:T(8,128)(2,1)S(1)} %multiply_convert_fusion.2), channel_id=1, replica_groups=mesh['group'=4,'dp'=8] {'group'}, dimensions={0}, use_global_device_ids=true | all-gather | bytes 327680 | tf_op jit(solution)/shard_map/all_gather | solution.py:84
  16.3 1.8 copy.71
  18.1 2.1 multiply_reduce_fusion.1
  22.0 2.1 copy.57
  24.1 7.2 %while.24 = (s32[]{:T(128)}, f32[4,256,16]{1,2,0:T(8,128)S(1)}, bf16[4,256,128]{2,1,0:T(8,128)(2,1)}, bf16[2048,128]{1,0:T(8,128)(2,1)}, s32[16]{0:T(128)S(1)}, /*index=5*/s32[]{:T(128)}) while((s32[]{:T(128)}, f32[4,256,16]{1,2,0:T(8,128)S(1)}, bf16[4,256,128]{2,1,0:T(8,128)(2,1)}, bf16[2048,128]{1,0:T(8,128)(2,1)}, ...), condition=%wide.region_5.6_spmd.clone, body=%wide.region_3.0_spmd.clone.sunk | while | flops 135792640 | bytes 643221 | solution.py:87
  26.0 1.7 select_reduce_fusion.2
  34.0 3.4 %all-to-all-start = ((f32[4,1,128]{2,1,0:T(1,128)}), f32[4,1,128]{2,1,0:T(1,128)S(1)}, u32[]{:S(2)}, u32[]{:S(2)}) async-start(f32[4,1,128]{2,1,0:T(1,128)} %reshape.153), calls=%async_computation | async-start | bytes 4096 | tf_op jit(solution)/shard_map/all_to_all | solution.py:93
  37.6 2.8 all-to-all-done
  42.4 39.2 %psum.14 = f32[]{:T(128)} all-reduce(f32[]{:T(128)} %get-tuple-element.205), channel_id=1, replica_groups=mesh['group'=4,'dp'=8] {'group','dp'}, use_global_device_ids=true, to_apply=%region_8.9 | all-reduce | flops 1 | bytes 8 | tf_op jit(solution)/shard_map/psum | solution.py:54
  83.2 4.8 %all-to-all-start.1 = ((f32[4,1,128]{2,1,0:T(1,128)}), f32[4,1,128]{2,1,0:T(1,128)S(1)}, u32[]{:S(2)}, u32[]{:S(2)}) async-start(f32[4,1,128]{2,1,0:T(1,128)} %reshape.155), calls=%async_computation.1 | async-start | bytes 4096 | tf_op jit(solution)/shard_map/all_to_all | solution.py:95
  88.6 2.4 all-to-all-done.1
  93.7 20.6 %while.25 = (s32[]{:T(128)}, f32[2048,128]{1,0:T(8,128)}, bf16[4,256,128]{2,1,0:T(8,128)(2,1)}, f32[4,256,16]{1,0,2:T(4,128)S(1)}, bf16[4,256,128]{2,1,0:T(8,128...) while((s32[]{:T(128)}, f32[2048,128]{1,0:T(8,128)}, ...), condition=%wide.region_12.13_spmd.clone, body=%wide.region_11.12_spmd.clone.sunk | while | flops 406329344 | bytes 20320600 | solution.py:108
  93.9 1.8 multiply_convert_fusion.4
  99.1 1.8 multiply_convert_fusion.4
  104.2 1.8 multiply_convert_fusion.4
  109.3 1.8 multiply_convert_fusion.4
  114.4 1.8 copy.70
  116.3 2.6 copy.67
  118.9 1.8 multiply_reduce_fusion
  121.2 2.7 convolution_convert_fusion.1
  125.2 10.7 %reduce-scatter.2.cloned.1.call-done = bf16[256,128]{0,1:T(8,128)(2,1)} async-done(((bf16[1024,128]{0,1:T(8,128)(2,1)}), bf16[256,128]{0,1:T(8,128)(2,1)}) %reduce-scatter.2.cloned.1.call-update) | async-done | bytes 65552 | tf_op jit(solution)/shard_map/reduce_scatter | solution.py:111
  137.7 2.1 fusion.14
  140.9 128.6 %all-reduce.2.cloned.1.call-done = f32[768,128]{0,1:T(8,128)} async-done(((f32[768,128]{0,1:T(8,128)}), f32[768,128]{0,1:T(8,128)}) %all-reduce.2.cloned.1.call-update) | async-done | bytes 393232 | tf_op jit(solution)/shard_map/psum | solution.py:132
  269.5 1.9 copy.69
  (133 shorter events, 35.7 us)
Async XLA Ops:
  7.2 10.9 %copy-start = (bf16[16,128,768]{2,1,0:T(8,128)(2,1)S(1)}, bf16[16,128,768]{2,1,0:T(8,128)(2,1)}, u32[]{:S(2)}) copy-start(bf16[16,128,768]{2,1,0:T(8,128)(2,1)} %param.11) | copy-start | bytes 9437188
  20.2 3.9 %copy-start.10 = (s32[16]{0:T(128)S(1)}, s32[16]{0:T(128)}, u32[]{:S(2)}) copy-start(s32[16]{0:T(128)} %param.15) | copy-start | bytes 196
  24.1 13.3 %copy-start.12 = (s32[8,32]{1,0:T(8,128)S(1)}, s32[8,32]{1,0:T(8,128)}, u32[]{:S(2)}) copy-start(s32[8,32]{1,0:T(8,128)} %param.14) | copy-start | bytes 3076
  24.1 17.6 %copy-start.11 = (s32[8]{0:T(128)S(1)}, s32[8]{0:T(128)}, u32[]{:S(2)}) copy-start(s32[8]{0:T(128)} %param.13) | copy-start | bytes 100
  34.0 6.3 %all-to-all-start = ((f32[4,1,128]{2,1,0:T(1,128)}), f32[4,1,128]{2,1,0:T(1,128)S(1)}, u32[]{:S(2)}, u32[]{:S(2)}) async-start(f32[4,1,128]{2,1,0:T(1,128)} %reshape.153), calls=%async_computation | async-start | bytes 4096 | tf_op jit(solution)/shard_map/all_to_all | solution.py:93
  83.2 7.8 %all-to-all-start.1 = ((f32[4,1,128]{2,1,0:T(1,128)}), f32[4,1,128]{2,1,0:T(1,128)S(1)}, u32[]{:S(2)}, u32[]{:S(2)}) async-start(f32[4,1,128]{2,1,0:T(1,128)} %reshape.155), calls=%async_computation.1 | async-start | bytes 4096 | tf_op jit(solution)/shard_map/all_to_all | solution.py:95
  88.1 47.9 %reduce-scatter.2.cloned.1.call-start = ((), (), s32[]{:S(2)}) async-start(), calls=%async_computation.3 | async-start | bytes 327680 | tf_op jit(solution)/shard_map/reduce_scatter | solution.py:111
  93.8 2.0 copy-start.3
  93.8 2.0 copy-start.8
  95.7 1.9 copy-start.1
  96.3 1.7 copy-start.9
  98.9 1.9 copy-start.3
  98.9 2.0 copy-start.8
  100.9 1.9 copy-start.1
  104.1 1.9 copy-start.3
  104.1 2.0 copy-start.8
  106.0 1.9 copy-start.1
  109.2 1.9 copy-start.3
  109.2 2.0 copy-start.8
  111.2 1.9 copy-start.1
  116.2 153.2 %all-reduce.2.cloned.1.call-start = ((), (), s32[]{:S(2)}) async-start(), calls=%async_computation.4 | async-start | bytes 786432 | tf_op jit(solution)/shard_map/psum | solution.py:132
  118.9 1.9 copy-start.5
  118.9 2.2 copy-start.6
  118.9 2.4 copy-start.7
  (8 other events, 10.0 us)
Sparse Core Ops, SparseCore 0:
  116.3 19.6 reduce-scatter.1
  142.7 126.7 all-reduce.1
where the time goes:
time: 281 us; the launch traced here: 278 us
  waiting for transfers between devices  145 us (52%)
  blocking collectives  46.7 us (17%)
  matrix products  32.1 us (11%)
  local copies, waits for them, and re-layouts  21.2 us (8%)
  between operations  14.9 us (5%)
  other arithmetic  10 us (4%)
  starting transfers between devices  8.24 us (3%)
    psum x1, waiting for transfers between devices, local(): grad_proj = lax.psum(local_weight, ('group', 'dp'))  129 us
    psum x1, blocking collectives, finish_loss(): hard_total = lax.psum(jnp.sum(counts * jnp.exp(scores)), ('group', 'dp'))  39.2 us
    dot_general x10, matrix products, contract_last(): lax.dot_general(left, right, (((1,), (1,)), ((), ())), preferred_element_...  17.7 us
    reduce_scatter x1, waiting for transfers between devices, local(): lax.psum_scatter(query_parts.reshape(groups * block_rows, embed_width).as...  10.7 us
    dot_general x6, matrix products, contract_first(): lax.dot_general(left, right, (((0,), (0,)), ((), ())), preferred_element_...  8.79 us
    unnamed x23, local copies, waits for them, and re-layouts  8.56 us
    all_gather x1, blocking collectives, local(): gathered = lax.all_gather(query_embed, 'group', axis=0, tiled=True)  7.56 us
  transfers between devices with their start and end apart: 4, of which 4 were waited for; matrix products, arithmetic and copies ran while one was open for 4% of the time, Pallas kernels for 0%

commit v1 on v0

--- a/solution.py
+++ b/solution.py
@@ -43,6 +43,24 @@
     return (query_part, passage_part)
 
 
+def sum_everywhere(value):
+    axes = ("dp", "group")
+    devices = lax.axis_size(axes)
+    rows = jnp.broadcast_to(value.reshape(1, 1, 1), (devices, 8, 128))
+    return jnp.sum(lax.all_to_all(rows, axes, 0, 0, tiled=True)[:, 0, 0])
+
+
+def sum_rows_everywhere(value):
+    axes = ("dp", "group")
+    devices = lax.axis_size(axes)
+    rows, columns = value.shape
+    parts = value.astype(jnp.bfloat16).reshape(devices, rows // devices, columns)
+    parts = lax.all_to_all(parts, axes, 0, 0, tiled=True)
+    own = jnp.sum(parts.astype(jnp.float32), axis=0).astype(jnp.bfloat16)
+    copies = jnp.broadcast_to(own[None], parts.shape)
+    return lax.all_to_all(copies, axes, 0, 0, tiled=True).reshape(rows, columns).astype(jnp.float32)
+
+
 def hard_counts(hard_ids, pool_size):
     columns = jnp.arange(pool_size, dtype=jnp.int32)
     return jnp.sum((hard_ids[:, :, None] == columns[None, None, :]).astype(jnp.float32), axis=1)
@@ -51,7 +69,7 @@
 def finish_loss(scores, positive, hard_ids, total_slots):
     counts = hard_counts(hard_ids, scores.shape[1])
     boost = scores.shape[1] / hard_ids.shape[1]
-    hard_total = lax.psum(jnp.sum(counts * jnp.exp(scores)), ("group", "dp"))
+    hard_total = sum_everywhere(jnp.sum(counts * jnp.exp(scores)))
     hard_mean = hard_total / total_slots
     columns = jnp.arange(scores.shape[1], dtype=jnp.int32)
     chosen = positive[:, None] == columns[None, :]
@@ -129,7 +147,7 @@
     local_weight = contract_first(query_flat, query_back) + contract_first(
         passage_flat, passage_back
     )
-    grad_proj = lax.psum(local_weight, ("group", "dp"))
+    grad_proj = sum_rows_everywhere(local_weight)
     return (losses, grad_proj, grad_query, grad_passage)
 
 

time: 281 us -> 148 us (0.53)
  waiting for transfers between devices: 145 us -> 29 us
  blocking collectives: 46.7 us -> 21 us
  starting transfers between devices: 8.24 us -> 14.3 us
    psum x1 -> x0, waiting for transfers between devices: 129 us -> none  [local(): grad_proj = lax.psum(local_weight, ('group', 'dp'))]
    psum x1 -> x0, blocking collectives: 39.2 us -> none  [finish_loss(): hard_total = lax.psum(jnp.sum(counts * jnp.exp(scores)), ('group', 'dp'))]
    all_to_all x0 -> x1, blocking collectives: none -> 13.4 us  [sum_everywhere(): return jnp.sum(lax.all_to_all(rows, axes, 0, 0, tiled=True)[:, 0, 0])]
    all_to_all x0 -> x2, waiting for transfers between devices: none -> 13.1 us  [the longest x1 8.71 us: sum_rows_everywhere(): parts = lax.all_to_all(parts, axes, 0, 0, tiled=True)]
    all_to_all x0 -> x2, starting transfers between devices: none -> 7.45 us  [the longest x1 5.08 us: sum_rows_everywhere(): parts = lax.all_to_all(parts, axes, 0, 0, tiled=True)]
    unnamed x23 -> x28, local copies, waits for them, and re-layouts: 8.56 us -> 8.08 us
  transfers between devices with their start and end apart: 4 -> 5, of which waited for: 4 -> 5; matrix products, arithmetic and copies ran while one was open for 4% -> 8% of each run, Pallas kernels for 0% -> 0%
where the time goes in v1:
time: 148 us; the launch traced here: 146 us
  matrix products  32.4 us (22%)
  waiting for transfers between devices  29 us (20%)
  local copies, waits for them, and re-layouts  22.8 us (15%)
  blocking collectives  21 us (14%)
  between operations  14.9 us (10%)
  starting transfers between devices  14.3 us (10%)
  other arithmetic  11.5 us (8%)
    dot_general x10, matrix products, contract_last(): lax.dot_general(left, right, (((1,), (1,)), ((), ())), preferred_element_...  18.8 us
    all_to_all x1, blocking collectives, sum_everywhere(): return jnp.sum(lax.all_to_all(rows, axes, 0, 0, tiled=True)[:, 0, 0])  13.4 us
    reduce_scatter x1, waiting for transfers between devices, local(): lax.psum_scatter(query_parts.reshape(groups * block_rows, embed_width).as...  10.2 us
    all_to_all x1, waiting for transfers between devices, sum_rows_everywhere(): parts = lax.all_to_all(parts, axes, 0, 0, tiled=True)  8.71 us
    unnamed x28, local copies, waits for them, and re-layouts  8.08 us
    dot_general x6, matrix products, contract_first(): lax.dot_general(left, right, (((0,), (0,)), ((), ())), preferred_element_...  8.02 us
    all_gather x1, blocking collectives, local(): gathered = lax.all_gather(query_embed, 'group', axis=0, tiled=True)  7.56 us
    all_to_all x1, starting transfers between devices, sum_rows_everywhere(): parts = lax.all_to_all(parts, axes, 0, 0, tiled=True)  5.08 us
  transfers between devices with their start and end apart: 5, of which 5 were waited for; matrix products, arithmetic and copies ran while one was open for 8% of the time, Pallas kernels for 0%

profile of v1, /device:TPU:1, one launch (start us, length us, event | category | flops | bytes accessed | tf_op | source)
XLA Modules:
  0.0 146.5 jit_solution(9609109347564185583)
XLA Ops:
  8.7 7.6 %all_gather.3 = bf16[1024,128]{0,1:T(8,128)(2,1)} all-gather(bf16[256,128]{0,1:T(8,128)(2,1)S(1)} %multiply_convert_fusion.2), channel_id=1, replica_groups=mesh['group'=4,'dp'=8] {'group'}, dimensions={0}, use_global_device_ids=true | all-gather | bytes 327680 | tf_op jit(solution)/shard_map/all_gather | solution.py:102
  16.3 1.8 %copy.85 = bf16[1024,128]{1,0:T(8,128)(2,1)} copy(bf16[1024,128]{0,1:T(8,128)(2,1)} %all_gather.3) | data formatting | bytes 524288
  18.1 2.1 %multiply_reduce_fusion.1 = (f32[2048]{0:T(1024)S(1)}, f32[2048,128]{0,1:T(8,128)S(1)}) fusion(bf16[2048,768]{1,0:T(8,128)(2,1)S(1)} %bitcast.114, bf16[768,128]{1,0:T(8,128)(2,1)} %param.12), kind=kOutput, calls=%fused_computation.32 | convolution fusion | flops 403175424 | bytes 4399104 | tf_op jit(solution)/shard_map/dot_general | solution.py:98
  22.0 2.1 %copy.70 = bf16[2048,128]{1,0:T(8,128)(2,1)} copy(bf16[2048,128]{0,1:T(8,128)(2,1)} %multiply_convert_fusion.1) | data formatting | bytes 1048576
  24.1 7.2 %while.24 = (s32[]{:T(128)}, f32[4,256,16]{1,2,0:T(8,128)S(1)}, bf16[4,256,128]{2,1,0:T(8,128)(2,1)}, bf16[2048,128]{1,0:T(8,128)(2,1)}, s32[16]{0:T(128)S(1)}, /*index=5*/s32[]{:T(128)}) while((s32[]{:T(128)}, f32[4,256,16]{1,2,0:T(8,128)S(1)}, bf16[4,256,128]{2,1,0:T(8,128)(2,1)}, bf16[2048,128]{1,0:T(8,128)(2,1)}, ...), condition=%wide.region_5.6_spmd.clone, body=%wide.region_3.0_spmd.clone.sunk | while | flops 135792640 | bytes 643221 | solution.py:105
  34.0 3.4 %all-to-all-start = ((f32[4,1,128]{2,1,0:T(1,128)}), f32[4,1,128]{2,1,0:T(1,128)S(1)}, u32[]{:S(2)}, u32[]{:S(2)}) async-start(f32[4,1,128]{2,1,0:T(1,128)} %reshape.164), calls=%async_computation | async-start | bytes 4096 | tf_op jit(solution)/shard_map/all_to_all | solution.py:111
  37.6 2.8 %all-to-all-done = f32[4,1,128]{2,1,0:T(1,128)S(1)} async-done(((f32[4,1,128]{2,1,0:T(1,128)}), f32[4,1,128]{2,1,0:T(1,128)S(1)}, u32[]{:S(2)}, u32[]{:S(2)}) %all-to-all-start) | async-done | bytes 2080 | tf_op jit(solution)/shard_map/all_to_all | solution.py:111
  43.0 13.4 %all_to_all.47 = f32[32,8,128]{2,1,0:T(8,128)S(1)} all-to-all(f32[32,8,128]{2,1,0:T(8,128)S(1)} %broadcast_in_dim.79), channel_id=1, replica_groups=mesh['group'=4,'dp'=8] {'dp','group'}, dimensions={0} | all-to-all | bytes 262144 | tf_op jit(solution)/shard_map/all_to_all | solution.py:50
  58.7 3.5 %all-to-all-start.2 = ((f32[4,1,128]{2,1,0:T(1,128)}), f32[4,1,128]{2,1,0:T(1,128)S(1)}, u32[]{:S(2)}, u32[]{:S(2)}) async-start(f32[4,1,128]{2,1,0:T(1,128)} %reshape.166), calls=%async_computation.2 | async-start | bytes 4096 | tf_op jit(solution)/shard_map/all_to_all | solution.py:113
  62.2 2.9 %all-to-all-done.2 = f32[4,1,128]{2,1,0:T(1,128)S(1)} async-done(((f32[4,1,128]{2,1,0:T(1,128)}), f32[4,1,128]{2,1,0:T(1,128)S(1)}, u32[]{:S(2)}, u32[]{:S(2)}) %all-to-all-start.2) | async-done | bytes 2080 | tf_op jit(solution)/shard_map/all_to_all | solution.py:113
  67.8 20.6 %while.25 = (s32[]{:T(128)}, f32[2048,128]{1,0:T(8,128)}, bf16[4,256,128]{2,1,0:T(8,128)(2,1)}, f32[4,256,16]{1,0,2:T(4,128)S(1)}, bf16[4,256,128]{2,1,0:T(8,128...) while((s32[]{:T(128)}, f32[2048,128]{1,0:T(8,128)}, ...), condition=%wide.region_12.13_spmd.clone, body=%wide.region_11.12_spmd.clone.sunk | while | flops 406329344 | bytes 20320600 | solution.py:126
  68.0 1.8 %multiply_convert_fusion.4 = bf16[256,16,128]{0,2,1:T(8,128)(2,1)S(1)} fusion(bf16[16,128,128]{2,1,0:T(8,128)(2,1)} %bitcast.119, f32[256,16]{0,1:T(8,128)S(1)} %get-tuple-element.316, f32[256,16]{0,1:T(8,128)S(1)} %get-tuple-element.317, pred[16,128]{1,0:T(8,128)(4,1)S(1)} %iota_compare_fusion.6, bf16[4,256,128]{2,1,0:T(8,128)(2,1)} %get-tuple-element.360, ...), kind=kOutput, calls=%fused_computation.9.clone.1 | convolution fusion | flops 136839168 | bytes 1673220 | tf_op jit(solution)/shard_map/while/body/eval_jaxpr/dot_general | solution.py:15
  73.1 1.8 %multiply_convert_fusion.4 = bf16[256,16,128]{0,2,1:T(8,128)(2,1)S(1)} fusion(bf16[16,128,128]{2,1,0:T(8,128)(2,1)} %bitcast.119, f32[256,16]{0,1:T(8,128)S(1)} %get-tuple-element.316, f32[256,16]{0,1:T(8,128)S(1)} %get-tuple-element.317, pred[16,128]{1,0:T(8,128)(4,1)S(1)} %iota_compare_fusion.6, bf16[4,256,128]{2,1,0:T(8,128)(2,1)} %get-tuple-element.360, ...), kind=kOutput, calls=%fused_computation.9.clone.1 | convolution fusion | flops 136839168 | bytes 1673220 | tf_op jit(solution)/shard_map/while/body/eval_jaxpr/dot_general | solution.py:15
  78.3 1.8 %multiply_convert_fusion.4 = bf16[256,16,128]{0,2,1:T(8,128)(2,1)S(1)} fusion(bf16[16,128,128]{2,1,0:T(8,128)(2,1)} %bitcast.119, f32[256,16]{0,1:T(8,128)S(1)} %get-tuple-element.316, f32[256,16]{0,1:T(8,128)S(1)} %get-tuple-element.317, pred[16,128]{1,0:T(8,128)(4,1)S(1)} %iota_compare_fusion.6, bf16[4,256,128]{2,1,0:T(8,128)(2,1)} %get-tuple-element.360, ...), kind=kOutput, calls=%fused_computation.9.clone.1 | convolution fusion | flops 136839168 | bytes 1673220 | tf_op jit(solution)/shard_map/while/body/eval_jaxpr/dot_general | solution.py:15
  83.4 1.8 %multiply_convert_fusion.4 = bf16[256,16,128]{0,2,1:T(8,128)(2,1)S(1)} fusion(bf16[16,128,128]{2,1,0:T(8,128)(2,1)} %bitcast.119, f32[256,16]{0,1:T(8,128)S(1)} %get-tuple-element.316, f32[256,16]{0,1:T(8,128)S(1)} %get-tuple-element.317, pred[16,128]{1,0:T(8,128)(4,1)S(1)} %iota_compare_fusion.6, bf16[4,256,128]{2,1,0:T(8,128)(2,1)} %get-tuple-element.360, ...), kind=kOutput, calls=%fused_computation.9.clone.1 | convolution fusion | flops 136839168 | bytes 1673220 | tf_op jit(solution)/shard_map/while/body/eval_jaxpr/dot_general | solution.py:15
  88.5 1.8 %copy.84 = bf16[1024,128]{0,1:T(8,128)(2,1)} copy(bf16[1024,128]{1,0:T(8,128)(2,1)} %bitcast.126) | data formatting | bytes 524288 | tf_op jit(solution)/shard_map/convert_element_type | solution.py:130
  90.3 2.6 %copy.81 = f32[2048,128]{0,1:T(8,128)} copy(f32[2048,128]{1,0:T(8,128)} %get-tuple-element.76) | data formatting | bytes 2097152 | tf_op jit(solution)/shard_map/while | solution.py:126
  92.9 1.8 %multiply_reduce_fusion = f32[2048]{0:T(1024)S(1)} fusion(f32[2048,128]{0,1:T(8,128)} %copy-done.4, f32[2048,128]{0,1:T(8,128)} %copy.81), kind=kLoop, calls=%fused_computation.30 | loop fusion | flops 522240 | bytes 2105344 | tf_op jit(solution)/shard_map/transpose(jvp())/reduce_sum | solution.py:11
  97.4 10.2 %reduce-scatter.2.cloned.1.call-done = bf16[256,128]{0,1:T(8,128)(2,1)} async-done(((bf16[1024,128]{0,1:T(8,128)(2,1)}), bf16[256,128]{0,1:T(8,128)(2,1)}) %reduce-scatter.2.cloned.1.call-update) | async-done | bytes 65552 | tf_op jit(solution)/shard_map/reduce_scatter | solution.py:129
  112.2 5.1 %all-to-all-start.3 = ((bf16[32,24,128]{2,1,0:T(8,128)(2,1)}), bf16[32,24,128]{2,1,0:T(8,128)(2,1)S(1)}, u32[]{:S(2)}, u32[]{:S(2)}) async-start(bf16[32,24,128]{2,1,0:T(8,128)(2,1)} %bitcast.124), calls=%async_computation.4 | async-start | bytes 393216 | tf_op jit(solution)/shard_map/all_to_all | solution.py:58
  117.8 8.7 %all-to-all-done.3 = bf16[32,24,128]{2,1,0:T(8,128)(2,1)S(1)} async-done(((bf16[32,24,128]{2,1,0:T(8,128)(2,1)}), bf16[32,24,128]{2,1,0:T(8,128)(2,1)S(1)}, u32[]{:S(2)}, u32[]{:S(2)}) %all-to-all-start.3) | async-done | bytes 196640 | tf_op jit(solution)/shard_map/all_to_all | solution.py:58
  127.2 2.4 %all-to-all-start.4 = ((bf16[32,24,128]{2,1,0:T(8,128)(2,1)}), bf16[32,24,128]{2,1,0:T(8,128)(2,1)S(1)}, u32[]{:S(2)}, u32[]{:S(2)}) async-start(bf16[32,24,128]{2,1,0:T(8,128)(2,1)} %broadcast_in_dim.85), calls=%async_computation.5 | async-start | bytes 393216 | tf_op jit(solution)/shard_map/all_to_all | solution.py:61
  129.6 3.8 %convolution_convert_fusion.1 = bf16[2048,768]{1,0:T(8,128)(2,1)} fusion(bf16[2048,128]{0,1:T(8,128)(2,1)} %copy-done.7, bf16[768,128]{1,0:T(8,128)(2,1)S(1)} %copy-done.8), kind=kOutput, calls=%fused_computation.23 | convolution fusion | flops 404226048 | bytes 3866624 | tf_op jit(solution)/shard_map/dot_general | solution.py:15
  134.4 4.4 %all-to-all-done.4 = bf16[32,24,128]{2,1,0:T(8,128)(2,1)S(1)} async-done(((bf16[32,24,128]{2,1,0:T(8,128)(2,1)}), bf16[32,24,128]{2,1,0:T(8,128)(2,1)S(1)}, u32[]{:S(2)}, u32[]{:S(2)}) %all-to-all-start.4) | async-done | bytes 196640 | tf_op jit(solution)/shard_map/all_to_all | solution.py:61
  (145 shorter events, 43.6 us)
Async XLA Ops:
  7.2 10.9 %copy-start = (bf16[16,128,768]{2,1,0:T(8,128)(2,1)S(1)}, bf16[16,128,768]{2,1,0:T(8,128)(2,1)}, u32[]{:S(2)}) copy-start(bf16[16,128,768]{2,1,0:T(8,128)(2,1)} %param.11) | copy-start | bytes 9437188
  20.2 3.9 %copy-start.13 = (s32[16]{0:T(128)S(1)}, s32[16]{0:T(128)}, u32[]{:S(2)}) copy-start(s32[16]{0:T(128)} %param.15) | copy-start | bytes 196
  24.1 13.3 %copy-start.15 = (s32[8,32]{1,0:T(8,128)S(1)}, s32[8,32]{1,0:T(8,128)}, u32[]{:S(2)}) copy-start(s32[8,32]{1,0:T(8,128)} %param.14) | copy-start | bytes 3076
  24.1 17.5 %copy-start.14 = (s32[8]{0:T(128)S(1)}, s32[8]{0:T(128)}, u32[]{:S(2)}) copy-start(s32[8]{0:T(128)} %param.13) | copy-start | bytes 100
  34.0 6.3 %all-to-all-start = ((f32[4,1,128]{2,1,0:T(1,128)}), f32[4,1,128]{2,1,0:T(1,128)S(1)}, u32[]{:S(2)}, u32[]{:S(2)}) async-start(f32[4,1,128]{2,1,0:T(1,128)} %reshape.164), calls=%async_computation | async-start | bytes 4096 | tf_op jit(solution)/shard_map/all_to_all | solution.py:111
  58.7 6.4 %all-to-all-start.2 = ((f32[4,1,128]{2,1,0:T(1,128)}), f32[4,1,128]{2,1,0:T(1,128)S(1)}, u32[]{:S(2)}, u32[]{:S(2)}) async-start(f32[4,1,128]{2,1,0:T(1,128)} %reshape.166), calls=%async_computation.2 | async-start | bytes 4096 | tf_op jit(solution)/shard_map/all_to_all | solution.py:113
  62.2 45.5 %reduce-scatter.2.cloned.1.call-start = ((), (), s32[]{:S(2)}) async-start(), calls=%async_computation.6 | async-start | bytes 327680 | tf_op jit(solution)/shard_map/reduce_scatter | solution.py:129
  67.8 2.0 %copy-start.3 = (bf16[2048,128]{1,0:T(8,128)(2,1)S(1)}, bf16[2048,128]{1,0:T(8,128)(2,1)}, u32[]{:S(2)}) copy-start(bf16[2048,128]{1,0:T(8,128)(2,1)} %get-tuple-element.361) | copy-start | bytes 1572868 | tf_op jit(solution)/shard_map/while
  67.9 2.0 %copy-start.11 = (bf16[4,256,128]{2,1,0:T(8,128)(2,1)S(1)}, bf16[4,256,128]{2,1,0:T(8,128)(2,1)}, u32[]{:S(2)}) copy-start(bf16[4,256,128]{2,1,0:T(8,128)(2,1)} %get-tuple-element.348) | copy-start | bytes 786436 | tf_op jit(solution)/shard_map/while
  69.8 1.9 %copy-start.1 = (f32[2048,128]{1,0:T(8,128)S(1)}, f32[2048,128]{1,0:T(8,128)}, u32[]{:S(2)}) copy-start(f32[2048,128]{1,0:T(8,128)} %get-tuple-element.347) | copy-start | bytes 3145732 | tf_op jit(solution)/shard_map/while
  73.0 1.9 %copy-start.3 = (bf16[2048,128]{1,0:T(8,128)(2,1)S(1)}, bf16[2048,128]{1,0:T(8,128)(2,1)}, u32[]{:S(2)}) copy-start(bf16[2048,128]{1,0:T(8,128)(2,1)} %get-tuple-element.361) | copy-start | bytes 1572868 | tf_op jit(solution)/shard_map/while
  73.0 2.0 %copy-start.11 = (bf16[4,256,128]{2,1,0:T(8,128)(2,1)S(1)}, bf16[4,256,128]{2,1,0:T(8,128)(2,1)}, u32[]{:S(2)}) copy-start(bf16[4,256,128]{2,1,0:T(8,128)(2,1)} %get-tuple-element.348) | copy-start | bytes 786436 | tf_op jit(solution)/shard_map/while
  75.0 1.9 %copy-start.1 = (f32[2048,128]{1,0:T(8,128)S(1)}, f32[2048,128]{1,0:T(8,128)}, u32[]{:S(2)}) copy-start(f32[2048,128]{1,0:T(8,128)} %get-tuple-element.347) | copy-start | bytes 3145732 | tf_op jit(solution)/shard_map/while
  78.2 1.9 %copy-start.3 = (bf16[2048,128]{1,0:T(8,128)(2,1)S(1)}, bf16[2048,128]{1,0:T(8,128)(2,1)}, u32[]{:S(2)}) copy-start(bf16[2048,128]{1,0:T(8,128)(2,1)} %get-tuple-element.361) | copy-start | bytes 1572868 | tf_op jit(solution)/shard_map/while
  78.2 2.0 %copy-start.11 = (bf16[4,256,128]{2,1,0:T(8,128)(2,1)S(1)}, bf16[4,256,128]{2,1,0:T(8,128)(2,1)}, u32[]{:S(2)}) copy-start(bf16[4,256,128]{2,1,0:T(8,128)(2,1)} %get-tuple-element.348) | copy-start | bytes 786436 | tf_op jit(solution)/shard_map/while
  80.1 1.9 %copy-start.1 = (f32[2048,128]{1,0:T(8,128)S(1)}, f32[2048,128]{1,0:T(8,128)}, u32[]{:S(2)}) copy-start(f32[2048,128]{1,0:T(8,128)} %get-tuple-element.347) | copy-start | bytes 3145732 | tf_op jit(solution)/shard_map/while
  83.3 1.9 %copy-start.3 = (bf16[2048,128]{1,0:T(8,128)(2,1)S(1)}, bf16[2048,128]{1,0:T(8,128)(2,1)}, u32[]{:S(2)}) copy-start(bf16[2048,128]{1,0:T(8,128)(2,1)} %get-tuple-element.361) | copy-start | bytes 1572868 | tf_op jit(solution)/shard_map/while
  83.3 2.0 %copy-start.11 = (bf16[4,256,128]{2,1,0:T(8,128)(2,1)S(1)}, bf16[4,256,128]{2,1,0:T(8,128)(2,1)}, u32[]{:S(2)}) copy-start(bf16[4,256,128]{2,1,0:T(8,128)(2,1)} %get-tuple-element.348) | copy-start | bytes 786436 | tf_op jit(solution)/shard_map/while
  85.2 1.9 %copy-start.1 = (f32[2048,128]{1,0:T(8,128)S(1)}, f32[2048,128]{1,0:T(8,128)}, u32[]{:S(2)}) copy-start(f32[2048,128]{1,0:T(8,128)} %get-tuple-element.347) | copy-start | bytes 3145732 | tf_op jit(solution)/shard_map/while
  92.9 2.2 %copy-start.6 = (f32[2048,128]{0,1:T(8,128)S(1)}, f32[2048,128]{0,1:T(8,128)}, u32[]{:S(2)}) copy-start(f32[2048,128]{0,1:T(8,128)} %copy.81) | copy-start | bytes 3145732
  97.4 32.2 %copy-start.8 = (bf16[768,128]{1,0:T(8,128)(2,1)S(1)}, bf16[768,128]{1,0:T(8,128)(2,1)}, u32[]{:S(2)}) copy-start(bf16[768,128]{1,0:T(8,128)(2,1)} %param.12) | copy-start | bytes 589828
  112.2 14.3 %all-to-all-start.3 = ((bf16[32,24,128]{2,1,0:T(8,128)(2,1)}), bf16[32,24,128]{2,1,0:T(8,128)(2,1)S(1)}, u32[]{:S(2)}, u32[]{:S(2)}) async-start(bf16[32,24,128]{2,1,0:T(8,128)(2,1)} %bitcast.124), calls=%async_computation.4 | async-start | bytes 393216 | tf_op jit(solution)/shard_map/all_to_all | solution.py:58
  127.2 11.6 %all-to-all-start.4 = ((bf16[32,24,128]{2,1,0:T(8,128)(2,1)}), bf16[32,24,128]{2,1,0:T(8,128)(2,1)S(1)}, u32[]{:S(2)}, u32[]{:S(2)}) async-start(bf16[32,24,128]{2,1,0:T(8,128)(2,1)} %broadcast_in_dim.85), calls=%async_computation.5 | async-start | bytes 393216 | tf_op jit(solution)/shard_map/all_to_all | solution.py:61
  129.6 3.8 %copy-start.10 = (bf16[256,128]{0,1:T(8,128)(2,1)S(1)}, bf16[256,128]{0,1:T(8,128)(2,1)}, u32[]{:S(2)}) copy-start(bf16[256,128]{0,1:T(8,128)(2,1)} %copy-done.9) | copy-start | bytes 196612
  (12 other events, 14.9 us)
Sparse Core Ops, SparseCore 0:
  90.4 17.1 reduce-scatter.1

commit v2 on v0

v2 whole, which is shorter than its diff:
```python
import functools

import jax
import jax.numpy as jnp
from jax import lax
from jax.experimental import pallas as pl
from jax.experimental.pallas import tpu as pltpu
from jax.sharding import PartitionSpec as P

smooth_temp = 0.1
norm_eps = 1e-06
center = 0.375
lanes = 128
axes = ("dp", "group")
f32 = jnp.float32
bf16 = jnp.bfloat16


def dot(left, right, left_dim, right_dim):
    return lax.dot_general(
        left, right, (((left_dim,), (right_dim,)), ((), ())), preferred_element_type=f32
    )


def split_parts(value):
    high = value.astype(bf16)
    rest = value - high.astype(f32)
    middle = rest.astype(bf16)
    low = (rest - middle.astype(f32)).astype(bf16)
    return (high, middle, low)


def exact_dot(value, picks):
    return sum(dot(part, picks, 1, 0) for part in split_parts(value))


def normalize(projected):
    return projected * lax.rsqrt(jnp.sum(projected * projected, axis=-1, keepdims=True) + norm_eps)


def normalize_back(projected, grad):
    inverse = lax.rsqrt(jnp.sum(projected * projected, axis=-1, keepdims=True) + norm_eps)
    along = jnp.sum(projected * grad, axis=-1, keepdims=True)
    return grad * inverse - projected * (inverse * inverse * inverse * along)


def iota(shape, dim):
    return lax.broadcasted_iota(jnp.int32, shape, dim)


def params(megabytes):
    return pltpu.CompilerParams(vmem_limit_bytes=megabytes * 2**20)


def cost(flops, nbytes, exps=0):
    return pl.CostEstimate(flops=int(flops), bytes_accessed=int(nbytes), transcendentals=int(exps))


VMEM = pl.BlockSpec(memory_space=pltpu.VMEM)
SMEM = pl.BlockSpec(memory_space=pltpu.SMEM)


def query_kernel(hidden, projection, hard_ids, positive, pre_out, packed_out):
    rows = hidden.shape[0]
    count, slots = hard_ids.shape
    pre = dot(hidden[...], projection[...], 1, 0)
    pre_out[...] = pre
    packed_out[:rows, :] = normalize(pre).astype(bf16)
    row = iota((count, lanes), 0)
    column = iota((count, lanes), 1)
    marks = jnp.full((count, lanes), -1.0, f32)
    for k in range(count):
        marks = jnp.where((row == k) & (column == slots), positive[k].astype(f32), marks)
    ids = jnp.concatenate(
        [hard_ids[...].astype(f32), jnp.full((count, lanes - slots), -1.0, f32)], axis=1
    )
    marks = jnp.where(column < slots, ids, marks)
    extra = packed_out.shape[0] - rows
    marks = jnp.concatenate([marks, jnp.full((extra - count, lanes), -1.0, f32)], axis=0)
    packed_out[rows:, :] = marks.astype(bf16)


def passage_kernel(hidden, projection, pre_out, embed_out):
    pre = dot(hidden[...], projection[...], 1, 0)
    pre_out[...] = pre
    embed_out[...] = normalize(pre).astype(bf16)


def token_picks(groups, count, length, width, rows_first):
    me = lax.axis_index("group")
    tokens = groups * count * length
    shape = (tokens, width) if rows_first else (width, tokens)
    token = iota(shape, 0 if rows_first else 1)
    query = iota(shape, 1 if rows_first else 0)
    member = jnp.bitwise_xor(token // (count * length), me)
    owner = member * count + (token % (count * length)) // length
    return jnp.where(owner == query, 1.0, 0.0).astype(bf16)


def forward_kernel(dims, lens, *refs):
    groups, count, length, passages, tokens, slots, step = dims
    packed = refs[:groups]
    embed, shares_out, inverse_out, stats_out, packet_out, queries, summed, marks = refs[groups:]
    rows = count * length
    at = pl.program_id(0)
    me = lax.axis_index("group")

    @pl.when(at == 0)
    def _():
        marks[...] = jnp.full(marks.shape, -1.0, f32)
        for k in range(groups):
            queries[k] = packed[k][:rows, :]
            member = jnp.bitwise_xor(me, k)
            start = pl.multiple_of(member * count, count)
            marks[pl.ds(start, count), :] = packed[k][rows:, :].astype(f32)[:count]

    def one(k, _):
        for p in range(step):
            part = embed[p * tokens : (p + 1) * tokens, :]
            similar = dot(part, queries[k], 1, 1)
            alive = iota(similar.shape, 0) < lens[at * step + p]
            grown = jnp.where(alive, jnp.exp(similar * (1.0 / smooth_temp)), 0.0)
            column = pl.multiple_of(k * rows, rows) if groups > 4 else k * rows
            shares_out[p * tokens : (p + 1) * tokens, pl.ds(column, rows)] = grown.astype(bf16)
            summed[pl.ds(at * step + p, 1), pl.ds(column, rows)] = jnp.sum(
                grown, axis=0, keepdims=True
            )
        return 0

    if groups > 4:
        lax.fori_loop(0, groups, one, 0)
    else:
        for k in range(groups):
            one(k, 0)

    @pl.when(at == pl.num_programs(0) - 1)
    def _():
        total = summed[...]
        inverse_out[...] = 1.0 / total
        width = marks.shape[0]
        scores = exact_dot(
            smooth_temp * jnp.log(total), token_picks(groups, count, length, width, True)
        )
        marks_t = marks[...].T
        ids = marks_t[:slots, :]
        first = me * passages
        counts = jnp.concatenate(
            [
                jnp.sum(
                    jnp.where(ids == (first + p).astype(f32), 1.0, 0.0), axis=0, keepdims=True
                )
                for p in range(passages)
            ],
            axis=0,
        )
        here = (iota((passages, width), 0) + first).astype(f32)
        chosen = here == marks_t[slots : slots + 1, :]
        grown = jnp.exp(scores - center * length)
        boost = groups * passages / slots
        boosted = jnp.where(chosen, 0.0, boost * counts)
        stats_out[:passages, :] = grown
        stats_out[passages : 2 * passages, :] = boosted
        stats_out[2 * passages :, :] = jnp.where(chosen, 1.0, 0.0)
        plain = jnp.sum(grown, axis=0, keepdims=True)
        hard = jnp.sum(boosted * grown * grown, axis=0, keepdims=True)
        kept = jnp.sum(jnp.where(chosen, scores, 0.0), axis=0, keepdims=True)
        sums = jnp.sum(counts * grown, axis=0, keepdims=True)
        sums = jnp.broadcast_to(jnp.sum(sums, axis=1, keepdims=True), sums.shape)
        packet = jnp.concatenate([plain, hard, kept, sums] * 2, axis=0)
        for k in range(packet_out.shape[0] // 8):
            packet_out[k * 8 : k * 8 + 8, :] = packet


def query_grad_kernel(dims, packets, stats, inverse, shares, embed, *refs):
    groups, count, length, passages, tokens, slots, step = dims
    parts_out = refs[:groups]
    weights_out, losses_out, weights, running = refs[groups:]
    rows = count * length
    at = pl.program_id(0)

    @pl.when(at == 0)
    def _():
        width = stats.shape[1]
        devices = packets.shape[0] // 8
        got = packets[...].reshape(devices, 8, width)
        dp = lax.axis_index("dp")
        ours = iota(got.shape, 0) // groups == dp
        pool = jnp.sum(jnp.where(ours, got, 0.0), axis=0)
        every = jnp.sum(got, axis=0)
        hard_mean = every[3:4, :] * (1.0 / (devices * count * slots))
        partition = pool[0:1, :] + pool[1:2, :] / hard_mean
        losses_out[...] = jnp.broadcast_to(
            jnp.log(partition) - (pool[2:3, :] - center * length), losses_out.shape
        )
        grown = stats[:passages, :]
        boosted = stats[passages : 2 * passages, :]
        chosen = stats[2 * passages :, :]
        grad = grown * (1.0 + boosted * grown / hard_mean) / partition - chosen
        spread = exact_dot(grad, token_picks(groups, count, length, width, False))
        found = (spread * inverse[...]).astype(bf16)
        for p in range(passages):
            weights[p] = found[p : p + 1, :]
        weights_out[...] = weights[...]
        running[...] = jnp.zeros(running.shape, f32)

    coefficient = jnp.concatenate(
        [
            shares[p * tokens : (p + 1) * tokens, :] * weights[at * step + p]
            for p in range(step)
        ],
        axis=0,
    )
    running[...] += dot(embed[...].T, coefficient, 1, 0)

    @pl.when(at == pl.num_programs(0) - 1)
    def _():
        for k in range(groups):
            parts_out[k][...] = running[:, k * rows : (k + 1) * rows].astype(bf16)


def passage_grad_kernel(dims, weights, shares, pre, hidden, *refs):
    groups, count, length, passages, tokens, slots, step = dims
    packed = refs[:groups]
    back_out, weight_out, queries = refs[groups:]
    rows = count * length
    at = pl.program_id(0)

    @pl.when(at == 0)
    def _():
        for k in range(groups):
            queries[k * rows : (k + 1) * rows, :] = packed[k][:rows, :]
        weight_out[...] = jnp.zeros(weight_out.shape, f32)

    coefficient = jnp.concatenate(
        [
            shares[p * tokens : (p + 1) * tokens, :] * weights[at * step + p]
            for p in range(step)
        ],
        axis=0,
    )
    grad = dot(coefficient, queries[...], 1, 0)
    back = normalize_back(pre[...], grad).astype(bf16)
    back_out[...] = back
    weight_out[...] += dot(back.T, hidden[...], 1, 0)


def query_back_kernel(pre, hidden, weight, *refs):
    parts = refs[:-2]
    back_out, weight_out = refs[-2:]
    grad = sum(part[...].astype(f32) for part in parts).T
    back = normalize_back(pre[...], grad).astype(bf16)
    back_out[...] = back
    total = weight[...] + dot(back.T, hidden[...], 1, 0)
    weight_out[...] = total.T.astype(bf16)


def sum_kernel(parts, copies_out):
    devices = copies_out.shape[0]
    total = parts[0].astype(f32)
    for k in range(1, devices):
        total += parts[k].astype(f32)
    total = total.astype(bf16)
    for k in range(devices):
        copies_out[k] = total


def local(query_hidden, passage_hidden, projection, positive, hard_ids, passage_len):
    count, length, width = query_hidden.shape
    passages, tokens, _ = passage_hidden.shape
    depth = projection.shape[1]
    slots = hard_ids.shape[1]
    groups = lax.axis_size("group")
    devices = lax.axis_size(axes)
    rows = count * length
    all_rows = groups * rows
    passage_rows = passages * tokens
    pool_width = -(-groups * count // lanes) * lanes
    step = 4 if passages % 4 == 0 else 1
    steps = passages // step
    step_rows = step * tokens
    dims = (groups, count, length, passages, tokens, slots, step)
    query_flat = query_hidden.reshape(rows, width)
    passage_flat = passage_hidden.reshape(passage_rows, width)
    shape = jax.ShapeDtypeStruct

    query_pre, packed = pl.pallas_call(
        query_kernel,
        out_shape=(shape((rows, depth), f32), shape((rows + 16, depth), bf16)),
        in_specs=[VMEM, VMEM, VMEM, SMEM],
        out_specs=(VMEM, VMEM),
        compiler_params=params(16),
        cost_estimate=cost(2 * rows * width * depth, rows * width * 2),
        name="query_embed",
    )(query_flat, projection, hard_ids, positive)

    def swap(value, k):
        return lax.ppermute(value, "group", [(i, i ^ k) for i in range(groups)])

    blocks = [packed] + [swap(packed, k) for k in range(1, groups)]

    def by_rows(columns):
        return pl.BlockSpec((step_rows, columns), lambda i: (i, 0))

    def whole(*dims_):
        return pl.BlockSpec(dims_, lambda i: (0,) * len(dims_))

    passage_pre, passage_embed = pl.pallas_call(
        passage_kernel,
        out_shape=(shape((passage_rows, depth), f32), shape((passage_rows, depth), bf16)),
        grid=(steps,),
        in_specs=[by_rows(width), whole(width, depth)],
        out_specs=(by_rows(depth), by_rows(depth)),
        compiler_params=params(16),
        cost_estimate=cost(2 * passage_rows * width * depth, passage_rows * (width * 2 + depth * 6)),
        name="passage_embed",
    )(passage_flat, projection)

    shares, inverse, stats, packets = pl.pallas_call(
        functools.partial(forward_kernel, dims),
        out_shape=(
            shape((passage_rows, all_rows), bf16),
            shape((passages, all_rows), f32),
            shape((3 * passages, pool_width), f32),
            shape((devices * 8, pool_width), f32),
        ),
        grid=(steps,),
        in_specs=[SMEM] + [whole(*packed.shape)] * groups + [by_rows(depth)],
        out_specs=(
            by_rows(all_rows),
            whole(passages, all_rows),
            whole(3 * passages, pool_width),
            whole(devices * 8, pool_width),
        ),
        scratch_shapes=[
            pltpu.VMEM((groups, rows, depth), bf16),
            pltpu.VMEM((passages, all_rows), f32),
            pltpu.VMEM((pool_width, lanes), f32),
        ],
        compiler_params=params(32),
        cost_estimate=cost(
            2 * passage_rows * all_rows * depth,
            passage_rows * all_rows * 2,
            passage_rows * all_rows,
        ),
        name="forward",
    )(passage_len, *blocks, passage_embed)

    packets = lax.all_to_all(packets, axes, 0, 0, tiled=True)

    outs = pl.pallas_call(
        functools.partial(query_grad_kernel, dims),
        out_shape=(
            *[shape((depth, rows), bf16)] * groups,
            shape((passages, 1, all_rows), bf16),
            shape((8, pool_width), f32),
        ),
        grid=(steps,),
        in_specs=[
            whole(*packets.shape),
            whole(*stats.shape),
            whole(*inverse.shape),
            by_rows(all_rows),
            by_rows(depth),
        ],
        out_specs=(
            *[whole(depth, rows)] * groups,
            whole(passages, 1, all_rows),
            whole(8, pool_width),
        ),
        scratch_shapes=[
            pltpu.VMEM((passages, 1, all_rows), bf16),
            pltpu.VMEM((depth, all_rows), f32),
        ],
        compiler_params=params(32),
        cost_estimate=cost(2 * passage_rows * all_rows * depth, passage_rows * all_rows * 2),
        name="query_grad",
    )(packets, stats, inverse, shares, passage_embed)
    parts = outs[:groups]
    weights, losses = outs[groups:]
    parts = [parts[0]] + [swap(parts[k], k) for k in range(1, groups)]

    passage_back, weight = pl.pallas_call(
        functools.partial(passage_grad_kernel, dims),
        out_shape=(shape((passage_rows, depth), bf16), shape((depth, width), f32)),
        grid=(steps,),
        in_specs=[
            whole(passages, 1, all_rows),
            by_rows(all_rows),
            by_rows(depth),
            by_rows(width),
        ]
        + [whole(*packed.shape)] * groups,
        out_specs=(by_rows(depth), whole(depth, width)),
        scratch_shapes=[pltpu.VMEM((all_rows, depth), bf16)],
        compiler_params=params(32),
        cost_estimate=cost(
            2 * passage_rows * (all_rows + width) * depth,
            passage_rows * (all_rows * 2 + width * 2 + depth * 6),
        ),
        name="passage_grad",
    )(weights, shares, passage_pre, passage_flat, *blocks)

    query_back, weight = pl.pallas_call(
        query_back_kernel,
        out_shape=(shape((rows, depth), bf16), shape((width, depth), bf16)),
        in_specs=[VMEM] * (3 + groups),
        out_specs=(VMEM, VMEM),
        compiler_params=params(16),
        cost_estimate=cost(2 * rows * width * depth, width * depth * 6 + rows * width * 2),
        name="query_back",
    )(query_pre, query_flat, weight, *parts)

    weight = weight.reshape(devices, width // devices, depth)
    weight = lax.all_to_all(weight, axes, 0, 0, tiled=True)
    copies = pl.pallas_call(
        sum_kernel,
        out_shape=shape(weight.shape, bf16),
        in_specs=[VMEM],
        out_specs=VMEM,
        compiler_params=params(16),
        name="sum_parts",
    )(weight)
    copies = lax.all_to_all(copies, axes, 0, 0, tiled=True)
    grad_proj = copies.reshape(width, depth).astype(f32)

    grad_query = dot(query_back, projection, 1, 1).astype(bf16).reshape(query_hidden.shape)
    grad_passage = dot(passage_back, projection, 1, 1).astype(bf16).reshape(passage_hidden.shape)
    own = lax.axis_index("group") * count
    return (lax.dynamic_slice(losses[0], (own,), (count,)), grad_proj, grad_query, grad_passage)


def solution(mesh):
    in_specs = (
        P(axes, None, None),
        P(axes, None, None),
        P(),
        P(axes),
        P(axes, None),
        P(axes),
    )
    out_specs = (P(axes), P(), P(axes, None, None), P(axes, None, None))
    return jax.shard_map(local, mesh=mesh, in_specs=in_specs, out_specs=out_specs, check_vma=False)
```

time: 281 us -> 64.3 us (0.23)
  waiting for transfers between devices: 145 us -> 14.2 us
  blocking collectives: 46.7 us -> 14.2 us
  matrix products: 32.1 us -> 3.65 us
  local copies, waits for them, and re-layouts: 21.2 us -> 6.68 us
  between operations: 14.9 us -> 0.8 us
  Pallas kernels: 0 us -> 13.9 us
  other arithmetic: 10 us -> 0.78 us
    psum x1 -> x0, waiting for transfers between devices: 129 us -> none  [local(): grad_proj = lax.psum(local_weight, ('group', 'dp'))]
    psum x1 -> x0, blocking collectives: 39.2 us -> none  [finish_loss(): hard_total = lax.psum(jnp.sum(counts * jnp.exp(scores)), ('group', 'dp'))]
    dot_general x22 -> x2, matrix products: 32.1 us -> 3.65 us  [dot(): lax.dot_general(left, right, (((left_dim,), (right_dim,)), ((), ())), pre...]
    all_to_all x0 -> x1, blocking collectives: none -> 14.2 us  [local(): packets = lax.all_to_all(packets, axes, 0, 0, tiled=True)]
    pallas_call x0 -> x7, Pallas kernels: none -> 13.9 us  [the longest x1 3.83 us: local(): pl.pallas_call(functools.partial(passage_grad_kernel, dims), out_shape=(s...]
    reduce_scatter x1 -> x0, waiting for transfers between devices: 10.7 us -> none  [local(): lax.psum_scatter(query_parts.reshape(groups * block_rows, embed_width).as...]
    all_to_all x2, waiting for transfers between devices: 5.17 us -> 14.2 us  [the longest x1 9.24 us: local(): weight = lax.all_to_all(weight, axes, 0, 0, tiled=True)]
    all_gather x1 -> x0, blocking collectives: 7.56 us -> none  [local(): gathered = lax.all_gather(query_embed, 'group', axis=0, tiled=True)]
  transfers between devices with their start and end apart: 4 -> 8, of which waited for: 4 -> 2; matrix products, arithmetic and copies ran while one was open for 4% -> 7% of each run, Pallas kernels for 0% -> 9%
where the time goes in v2:
time: 64.3 us; the launch traced here: 63.9 us
  waiting for transfers between devices  14.2 us (22%)
  blocking collectives  14.2 us (22%)
  Pallas kernels  13.9 us (22%)
  starting transfers between devices  9.69 us (15%)
  local copies, waits for them, and re-layouts  6.68 us (10%)
  matrix products  3.65 us (6%)
  between operations  0.8 us (1%)
  other arithmetic  0.78 us (1%)
    all_to_all x1, blocking collectives, local(): packets = lax.all_to_all(packets, axes, 0, 0, tiled=True)  14.2 us
    all_to_all x1, waiting for transfers between devices, local(): weight = lax.all_to_all(weight, axes, 0, 0, tiled=True)  9.24 us
    unnamed x20, local copies, waits for them, and re-layouts  6.1 us
    ppermute x6, starting transfers between devices, swap(): return lax.ppermute(value, 'group', [(i, i ^ k) for i in range(groups)])  5.05 us
    all_to_all x1, waiting for transfers between devices, local(): copies = lax.all_to_all(copies, axes, 0, 0, tiled=True)  4.93 us
    pallas_call x1, Pallas kernels, local(): pl.pallas_call(functools.partial(passage_grad_kernel, dims), out_shape=(s...  3.83 us
    pallas_call x1, Pallas kernels, local(): pl.pallas_call(functools.partial(forward_kernel, dims), out_shape=(shape(...  3.74 us
    dot_general x2, matrix products, dot(): lax.dot_general(left, right, (((left_dim,), (right_dim,)), ((), ())), pre...  3.65 us
  transfers between devices with their start and end apart: 8, of which 2 were waited for; matrix products, arithmetic and copies ran while one was open for 7% of the time, Pallas kernels for 9%

profile of v2, /device:TPU:1, one launch (start us, length us, event | category | flops | bytes accessed | tf_op | source)
XLA Modules:
  0.0 63.9 jit_solution(9296391987718242632)
XLA Ops:
  0.7 0.9 %copy-done.2 = bf16[768,128]{1,0:T(8,128)(2,1)S(1)} copy-done((bf16[768,128]{1,0:T(8,128)(2,1)S(1)}, bf16[768,128]{1,0:T(8,128)(2,1)}, u32[]{:S(2)}) %copy-start.2) | copy-done | bytes 196632
  1.6 1.0 %copy-done.5 = bf16[8,32,768]{2,1,0:T(8,128)(2,1)S(1)} copy-done((bf16[8,32,768]{2,1,0:T(8,128)(2,1)S(1)}, bf16[8,32,768]{2,1,0:T(8,128)(2,1)}, u32[]{:S(2)}) %copy-start.5) | copy-done | bytes 393240
  2.6 0.7 %copy-done.7 = s32[8,32]{1,0:T(8,128)S(1)} copy-done((s32[8,32]{1,0:T(8,128)S(1)}, s32[8,32]{1,0:T(8,128)}, u32[]{:S(2)}) %copy-start.7) | copy-done | bytes 1048
  3.3 0.7 %copy-done.8 = s32[8]{0:T(128)S(1)} copy-done((s32[8]{0:T(128)S(1)}, s32[8]{0:T(128)}, u32[]{:S(2)}) %copy-start.8) | copy-done | bytes 56
  3.9 0.9 %query_embed.1 = (f32[256,128]{1,0:T(8,128)S(1)}, bf16[272,128]{1,0:T(8,128)(2,1)S(1)}) custom-call(bf16[256,768]{1,0:T(8,128)(2,1)S(1)} %bitcast.18, bf16[768,128]{1,0:T(8,128)(2,1)S(1)} %copy-done.2, s32[8,32]{1,0:T(8,128)S(1)} %copy-done.7, s32[8]{0:T(128)S(1)} %copy-done.8), custom_call_target="tpu_custom_call" | custom-call | flops 50331648 | bytes 393216 | tf_op jit(solution)/shard_map/query_embed/pallas_call | solution.py:286
  4.9 2.7 %collective-permute-start.1 = (bf16[272,128]{1,0:T(8,128)(2,1)S(1)}, bf16[272,128]{1,0:T(8,128)(2,1)S(1)}, u32[]{:S(2)}, u32[]{:S(2)}) collective-permute-start(bf16[272,128]{1,0:T(8,128)(2,1)S(1)} %get-tuple-element.22.refs_0_), channel_id=1, source_target_pairs={{0,16},{8,24},{16,0},{24,8},{1,17},{9,25},{17,1},{25,9},{2,18},{10... | collective-permute-start | bytes 208904 | tf_op jit(solution)/shard_map/ppermute | solution.py:297
  7.6 1.9 %copy-done = bf16[16,128,768]{2,1,0:T(8,128)(2,1)S(1)} copy-done((bf16[16,128,768]{2,1,0:T(8,128)(2,1)S(1)}, bf16[16,128,768]{2,1,0:T(8,128)(2,1)}, u32[]{:S(2)}) %copy-start) | copy-done | bytes 3145752
  9.5 0.9 %copy-done.3 = bf16[768,128]{1,0:T(8,128)(2,1)S(1)} copy-done((bf16[768,128]{1,0:T(8,128)(2,1)S(1)}, bf16[768,128]{1,0:T(8,128)(2,1)}, u32[]{:S(2)}) %copy-start.3) | copy-done | bytes 196632
  10.5 1.8 %passage_embed.1 = (f32[2048,128]{1,0:T(8,128)S(1)}, bf16[2048,128]{1,0:T(8,128)(2,1)S(1)}) custom-call(bf16[2048,768]{1,0:T(8,128)(2,1)S(1)} %bitcast.16, bf16[768,128]{1,0:T(8,128)(2,1)S(1)} %copy-done.3), custom_call_target="tpu_custom_call" | custom-call | flops 402653184 | bytes 4718592 | tf_op jit(solution)/shard_map/passage_embed/pallas_call | solution.py:307
  12.3 3.7 %forward.1 = (bf16[2048,1024]{1,0:T(8,128)(2,1)S(1)}, f32[16,1024]{1,0:T(8,128)S(1)}, f32[48,128]{1,0:T(8,128)S(1)}, f32[256,128]{1,0:T(8,128)S(1)}) custom-call(s32[16]{0:T(128)S(1)} %copy-done.9, bf16[272,128]{1,0:T(8,128)(2,1)S(1)} %get-tuple-element.22.refs_0_, bf16[272,128]{1,0:T(8,128)(2,1)S(1)} %collective-permute-done.refs_1_, ...), custom_call_target="tpu_custom_call" | custom-call | flops 536870912 | bytes 4194304 | tf_op jit(solution)/shard_map/forward/pallas_call | solution.py:318
  16.1 14.2 %all_to_all.21 = f32[32,8,128]{2,1,0:T(8,128)S(1)} all-to-all(f32[32,8,128]{2,1,0:T(8,128)S(1)} %bitcast.21), channel_id=1, replica_groups=mesh['group'=4,'dp'=8] {'dp','group'}, dimensions={0} | all-to-all | bytes 262144 | tf_op jit(solution)/shard_map/all_to_all | solution.py:348
  30.3 1.7 %query_grad.1 = (bf16[128,256]{1,0:T(8,128)(2,1)S(1)}, bf16[128,256]{1,0:T(8,128)(2,1)S(1)}, bf16[128,256]{1,0:T(8,128)(2,1)S(1)}, bf16[128,256]{1,0:T(8,128)(2,...) custom-call(f32[256,128]{1,0:T(8,128)S(1)} %bitcast.20, f32[48,128]{1,0:T(8,128)S(1)} %get-tuple-element.25.stats, ...), custom_call_target="tpu_custom_call" | custom-call | flops 536870912 | bytes 4194304 | tf_op jit(solution)/shard_map/query_grad/pallas_call | solution.py:350
  32.5 1.7 %collective-permute-start.5 = (bf16[128,256]{1,0:T(8,128)(2,1)S(1)}, bf16[128,256]{1,0:T(8,128)(2,1)S(1)}, u32[]{:S(2)}, u32[]{:S(2)}) collective-permute-start(bf16[128,256]{1,0:T(8,128)(2,1)S(1)} %get-tuple-element.36), channel_id=1, source_target_pairs={{0,24},{8,16},{16,8},{24,0},{1,25},{9,17},{17,9},{25,1},{2,26},{10... | collective-permute-start | bytes 196616 | tf_op jit(solution)/shard_map/ppermute | solution.py:297
  34.2 3.8 %passage_grad.1 = (bf16[2048,128]{1,0:T(8,128)(2,1)S(1)}, f32[128,768]{1,0:T(8,128)S(1)}) custom-call(bf16[16,1,1024]{2,1,0:T(2,128)(2,1)S(1)} %get-tuple-element.30.weights, bf16[2048,1024]{1,0:T(8,128)(2,1)S(1)} %get-tuple-element.27.shares, f32[2048,128]{1,0:T(8,128)S(1)} %get-tuple-element.31.pre, bf16[2048,768]{1,0:T(8,128)(2,1)S(1)} %bitcast.17, ...), custom_call_target="tpu_custom_call" | custom-call | flops 939524096 | bytes 8912896 | tf_op jit(solution)/shard_map/passage_grad/pallas_call | solution.py:382
  38.1 1.2 %query_back.1 = (bf16[256,128]{1,0:T(8,128)(2,1)S(1)}, bf16[768,128]{1,0:T(8,128)(2,1)}) custom-call(f32[256,128]{1,0:T(8,128)S(1)} %get-tuple-element.29.pre, bf16[256,768]{1,0:T(8,128)(2,1)S(1)} %bitcast.19, f32[128,768]{1,0:T(8,128)S(1)} %get-tuple-element.32.weight, bf16[128,256]{1,0:T(8,128)(2,1)S(1)} %get-tuple-element.33.refs_0_, ...), custom_call_target="tpu_custom_call" | custom-call | flops 50331648 | bytes 983040 | tf_op jit(solution)/shard_map/query_back/pallas_call | solution.py:403
  39.3 2.3 %all-to-all-start.1 = ((bf16[32,24,128]{2,1,0:T(8,128)(2,1)}), bf16[32,24,128]{2,1,0:T(8,128)(2,1)S(1)}, u32[]{:S(2)}, u32[]{:S(2)}) async-start(bf16[32,24,128]{2,1,0:T(8,128)(2,1)} %bitcast.5), calls=%async_computation.1 | async-start | bytes 393216 | tf_op jit(solution)/shard_map/all_to_all | solution.py:414
  41.6 9.2 %all-to-all-done.1.parts = bf16[32,24,128]{2,1,0:T(8,128)(2,1)S(1)} async-done(((bf16[32,24,128]{2,1,0:T(8,128)(2,1)}), bf16[32,24,128]{2,1,0:T(8,128)(2,1)S(1)}, u32[]{:S(2)}, u32[]{:S(2)}) %all-to-all-start.1) | async-done | bytes 196640 | tf_op jit(solution)/shard_map/all_to_all | solution.py:414
  50.9 0.7 %sum_parts.1 = bf16[32,24,128]{2,1,0:T(8,128)(2,1)} custom-call(bf16[32,24,128]{2,1,0:T(8,128)(2,1)S(1)} %all-to-all-done.1.parts), custom_call_target="tpu_custom_call" | custom-call | tf_op jit(solution)/shard_map/sum_parts/pallas_call | solution.py:415
  51.6 2.3 %all-to-all-start.2 = ((bf16[32,24,128]{2,1,0:T(8,128)(2,1)}), bf16[32,24,128]{2,1,0:T(8,128)(2,1)S(1)}, u32[]{:S(2)}, u32[]{:S(2)}) async-start(bf16[32,24,128]{2,1,0:T(8,128)(2,1)} %sum_parts.1), calls=%async_computation.2 | async-start | bytes 393216 | tf_op jit(solution)/shard_map/all_to_all | solution.py:423
  54.0 2.6 %convolution_convert_fusion = bf16[2048,768]{1,0:T(8,128)(2,1)} fusion(bf16[2048,128]{1,0:T(8,128)(2,1)S(1)} %get-tuple-element.39, bf16[768,128]{1,0:T(8,128)(2,1)S(1)} %copy-done.4), kind=kOutput, calls=%fused_computation | convolution fusion | flops 404226048 | bytes 3866624 | tf_op jit(solution)/shard_map/dot_general | solution.py:20
  56.6 0.6 dynamic-slice_bitcast_fusion
  57.2 1.0 %convolution_convert_fusion.1 = bf16[256,768]{1,0:T(8,128)(2,1)} fusion(bf16[256,128]{1,0:T(8,128)(2,1)S(1)} %get-tuple-element.38, bf16[768,128]{1,0:T(8,128)(2,1)S(1)} %copy-done.4), kind=kOutput, calls=%fused_computation.1 | convolution fusion | flops 50528256 | bytes 655360 | tf_op jit(solution)/shard_map/dot_general | solution.py:20
  58.2 4.9 %all-to-all-done.2 = bf16[32,24,128]{2,1,0:T(8,128)(2,1)S(1)} async-done(((bf16[32,24,128]{2,1,0:T(8,128)(2,1)}), bf16[32,24,128]{2,1,0:T(8,128)(2,1)S(1)}, u32[]{:S(2)}, u32[]{:S(2)}) %all-to-all-start.2) | async-done | bytes 196640 | tf_op jit(solution)/shard_map/all_to_all | solution.py:423
  63.1 0.8 %bitcast_convert_fusion = f32[768,128]{1,0:T(8,128)} fusion(bf16[32,24,128]{2,1,0:T(8,128)(2,1)S(1)} %all-to-all-done.2), kind=kLoop, calls=%fused_computation.2 | loop fusion | flops 98304 | bytes 589824 | tf_op jit(solution)/shard_map/convert_element_type | solution.py:424
  (25 shorter events, 0.7 us)
Async XLA Ops:
  0.6 11.7 %copy-start.9 = (s32[16]{0:T(128)S(1)}, s32[16]{0:T(128)}, u32[]{:S(2)}) copy-start(s32[16]{0:T(128)} %lens.1) | copy-start | bytes 196
  0.6 0.9 %copy-start.2 = (bf16[768,128]{1,0:T(8,128)(2,1)S(1)}, bf16[768,128]{1,0:T(8,128)(2,1)}, u32[]{:S(2)}) copy-start(bf16[768,128]{1,0:T(8,128)(2,1)} %projection.3) | copy-start | bytes 589828
  1.6 1.0 %copy-start.5 = (bf16[8,32,768]{2,1,0:T(8,128)(2,1)S(1)}, bf16[8,32,768]{2,1,0:T(8,128)(2,1)}, u32[]{:S(2)}) copy-start(bf16[8,32,768]{2,1,0:T(8,128)(2,1)} %param.6) | copy-start | bytes 1179652
  2.6 0.7 %copy-start.7 = (s32[8,32]{1,0:T(8,128)S(1)}, s32[8,32]{1,0:T(8,128)}, u32[]{:S(2)}) copy-start(s32[8,32]{1,0:T(8,128)} %hard_ids.1) | copy-start | bytes 3076
  3.3 0.7 %copy-start.8 = (s32[8]{0:T(128)S(1)}, s32[8]{0:T(128)}, u32[]{:S(2)}) copy-start(s32[8]{0:T(128)} %positive.1) | copy-start | bytes 100
  4.8 7.5 %collective-permute-start = (bf16[272,128]{1,0:T(8,128)(2,1)S(1)}, bf16[272,128]{1,0:T(8,128)(2,1)S(1)}, u32[]{:S(2)}, u32[]{:S(2)}) collective-permute-start(bf16[272,128]{1,0:T(8,128)(2,1)S(1)} %get-tuple-element.22.refs_0_), channel_id=1, source_target_pairs={{0,8},{8,0},{16,24},{24,16},{1,9},{9,1},{17,25},{25,17},{2,10},{10... | collective-permute-start | bytes 208904 | tf_op jit(solution)/shard_map/ppermute | solution.py:297
  4.9 7.4 %collective-permute-start.1 = (bf16[272,128]{1,0:T(8,128)(2,1)S(1)}, bf16[272,128]{1,0:T(8,128)(2,1)S(1)}, u32[]{:S(2)}, u32[]{:S(2)}) collective-permute-start(bf16[272,128]{1,0:T(8,128)(2,1)S(1)} %get-tuple-element.22.refs_0_), channel_id=1, source_target_pairs={{0,16},{8,24},{16,0},{24,8},{1,17},{9,25},{17,1},{25,9},{2,18},{10... | collective-permute-start | bytes 208904 | tf_op jit(solution)/shard_map/ppermute | solution.py:297
  7.6 4.7 %collective-permute-start.2 = (bf16[272,128]{1,0:T(8,128)(2,1)S(1)}, bf16[272,128]{1,0:T(8,128)(2,1)S(1)}, u32[]{:S(2)}, u32[]{:S(2)}) collective-permute-start(bf16[272,128]{1,0:T(8,128)(2,1)S(1)} %get-tuple-element.22.refs_0_), channel_id=1, source_target_pairs={{0,24},{8,16},{16,8},{24,0},{1,25},{9,17},{17,9},{25,1},{2,26},{10... | collective-permute-start | bytes 208904 | tf_op jit(solution)/shard_map/ppermute | solution.py:297
  7.6 1.9 %copy-start = (bf16[16,128,768]{2,1,0:T(8,128)(2,1)S(1)}, bf16[16,128,768]{2,1,0:T(8,128)(2,1)}, u32[]{:S(2)}) copy-start(bf16[16,128,768]{2,1,0:T(8,128)(2,1)} %param.7) | copy-start | bytes 9437188
  9.5 0.9 %copy-start.3 = (bf16[768,128]{1,0:T(8,128)(2,1)S(1)}, bf16[768,128]{1,0:T(8,128)(2,1)}, u32[]{:S(2)}) copy-start(bf16[768,128]{1,0:T(8,128)(2,1)} %projection.3) | copy-start | bytes 589828
  16.1 18.1 %copy-start.1 = (bf16[16,128,768]{2,1,0:T(8,128)(2,1)S(1)}, bf16[16,128,768]{2,1,0:T(8,128)(2,1)}, u32[]{:S(2)}) copy-start(bf16[16,128,768]{2,1,0:T(8,128)(2,1)} %param.7) | copy-start | bytes 9437188
  32.0 6.1 %collective-permute-start.3 = (bf16[128,256]{1,0:T(8,128)(2,1)S(1)}, bf16[128,256]{1,0:T(8,128)(2,1)S(1)}, u32[]{:S(2)}, u32[]{:S(2)}) collective-permute-start(bf16[128,256]{1,0:T(8,128)(2,1)S(1)} %get-tuple-element.34), channel_id=1, source_target_pairs={{0,8},{8,0},{16,24},{24,16},{1,9},{9,1},{17,25},{25,17},{2,10},{10... | collective-permute-start | bytes 196616 | tf_op jit(solution)/shard_map/ppermute | solution.py:297
  32.4 5.7 %collective-permute-start.4 = (bf16[128,256]{1,0:T(8,128)(2,1)S(1)}, bf16[128,256]{1,0:T(8,128)(2,1)S(1)}, u32[]{:S(2)}, u32[]{:S(2)}) collective-permute-start(bf16[128,256]{1,0:T(8,128)(2,1)S(1)} %get-tuple-element.35), channel_id=1, source_target_pairs={{0,16},{8,24},{16,0},{24,8},{1,17},{9,25},{17,1},{25,9},{2,18},{10... | collective-permute-start | bytes 196616 | tf_op jit(solution)/shard_map/ppermute | solution.py:297
  32.5 5.6 %collective-permute-start.5 = (bf16[128,256]{1,0:T(8,128)(2,1)S(1)}, bf16[128,256]{1,0:T(8,128)(2,1)S(1)}, u32[]{:S(2)}, u32[]{:S(2)}) collective-permute-start(bf16[128,256]{1,0:T(8,128)(2,1)S(1)} %get-tuple-element.36), channel_id=1, source_target_pairs={{0,24},{8,16},{16,8},{24,0},{1,25},{9,17},{17,9},{25,1},{2,26},{10... | collective-permute-start | bytes 196616 | tf_op jit(solution)/shard_map/ppermute | solution.py:297
  34.2 3.9 %copy-start.6 = (bf16[8,32,768]{2,1,0:T(8,128)(2,1)S(1)}, bf16[8,32,768]{2,1,0:T(8,128)(2,1)}, u32[]{:S(2)}) copy-start(bf16[8,32,768]{2,1,0:T(8,128)(2,1)} %param.6) | copy-start | bytes 1179652
  34.2 19.7 %copy-start.4 = (bf16[768,128]{1,0:T(8,128)(2,1)S(1)}, bf16[768,128]{1,0:T(8,128)(2,1)}, u32[]{:S(2)}) copy-start(bf16[768,128]{1,0:T(8,128)(2,1)} %projection.3) | copy-start | bytes 589828
  39.3 11.6 %all-to-all-start.1 = ((bf16[32,24,128]{2,1,0:T(8,128)(2,1)}), bf16[32,24,128]{2,1,0:T(8,128)(2,1)S(1)}, u32[]{:S(2)}, u32[]{:S(2)}) async-start(bf16[32,24,128]{2,1,0:T(8,128)(2,1)} %bitcast.5), calls=%async_computation.1 | async-start | bytes 393216 | tf_op jit(solution)/shard_map/all_to_all | solution.py:414
  51.6 11.5 %all-to-all-start.2 = ((bf16[32,24,128]{2,1,0:T(8,128)(2,1)}), bf16[32,24,128]{2,1,0:T(8,128)(2,1)S(1)}, u32[]{:S(2)}, u32[]{:S(2)}) async-start(bf16[32,24,128]{2,1,0:T(8,128)(2,1)} %sum_parts.1), calls=%async_computation.2 | async-start | bytes 393216 | tf_op jit(solution)/shard_map/all_to_all | solution.py:423

commit v3 on v2

v3 whole, which is shorter than its diff:
```python
import functools

import jax
import jax.numpy as jnp
from jax import lax
from jax.experimental import pallas as pl
from jax.experimental.pallas import tpu as pltpu
from jax.sharding import PartitionSpec as P

smooth_temp = 0.1
norm_eps = 1e-06
center = 0.375
lanes = 128
axes = ("dp", "group")
f32 = jnp.float32
bf16 = jnp.bfloat16


def dot(left, right, left_dim, right_dim):
    return lax.dot_general(
        left, right, (((left_dim,), (right_dim,)), ((), ())), preferred_element_type=f32
    )


def split_parts(value):
    high = value.astype(bf16)
    rest = value - high.astype(f32)
    middle = rest.astype(bf16)
    low = (rest - middle.astype(f32)).astype(bf16)
    return (high, middle, low)


def exact_dot(value, picks):
    return sum(dot(part, picks, 1, 0) for part in split_parts(value))


def normalize(projected):
    return projected * lax.rsqrt(jnp.sum(projected * projected, axis=-1, keepdims=True) + norm_eps)


def normalize_back(projected, grad):
    inverse = lax.rsqrt(jnp.sum(projected * projected, axis=-1, keepdims=True) + norm_eps)
    along = jnp.sum(projected * grad, axis=-1, keepdims=True)
    return grad * inverse - projected * (inverse * inverse * inverse * along)


def iota(shape, dim):
    return lax.broadcasted_iota(jnp.int32, shape, dim)


def params(megabytes):
    return pltpu.CompilerParams(vmem_limit_bytes=megabytes * 2**20)


def cost(flops, nbytes, exps=0):
    return pl.CostEstimate(flops=int(flops), bytes_accessed=int(nbytes), transcendentals=int(exps))


VMEM = pl.BlockSpec(memory_space=pltpu.VMEM)
SMEM = pl.BlockSpec(memory_space=pltpu.SMEM)
HBM = pl.BlockSpec(memory_space=pltpu.HBM)


def in_hbm(*values):
    return [pltpu.with_memory_space_constraint(value, pltpu.HBM) for value in values]


def query_kernel(
    hidden_hbm, projection_hbm, ids_hbm, positive_hbm, pre_out, packed_out, hidden, projection, hard_ids, positive, sems
):
    copies = [
        pltpu.make_async_copy(source, target, sems.at[k])
        for k, (source, target) in enumerate(
            [
                (projection_hbm, projection),
                (hidden_hbm, hidden),
                (ids_hbm, hard_ids),
                (positive_hbm, positive),
            ]
        )
    ]
    for copy in copies:
        copy.start()
    for copy in copies[2:]:
        copy.wait()
    rows = hidden.shape[0]
    count, slots = hard_ids.shape
    row = iota((count, lanes), 0)
    column = iota((count, lanes), 1)
    marks = jnp.full((count, lanes), -1.0, f32)
    for k in range(count):
        marks = jnp.where((row == k) & (column == slots), positive[k].astype(f32), marks)
    ids = jnp.concatenate(
        [hard_ids[...].astype(f32), jnp.full((count, lanes - slots), -1.0, f32)], axis=1
    )
    marks = jnp.where(column < slots, ids, marks)
    extra = packed_out.shape[0] - rows
    marks = jnp.concatenate([marks, jnp.full((extra - count, lanes), -1.0, f32)], axis=0)
    packed_out[rows:, :] = marks.astype(bf16)
    for copy in copies[:2]:
        copy.wait()
    pre = dot(hidden[...], projection[...], 1, 0)
    pre_out[...] = pre
    packed_out[:rows, :] = normalize(pre).astype(bf16)


def passage_kernel(step, hidden, projection_hbm, pre_out, embed_out, projection, sem):
    copy = pltpu.make_async_copy(projection_hbm, projection, sem)
    copy.start()
    copy.wait()
    for start in range(0, hidden.shape[0], step):
        part = slice(start, start + step)
        pre = dot(hidden[part, :], projection[...], 1, 0)
        pre_out[part, :] = pre
        embed_out[part, :] = normalize(pre).astype(bf16)


def token_picks(groups, count, length, width, rows_first):
    me = lax.axis_index("group")
    tokens = groups * count * length
    shape = (tokens, width) if rows_first else (width, tokens)
    token = iota(shape, 0 if rows_first else 1)
    query = iota(shape, 1 if rows_first else 0)
    member = jnp.bitwise_xor(token // (count * length), me)
    owner = member * count + (token % (count * length)) // length
    return jnp.where(owner == query, 1.0, 0.0).astype(bf16)


def forward_kernel(dims, lens, *refs):
    groups, count, length, passages, tokens, slots, step = dims
    packed = refs[:groups]
    embed, shares_out, inverse_out, stats_out, packet_out, summed, marks = refs[groups:]
    rows = count * length
    me = lax.axis_index("group")
    marks[...] = jnp.full(marks.shape, -1.0, f32)
    for k in range(groups):
        member = jnp.bitwise_xor(me, k)
        start = pl.multiple_of(member * count, count)
        marks[pl.ds(start, count), :] = packed[k][rows:, :].astype(f32)[:count]

    @pl.loop(0, passages // step, unroll=True)
    def _(at):
        start = pl.multiple_of(at * (step * tokens), step * tokens)
        part = embed[pl.ds(start, step * tokens), :]
        for k in range(groups):
            similar = dot(part, packed[k][:rows, :], 1, 1)
            for p in range(step):
                piece = similar[p * tokens : (p + 1) * tokens, :]
                alive = iota(piece.shape, 0) < lens[at * step + p]
                grown = jnp.where(alive, jnp.exp(piece * (1.0 / smooth_temp)), 0.0)
                shares_out[pl.ds(start + p * tokens, tokens), k * rows : (k + 1) * rows] = (
                    grown.astype(bf16)
                )
                summed[pl.ds(at * step + p, 1), k * rows : (k + 1) * rows] = jnp.sum(
                    grown, axis=0, keepdims=True
                )

    total = summed[...]
    inverse_out[...] = 1.0 / total
    width = marks.shape[0]
    scores = exact_dot(
        smooth_temp * jnp.log(total), token_picks(groups, count, length, width, True)
    )
    marks_t = marks[...].T
    ids = marks_t[:slots, :]
    first = me * passages
    counts = jnp.concatenate(
        [
            jnp.sum(jnp.where(ids == (first + p).astype(f32), 1.0, 0.0), axis=0, keepdims=True)
            for p in range(passages)
        ],
        axis=0,
    )
    here = (iota((passages, width), 0) + first).astype(f32)
    chosen = here == marks_t[slots : slots + 1, :]
    grown = jnp.exp(scores - center * length)
    boost = groups * passages / slots
    boosted = jnp.where(chosen, 0.0, boost * counts)
    stats_out[:passages, :] = grown
    stats_out[passages : 2 * passages, :] = boosted
    stats_out[2 * passages :, :] = jnp.where(chosen, 1.0, 0.0)
    plain = jnp.sum(grown, axis=0, keepdims=True)
    hard = jnp.sum(boosted * grown * grown, axis=0, keepdims=True)
    kept = jnp.sum(jnp.where(chosen, scores, 0.0), axis=0, keepdims=True)
    sums = jnp.sum(counts * grown, axis=0, keepdims=True)
    sums = jnp.broadcast_to(jnp.sum(sums, axis=1, keepdims=True), sums.shape)
    queries = groups * count
    if packet_out.shape[1] == 1:
        lane = iota(plain.shape, 1)
        packet = jnp.where(lane < queries, plain, sums)
        packet = jnp.where(lane // queries == 1, pltpu.roll(hard, queries, 1), packet)
        packet = jnp.where(lane // queries == 2, pltpu.roll(kept, 2 * queries, 1), packet)
    else:
        packet = jnp.concatenate([plain, hard, kept, sums] * 2, axis=0)
    for k in range(packet_out.shape[0]):
        packet_out[k] = packet


def query_grad_kernel(dims, packets, stats, inverse, shares, embed, *refs):
    groups, count, length, passages, tokens, slots, step = dims
    parts_out = refs[:groups]
    weights, losses_out, running = refs[groups:]
    rows = count * length
    width = stats.shape[1]
    devices = packets.shape[0]
    dp = lax.axis_index("dp")
    pool = packets[pl.ds(dp * groups, groups)].sum(axis=0)
    every = packets[...].sum(axis=0)
    queries = groups * count
    if packets.shape[1] == 1:
        plain, hard, kept = pool, pltpu.roll(pool, width - queries, 1), pltpu.roll(pool, width - 2 * queries, 1)
        sums = every[:, 3 * queries : 3 * queries + 1]
    else:
        plain, hard, kept, sums = pool[0:1, :], pool[1:2, :], pool[2:3, :], every[3:4, 0:1]
    hard_mean = sums * (1.0 / (devices * count * slots))
    partition = jnp.where(iota(plain.shape, 1) < queries, plain + hard / hard_mean, 1.0)
    losses_out[...] = jnp.broadcast_to(
        jnp.log(partition) - (kept - center * length), losses_out.shape
    )
    grown = stats[:passages, :]
    boosted = stats[passages : 2 * passages, :]
    chosen = stats[2 * passages :, :]
    grad = grown * (1.0 + boosted * grown / hard_mean) / partition - chosen
    spread = exact_dot(grad, token_picks(groups, count, length, width, False))
    found = (spread * inverse[...]).astype(bf16)
    for p in range(passages):
        weights[p] = found[p : p + 1, :]
    running[...] = jnp.zeros(running.shape, f32)

    @pl.loop(0, passages // step, unroll=True)
    def _(at):
        start = pl.multiple_of(at * (step * tokens), step * tokens)
        running[...] += dot(
            embed[pl.ds(start, step * tokens), :].T,
            coefficients(dims, shares, weights, at),
            1,
            0,
        )

    for k in range(groups):
        parts_out[k][...] = running[:, k * rows : (k + 1) * rows].astype(bf16)


def coefficients(dims, shares, weights, at):
    passages, tokens, _, step = dims[3:]
    start = pl.multiple_of(at * (step * tokens), step * tokens)
    return jnp.concatenate(
        [
            shares[pl.ds(start + p * tokens, tokens), :] * weights[at * step + p]
            for p in range(step)
        ],
        axis=0,
    )


def passage_grad_kernel(dims, weights, shares, pre, hidden, query_pre, query_hidden, *refs):
    groups, count, length, passages, tokens, slots, step = dims
    packed = refs[:groups]
    back_out, weight_out, pre_out, hidden_out, queries, running = refs[groups:]
    rows = count * length
    for k in range(groups):
        queries[k * rows : (k + 1) * rows, :] = packed[k][:rows, :]
    running[...] = jnp.zeros(running.shape, f32)

    @pl.loop(0, passages // step, unroll=True)
    def _(at):
        part = pl.ds(pl.multiple_of(at * (step * tokens), step * tokens), step * tokens)
        grad = dot(coefficients(dims, shares, weights, at), queries[...], 1, 0)
        back = normalize_back(pre[part, :], grad).astype(bf16)
        back_out[part, :] = back
        running[...] += dot(back.T, hidden[part, :], 1, 0)

    weight_out[...] = running[...].T
    pre_out[...] = query_pre[...].T
    hidden_out[...] = query_hidden[...].T


def query_back_kernel(pre, hidden, weight, *refs):
    parts = refs[:-2]
    back_out, weight_out = refs[-2:]
    grad = sum(part[...].astype(f32) for part in parts)
    projected = pre[...]
    inverse = lax.rsqrt(jnp.sum(projected * projected, axis=0, keepdims=True) + norm_eps)
    along = jnp.sum(projected * grad, axis=0, keepdims=True)
    back = (grad * inverse - projected * (inverse * inverse * inverse * along)).astype(bf16)
    back_out[...] = back
    weight_out[...] = (weight[...] + dot(hidden[...], back, 1, 1)).astype(bf16)


def sum_kernel(parts, copies_out):
    devices = copies_out.shape[0]
    total = parts[0].astype(f32)
    for k in range(1, devices):
        total += parts[k].astype(f32)
    total = total.astype(bf16)
    for k in range(devices):
        copies_out[k] = total


def local(query_hidden, passage_hidden, projection, positive, hard_ids, passage_len):
    count, length, width = query_hidden.shape
    passages, tokens, _ = passage_hidden.shape
    depth = projection.shape[1]
    slots = hard_ids.shape[1]
    groups = lax.axis_size("group")
    devices = lax.axis_size(axes)
    rows = count * length
    all_rows = groups * rows
    passage_rows = passages * tokens
    pool_width = -(-groups * count // lanes) * lanes
    packet_rows = 1 if 3 * groups * count < lanes else 8
    step = 4 if groups <= 4 else 1
    dims = (groups, count, length, passages, tokens, slots, step)
    query_flat = query_hidden.reshape(rows, width)
    passage_flat = passage_hidden.reshape(passage_rows, width)
    shape = jax.ShapeDtypeStruct

    query_pre, packed = pl.pallas_call(
        query_kernel,
        out_shape=(shape((rows, depth), f32), shape((rows + 16, depth), bf16)),
        in_specs=[HBM] * 4,
        out_specs=(VMEM, VMEM),
        scratch_shapes=[
            pltpu.VMEM((rows, width), bf16),
            pltpu.VMEM((width, depth), bf16),
            pltpu.VMEM((count, slots), jnp.int32),
            pltpu.SMEM((count,), jnp.int32),
            pltpu.SemaphoreType.DMA((4,)),
        ],
        compiler_params=params(16),
        cost_estimate=cost(2 * rows * width * depth, rows * width * 2),
        name="query_embed",
    )(*in_hbm(query_flat, projection, hard_ids, positive))

    def swap(value, k):
        return lax.ppermute(value, "group", [(i, i ^ k) for i in range(groups)])

    blocks = [packed] + [swap(packed, k) for k in range(1, groups)]

    passage_pre, passage_embed = pl.pallas_call(
        functools.partial(passage_kernel, 4 * tokens),
        out_shape=(shape((passage_rows, depth), f32), shape((passage_rows, depth), bf16)),
        in_specs=[VMEM, HBM],
        out_specs=(VMEM, VMEM),
        scratch_shapes=[pltpu.VMEM((width, depth), bf16), pltpu.SemaphoreType.DMA],
        compiler_params=params(16),
        cost_estimate=cost(2 * passage_rows * width * depth, passage_rows * (width * 2 + depth * 6)),
        name="passage_embed",
    )(passage_flat, *in_hbm(projection))

    shares, inverse, stats, packets = pl.pallas_call(
        functools.partial(forward_kernel, dims),
        out_shape=(
            shape((passage_rows, all_rows), bf16),
            shape((passages, all_rows), f32),
            shape((3 * passages, pool_width), f32),
            shape((devices, packet_rows, pool_width), f32),
        ),
        in_specs=[SMEM] + [VMEM] * (groups + 1),
        out_specs=(VMEM, VMEM, VMEM, VMEM),
        scratch_shapes=[
            pltpu.VMEM((passages, all_rows), f32),
            pltpu.VMEM((pool_width, lanes), f32),
        ],
        compiler_params=params(32),
        cost_estimate=cost(
            2 * passage_rows * all_rows * depth,
            passage_rows * all_rows * 2,
            passage_rows * all_rows,
        ),
        name="forward",
    )(passage_len, *blocks, passage_embed)

    packets = lax.all_to_all(packets, axes, 0, 0, tiled=True)

    outs = pl.pallas_call(
        functools.partial(query_grad_kernel, dims),
        out_shape=(
            *[shape((depth, rows), bf16)] * groups,
            shape((passages, 1, all_rows), bf16),
            shape((8, pool_width), f32),
        ),
        in_specs=[VMEM] * 5,
        out_specs=(VMEM,) * (groups + 2),
        scratch_shapes=[pltpu.VMEM((depth, all_rows), f32)],
        compiler_params=params(32),
        cost_estimate=cost(2 * passage_rows * all_rows * depth, passage_rows * all_rows * 2),
        name="query_grad",
    )(packets, stats, inverse, shares, passage_embed)
    parts = outs[:groups]
    weights, losses = outs[groups:]
    parts = [parts[0]] + [swap(parts[k], k) for k in range(1, groups)]

    passage_back, weight, pre_t, hidden_t = pl.pallas_call(
        functools.partial(passage_grad_kernel, dims),
        out_shape=(
            shape((passage_rows, depth), bf16),
            shape((width, depth), f32),
            shape((depth, rows), f32),
            shape((width, rows), bf16),
        ),
        in_specs=[VMEM] * (6 + groups),
        out_specs=(VMEM,) * 4,
        scratch_shapes=[pltpu.VMEM((all_rows, depth), bf16), pltpu.VMEM((depth, width), f32)],
        compiler_params=params(32),
        cost_estimate=cost(
            2 * passage_rows * (all_rows + width) * depth,
            passage_rows * (all_rows * 2 + width * 2 + depth * 6),
        ),
        name="passage_grad",
    )(weights, shares, passage_pre, passage_flat, query_pre, query_flat, *blocks)

    query_back, weight = pl.pallas_call(
        query_back_kernel,
        out_shape=(shape((depth, rows), bf16), shape((width, depth), bf16)),
        in_specs=[VMEM] * (3 + groups),
        out_specs=(VMEM, VMEM),
        compiler_params=params(16),
        cost_estimate=cost(2 * rows * width * depth, width * depth * 6 + rows * width * 2),
        name="query_back",
    )(pre_t, hidden_t, weight, *parts)

    weight = weight.reshape(devices, width // devices, depth)
    weight = lax.all_to_all(weight, axes, 0, 0, tiled=True)
    copies = pl.pallas_call(
        sum_kernel,
        out_shape=shape(weight.shape, bf16),
        in_specs=[VMEM],
        out_specs=VMEM,
        compiler_params=params(16),
        name="sum_parts",
    )(weight)
    copies = lax.all_to_all(copies, axes, 0, 0, tiled=True)
    grad_proj = copies.reshape(width, depth).astype(f32)

    grad_query = dot(query_back, projection, 0, 1).astype(bf16).reshape(query_hidden.shape)
    grad_passage = dot(passage_back, projection, 1, 1).astype(bf16).reshape(passage_hidden.shape)
    own = lax.axis_index("group") * count
    return (lax.dynamic_slice(losses[0], (own,), (count,)), grad_proj, grad_query, grad_passage)


def solution(mesh):
    in_specs = (
        P(axes, None, None),
        P(axes, None, None),
        P(),
        P(axes),
        P(axes, None),
        P(axes),
    )
    out_specs = (P(axes), P(), P(axes, None, None), P(axes, None, None))
    return jax.shard_map(local, mesh=mesh, in_specs=in_specs, out_specs=out_specs, check_vma=False)
```

time: 64.3 us -> 57.9 us (0.900)
  local copies, waits for them, and re-layouts: 6.68 us -> 2.49 us
  Pallas kernels: 13.9 us -> 11.9 us
  blocking collectives: 14.2 us -> 12.6 us
  waiting for transfers between devices: 14.2 us -> 15.3 us
    unnamed x20 -> x10, local copies, waits for them, and re-layouts: 6.1 us -> 1.91 us
    all_to_all x1, blocking collectives: 14.2 us -> 12.6 us  [local(): packets = lax.all_to_all(packets, axes, 0, 0, tiled=True)]
    pallas_call x1, Pallas kernels: 3.83 us -> 2.59 us  [local(): pl.pallas_call(functools.partial(passage_grad_kernel, dims), out_shape=(s...]
    ppermute x6, waiting for transfers between devices: 0.02 us -> 1.08 us  [swap(): return lax.ppermute(value, 'group', [(i, i ^ k) for i in range(groups)])]
    pallas_call x1, Pallas kernels: 3.74 us -> 3.01 us  [local(): pl.pallas_call(functools.partial(forward_kernel, dims), out_shape=(shape(...]
  transfers between devices with their start and end apart: 8 -> 8, of which waited for: 2 -> 4; matrix products, arithmetic and copies ran while one was open for 7% -> 7% of each run, Pallas kernels for 9% -> 8%
where the time goes in v3:
time: 57.9 us; the launch traced here: 57.6 us
  waiting for transfers between devices  15.3 us (26%)
  blocking collectives  12.6 us (22%)
  Pallas kernels  11.9 us (21%)
  starting transfers between devices  9.99 us (17%)
  matrix products  3.69 us (6%)
  local copies, waits for them, and re-layouts  2.49 us (4%)
  other arithmetic  0.78 us (1%)
  between operations  0.77 us (1%)
    all_to_all x1, blocking collectives, local(): packets = lax.all_to_all(packets, axes, 0, 0, tiled=True)  12.6 us
    all_to_all x1, waiting for transfers between devices, local(): weight = lax.all_to_all(weight, axes, 0, 0, tiled=True)  9.36 us
    ppermute x6, starting transfers between devices, swap(): return lax.ppermute(value, 'group', [(i, i ^ k) for i in range(groups)])  5.25 us
    all_to_all x1, waiting for transfers between devices, local(): copies = lax.all_to_all(copies, axes, 0, 0, tiled=True)  4.89 us
    dot_general x2, matrix products, dot(): lax.dot_general(left, right, (((left_dim,), (right_dim,)), ((), ())), pre...  3.69 us
    pallas_call x1, Pallas kernels, local(): pl.pallas_call(functools.partial(forward_kernel, dims), out_shape=(shape(...  3.01 us
    pallas_call x1, Pallas kernels, local(): pl.pallas_call(functools.partial(passage_grad_kernel, dims), out_shape=(s...  2.59 us
    all_to_all x1, starting transfers between devices, local(): weight = lax.all_to_all(weight, axes, 0, 0, tiled=True)  2.42 us
  transfers between devices with their start and end apart: 8, of which 4 were waited for; matrix products, arithmetic and copies ran while one was open for 7% of the time, Pallas kernels for 8%

profile of v3, /device:TPU:1, one launch (start us, length us, event | category | flops | bytes accessed | tf_op | source)
XLA Modules:
  0.0 57.6 jit_solution(1741469578789524071)
XLA Ops:
  0.6 1.5 %query_embed.1 = (f32[256,128]{1,0:T(8,128)S(1)}, bf16[272,128]{1,0:T(8,128)(2,1)S(1)}) custom-call(bf16[256,768]{1,0:T(8,128)(2,1)} %bitcast.16, bf16[768,128]{1,0:T(8,128)(2,1)} %projection_hbm.3, s32[8,32]{1,0:T(8,128)} %ids_hbm.1, s32[8]{0:T(128)} %positive_hbm.1), custom_call_target="tpu_custom_call" | custom-call | flops 50331648 | bytes 393216 | tf_op jit(solution)/shard_map/query_embed/pallas_call | solution.py:318
  2.1 0.1 collective-permute-start
  2.2 2.7 %collective-permute-start.1 = (bf16[272,128]{1,0:T(8,128)(2,1)S(1)}, bf16[272,128]{1,0:T(8,128)(2,1)S(1)}, u32[]{:S(2)}, u32[]{:S(2)}) collective-permute-start(bf16[272,128]{1,0:T(8,128)(2,1)S(1)} %get-tuple-element.24.refs_0_), channel_id=1, source_target_pairs={{0,16},{8,24},{16,0},{24,8},{1,17},{9,25},{17,1},{25,9},{2,18},{10... | collective-permute-start | bytes 208904 | tf_op jit(solution)/shard_map/ppermute | solution.py:336
  5.0 1.9 %copy-done = bf16[16,128,768]{2,1,0:T(8,128)(2,1)S(1)} copy-done((bf16[16,128,768]{2,1,0:T(8,128)(2,1)S(1)}, bf16[16,128,768]{2,1,0:T(8,128)(2,1)}, u32[]{:S(2)}) %copy-start) | copy-done | bytes 3145752
  6.9 2.0 %passage_embed.1 = (f32[2048,128]{1,0:T(8,128)S(1)}, bf16[2048,128]{1,0:T(8,128)(2,1)S(1)}) custom-call(bf16[2048,768]{1,0:T(8,128)(2,1)S(1)} %bitcast.14, bf16[768,128]{1,0:T(8,128)(2,1)} %projection_hbm.3), custom_call_target="tpu_custom_call" | custom-call | flops 402653184 | bytes 4718592 | tf_op jit(solution)/shard_map/passage_embed/pallas_call | solution.py:340
  8.9 0.2 collective-permute-done.2.refs_3_
  9.1 3.0 %forward.1 = (bf16[2048,1024]{1,0:T(8,128)(2,1)S(1)}, f32[16,1024]{1,0:T(8,128)S(1)}, f32[48,128]{1,0:T(8,128)S(1)}, f32[32,1,128]{2,1,0:T(1,128)S(1)}) custom-call(s32[16]{0:T(128)S(1)} %copy-done.3, bf16[272,128]{1,0:T(8,128)(2,1)S(1)} %get-tuple-element.24.refs_0_, bf16[272,128]{1,0:T(8,128)(2,1)S(1)} %collective-permute-done.refs_1_, ...), custom_call_target="tpu_custom_call" | custom-call | flops 536870912 | bytes 4194304 | tf_op jit(solution)/shard_map/forward/pallas_call | solution.py:351
  12.1 12.6 %all_to_all.15.packets = f32[32,1,128]{2,1,0:T(1,128)S(1)} all-to-all(f32[32,1,128]{2,1,0:T(1,128)S(1)} %get-tuple-element.26), channel_id=1, replica_groups=mesh['group'=4,'dp'=8] {'dp','group'}, dimensions={0} | all-to-all | bytes 32768 | tf_op jit(solution)/shard_map/all_to_all | solution.py:374
  24.7 1.1 %query_grad.1 = (bf16[128,256]{1,0:T(8,128)(2,1)S(1)}, bf16[128,256]{1,0:T(8,128)(2,1)S(1)}, bf16[128,256]{1,0:T(8,128)(2,1)S(1)}, bf16[128,256]{1,0:T(8,128)(2,...) custom-call(f32[32,1,128]{2,1,0:T(1,128)S(1)} %all_to_all.15.packets, ...), custom_call_target="tpu_custom_call" | custom-call | flops 536870912 | bytes 4194304 | tf_op jit(solution)/shard_map/query_grad/pallas_call | solution.py:376
  25.8 0.7 %collective-permute-start.3 = (bf16[128,256]{1,0:T(8,128)(2,1)S(1)}, bf16[128,256]{1,0:T(8,128)(2,1)S(1)}, u32[]{:S(2)}, u32[]{:S(2)}) collective-permute-start(bf16[128,256]{1,0:T(8,128)(2,1)S(1)} %get-tuple-element.38), channel_id=1, source_target_pairs={{0,8},{8,0},{16,24},{24,16},{1,9},{9,1},{17,25},{25,17},{2,10},{10... | collective-permute-start | bytes 196616 | tf_op jit(solution)/shard_map/ppermute | solution.py:336
  26.5 0.3 collective-permute-start.4
  26.8 1.4 %collective-permute-start.5 = (bf16[128,256]{1,0:T(8,128)(2,1)S(1)}, bf16[128,256]{1,0:T(8,128)(2,1)S(1)}, u32[]{:S(2)}, u32[]{:S(2)}) collective-permute-start(bf16[128,256]{1,0:T(8,128)(2,1)S(1)} %get-tuple-element.40), channel_id=1, source_target_pairs={{0,24},{8,16},{16,8},{24,0},{1,25},{9,17},{17,9},{25,1},{2,26},{10... | collective-permute-start | bytes 196616 | tf_op jit(solution)/shard_map/ppermute | solution.py:336
  28.2 2.6 %passage_grad.1 = (bf16[2048,128]{1,0:T(8,128)(2,1)S(1)}, f32[768,128]{1,0:T(8,128)S(1)}, f32[128,256]{1,0:T(8,128)S(1)}, bf16[768,256]{1,0:T(8,128)(2,1)S(1)}) custom-call(bf16[16,1,1024]{2,1,0:T(2,128)(2,1)S(1)} %get-tuple-element.31.weights, bf16[2048,1024]{1,0:T(8,128)(2,1)S(1)} %get-tuple-element.29.shares, f32[2048,128]{1,0:T(8,128)S(1)} %get-tuple-element.32.pre, ...), custom_call_target="tpu_custom_call" | custom-call | flops 939524096 | bytes 8912896 | tf_op jit(solution)/shard_map/passage_grad/pallas_call | solution.py:394
  30.9 0.9 %collective-permute-done.5.refs_3_ = bf16[128,256]{1,0:T(8,128)(2,1)S(1)} collective-permute-done((bf16[128,256]{1,0:T(8,128)(2,1)S(1)}, bf16[128,256]{1,0:T(8,128)(2,1)S(1)}, u32[]{:S(2)}, u32[]{:S(2)}) %collective-permute-start.5) | collective-permute-done | bytes 65568 | tf_op jit(solution)/shard_map/ppermute | solution.py:336
  31.8 1.0 %query_back.1 = (bf16[128,256]{1,0:T(8,128)(2,1)S(1)}, bf16[768,128]{1,0:T(8,128)(2,1)}) custom-call(f32[128,256]{1,0:T(8,128)S(1)} %get-tuple-element.34.pre, bf16[768,256]{1,0:T(8,128)(2,1)S(1)} %get-tuple-element.35.hidden, f32[768,128]{1,0:T(8,128)S(1)} %get-tuple-element.36.weight, bf16[128,256]{1,0:T(8,128)(2,1)S(1)} %get-tuple-element.37.refs_0_, ...), custom_call_target="tpu_custom_call" | custom-call | flops 50331648 | bytes 983040 | tf_op jit(solution)/shard_map/query_back/pallas_call | solution.py:413
  32.8 2.4 %all-to-all-start.1 = ((bf16[32,24,128]{2,1,0:T(8,128)(2,1)}), bf16[32,24,128]{2,1,0:T(8,128)(2,1)S(1)}, u32[]{:S(2)}, u32[]{:S(2)}) async-start(bf16[32,24,128]{2,1,0:T(8,128)(2,1)} %bitcast.3), calls=%async_computation.1 | async-start | bytes 393216 | tf_op jit(solution)/shard_map/all_to_all | solution.py:424
  35.2 9.4 %all-to-all-done.1.parts = bf16[32,24,128]{2,1,0:T(8,128)(2,1)S(1)} async-done(((bf16[32,24,128]{2,1,0:T(8,128)(2,1)}), bf16[32,24,128]{2,1,0:T(8,128)(2,1)S(1)}, u32[]{:S(2)}, u32[]{:S(2)}) %all-to-all-start.1) | async-done | bytes 196640 | tf_op jit(solution)/shard_map/all_to_all | solution.py:424
  44.6 0.7 %sum_parts.1 = bf16[32,24,128]{2,1,0:T(8,128)(2,1)} custom-call(bf16[32,24,128]{2,1,0:T(8,128)(2,1)S(1)} %all-to-all-done.1.parts), custom_call_target="tpu_custom_call" | custom-call | tf_op jit(solution)/shard_map/sum_parts/pallas_call | solution.py:425
  45.3 2.3 %all-to-all-start.2 = ((bf16[32,24,128]{2,1,0:T(8,128)(2,1)}), bf16[32,24,128]{2,1,0:T(8,128)(2,1)S(1)}, u32[]{:S(2)}, u32[]{:S(2)}) async-start(bf16[32,24,128]{2,1,0:T(8,128)(2,1)} %sum_parts.1), calls=%async_computation.2 | async-start | bytes 393216 | tf_op jit(solution)/shard_map/all_to_all | solution.py:433
  47.6 2.7 %convolution_convert_fusion = bf16[2048,768]{1,0:T(8,128)(2,1)} fusion(bf16[2048,128]{1,0:T(8,128)(2,1)S(1)} %get-tuple-element.43, bf16[768,128]{1,0:T(8,128)(2,1)S(1)} %copy-done.4), kind=kOutput, calls=%fused_computation | convolution fusion | flops 404226048 | bytes 3866624 | tf_op jit(solution)/shard_map/dot_general | solution.py:20
  50.3 0.6 %dynamic-slice_bitcast_fusion = f32[8]{0:T(128)} fusion(f32[1,128]{1,0:T(1,128)S(1)} %slice.3, s32[]{:T(128)S(6)} %select_n.3), kind=kLoop, calls=%fused_computation.3 | loop fusion | bytes 68 | tf_op jit(solution)/shard_map/dynamic_slice | solution.py:439
  50.9 1.0 %convolution_convert_fusion.1 = bf16[256,768]{1,0:T(8,128)(2,1)} fusion(bf16[128,256]{1,0:T(8,128)(2,1)S(1)} %get-tuple-element.42, bf16[768,128]{1,0:T(8,128)(2,1)S(1)} %copy-done.4), kind=kOutput, calls=%fused_computation.1 | convolution fusion | flops 50528256 | bytes 655360 | tf_op jit(solution)/shard_map/dot_general | solution.py:20
  51.9 4.9 %all-to-all-done.2 = bf16[32,24,128]{2,1,0:T(8,128)(2,1)S(1)} async-done(((bf16[32,24,128]{2,1,0:T(8,128)(2,1)}), bf16[32,24,128]{2,1,0:T(8,128)(2,1)S(1)}, u32[]{:S(2)}, u32[]{:S(2)}) %all-to-all-start.2) | async-done | bytes 196640 | tf_op jit(solution)/shard_map/all_to_all | solution.py:433
  56.8 0.8 %bitcast_convert_fusion = f32[768,128]{1,0:T(8,128)} fusion(bf16[32,24,128]{2,1,0:T(8,128)(2,1)S(1)} %all-to-all-done.2), kind=kLoop, calls=%fused_computation.2 | loop fusion | flops 98304 | bytes 589824 | tf_op jit(solution)/shard_map/convert_element_type | solution.py:434
  (15 shorter events, 0.1 us)
Async XLA Ops:
  0.6 8.4 %copy-start.3 = (s32[16]{0:T(128)S(1)}, s32[16]{0:T(128)}, u32[]{:S(2)}) copy-start(s32[16]{0:T(128)} %lens.1) | copy-start | bytes 196
  2.1 6.7 %collective-permute-start = (bf16[272,128]{1,0:T(8,128)(2,1)S(1)}, bf16[272,128]{1,0:T(8,128)(2,1)S(1)}, u32[]{:S(2)}, u32[]{:S(2)}) collective-permute-start(bf16[272,128]{1,0:T(8,128)(2,1)S(1)} %get-tuple-element.24.refs_0_), channel_id=1, source_target_pairs={{0,8},{8,0},{16,24},{24,16},{1,9},{9,1},{17,25},{25,17},{2,10},{10... | collective-permute-start | bytes 208904 | tf_op jit(solution)/shard_map/ppermute | solution.py:336
  2.2 6.6 %collective-permute-start.1 = (bf16[272,128]{1,0:T(8,128)(2,1)S(1)}, bf16[272,128]{1,0:T(8,128)(2,1)S(1)}, u32[]{:S(2)}, u32[]{:S(2)}) collective-permute-start(bf16[272,128]{1,0:T(8,128)(2,1)S(1)} %get-tuple-element.24.refs_0_), channel_id=1, source_target_pairs={{0,16},{8,24},{16,0},{24,8},{1,17},{9,25},{17,1},{25,9},{2,18},{10... | collective-permute-start | bytes 208904 | tf_op jit(solution)/shard_map/ppermute | solution.py:336
  4.9 4.1 %collective-permute-start.2 = (bf16[272,128]{1,0:T(8,128)(2,1)S(1)}, bf16[272,128]{1,0:T(8,128)(2,1)S(1)}, u32[]{:S(2)}, u32[]{:S(2)}) collective-permute-start(bf16[272,128]{1,0:T(8,128)(2,1)S(1)} %get-tuple-element.24.refs_0_), channel_id=1, source_target_pairs={{0,24},{8,16},{16,8},{24,0},{1,25},{9,17},{17,9},{25,1},{2,26},{10... | collective-permute-start | bytes 208904 | tf_op jit(solution)/shard_map/ppermute | solution.py:336
  5.0 1.9 %copy-start = (bf16[16,128,768]{2,1,0:T(8,128)(2,1)S(1)}, bf16[16,128,768]{2,1,0:T(8,128)(2,1)}, u32[]{:S(2)}) copy-start(bf16[16,128,768]{2,1,0:T(8,128)(2,1)} %param.7) | copy-start | bytes 9437188
  12.1 16.2 %copy-start.1 = (bf16[16,128,768]{2,1,0:T(8,128)(2,1)S(1)}, bf16[16,128,768]{2,1,0:T(8,128)(2,1)}, u32[]{:S(2)}) copy-start(bf16[16,128,768]{2,1,0:T(8,128)(2,1)} %param.7) | copy-start | bytes 9437188
  12.1 16.2 %copy-start.2 = (bf16[8,32,768]{2,1,0:T(8,128)(2,1)S(1)}, bf16[8,32,768]{2,1,0:T(8,128)(2,1)}, u32[]{:S(2)}) copy-start(bf16[8,32,768]{2,1,0:T(8,128)(2,1)} %param.6) | copy-start | bytes 1179652
  25.8 5.0 %collective-permute-start.3 = (bf16[128,256]{1,0:T(8,128)(2,1)S(1)}, bf16[128,256]{1,0:T(8,128)(2,1)S(1)}, u32[]{:S(2)}, u32[]{:S(2)}) collective-permute-start(bf16[128,256]{1,0:T(8,128)(2,1)S(1)} %get-tuple-element.38), channel_id=1, source_target_pairs={{0,8},{8,0},{16,24},{24,16},{1,9},{9,1},{17,25},{25,17},{2,10},{10... | collective-permute-start | bytes 196616 | tf_op jit(solution)/shard_map/ppermute | solution.py:336
  26.5 4.3 %collective-permute-start.4 = (bf16[128,256]{1,0:T(8,128)(2,1)S(1)}, bf16[128,256]{1,0:T(8,128)(2,1)S(1)}, u32[]{:S(2)}, u32[]{:S(2)}) collective-permute-start(bf16[128,256]{1,0:T(8,128)(2,1)S(1)} %get-tuple-element.39), channel_id=1, source_target_pairs={{0,16},{8,24},{16,0},{24,8},{1,17},{9,25},{17,1},{25,9},{2,18},{10... | collective-permute-start | bytes 196616 | tf_op jit(solution)/shard_map/ppermute | solution.py:336
  26.8 5.0 %collective-permute-start.5 = (bf16[128,256]{1,0:T(8,128)(2,1)S(1)}, bf16[128,256]{1,0:T(8,128)(2,1)S(1)}, u32[]{:S(2)}, u32[]{:S(2)}) collective-permute-start(bf16[128,256]{1,0:T(8,128)(2,1)S(1)} %get-tuple-element.40), channel_id=1, source_target_pairs={{0,24},{8,16},{16,8},{24,0},{1,25},{9,17},{17,9},{25,1},{2,26},{10... | collective-permute-start | bytes 196616 | tf_op jit(solution)/shard_map/ppermute | solution.py:336
  28.2 19.4 %copy-start.4 = (bf16[768,128]{1,0:T(8,128)(2,1)S(1)}, bf16[768,128]{1,0:T(8,128)(2,1)}, u32[]{:S(2)}) copy-start(bf16[768,128]{1,0:T(8,128)(2,1)} %projection_hbm.3) | copy-start | bytes 589828
  32.8 11.8 %all-to-all-start.1 = ((bf16[32,24,128]{2,1,0:T(8,128)(2,1)}), bf16[32,24,128]{2,1,0:T(8,128)(2,1)S(1)}, u32[]{:S(2)}, u32[]{:S(2)}) async-start(bf16[32,24,128]{2,1,0:T(8,128)(2,1)} %bitcast.3), calls=%async_computation.1 | async-start | bytes 393216 | tf_op jit(solution)/shard_map/all_to_all | solution.py:424
  45.3 11.5 %all-to-all-start.2 = ((bf16[32,24,128]{2,1,0:T(8,128)(2,1)}), bf16[32,24,128]{2,1,0:T(8,128)(2,1)S(1)}, u32[]{:S(2)}, u32[]{:S(2)}) async-start(bf16[32,24,128]{2,1,0:T(8,128)(2,1)} %sum_parts.1), calls=%async_computation.2 | async-start | bytes 393216 | tf_op jit(solution)/shard_map/all_to_all | solution.py:433

commit v4 on v3

--- a/solution.py
+++ b/solution.py
@@ -11,6 +11,7 @@
 norm_eps = 1e-06
 center = 0.375
 lanes = 128
+near = 2
 axes = ("dp", "group")
 f32 = jnp.float32
 bf16 = jnp.bfloat16
@@ -57,7 +58,6 @@
 
 
 VMEM = pl.BlockSpec(memory_space=pltpu.VMEM)
-SMEM = pl.BlockSpec(memory_space=pltpu.SMEM)
 HBM = pl.BlockSpec(memory_space=pltpu.HBM)
 
 
@@ -66,7 +66,20 @@
 
 
 def query_kernel(
-    hidden_hbm, projection_hbm, ids_hbm, positive_hbm, pre_out, packed_out, hidden, projection, hard_ids, positive, sems
+    hidden_hbm,
+    projection_hbm,
+    ids_hbm,
+    positive_hbm,
+    lens_hbm,
+    pre_out,
+    packed_out,
+    projection,
+    lens_out,
+    hidden,
+    hard_ids,
+    positive,
+    lens,
+    sems,
 ):
     copies = [
         pltpu.make_async_copy(source, target, sems.at[k])
@@ -76,6 +89,7 @@
                 (hidden_hbm, hidden),
                 (ids_hbm, hard_ids),
                 (positive_hbm, positive),
+                (lens_hbm, lens),
             ]
         )
     ]
@@ -97,6 +111,8 @@
     extra = packed_out.shape[0] - rows
     marks = jnp.concatenate([marks, jnp.full((extra - count, lanes), -1.0, f32)], axis=0)
     packed_out[rows:, :] = marks.astype(bf16)
+    for p in range(lens_out.shape[0]):
+        lens_out[p : p + 1, :] = jnp.full((1, lanes), lens[p], jnp.int32)
     for copy in copies[:2]:
         copy.wait()
     pre = dot(hidden[...], projection[...], 1, 0)
@@ -104,15 +120,10 @@
     packed_out[:rows, :] = normalize(pre).astype(bf16)
 
 
-def passage_kernel(step, hidden, projection_hbm, pre_out, embed_out, projection, sem):
-    copy = pltpu.make_async_copy(projection_hbm, projection, sem)
-    copy.start()
-    copy.wait()
-    for start in range(0, hidden.shape[0], step):
-        part = slice(start, start + step)
-        pre = dot(hidden[part, :], projection[...], 1, 0)
-        pre_out[part, :] = pre
-        embed_out[part, :] = normalize(pre).astype(bf16)
+def parted(index, size):
+    if size & (size - 1) == 0:
+        return lax.shift_right_logical(index, size.bit_length() - 1)
+    return index // size
 
 
 def token_picks(groups, count, length, width, rows_first):
@@ -121,15 +132,45 @@
     shape = (tokens, width) if rows_first else (width, tokens)
     token = iota(shape, 0 if rows_first else 1)
     query = iota(shape, 1 if rows_first else 0)
-    member = jnp.bitwise_xor(token // (count * length), me)
-    owner = member * count + (token % (count * length)) // length
+    owner = jnp.bitwise_xor(parted(token, length), me * count)
     return jnp.where(owner == query, 1.0, 0.0).astype(bf16)
 
 
-def forward_kernel(dims, lens, *refs):
+def forward_step(dims, at, lens, part, packed, shares_out, summed):
+    groups, count, length, passages, tokens, slots, step = dims
+    rows = count * length
+    for k, block in enumerate(packed):
+        columns = slice(k * rows, (k + 1) * rows)
+        similar = dot(part, block[:rows, :], 1, 1)
+        for p in range(step):
+            piece = similar[p * tokens : (p + 1) * tokens, :]
+            live = jnp.concatenate([lens[at * step + p : at * step + p + 1, :]] * (rows // lanes), axis=1)
+            grown = jnp.exp(piece * (1.0 / smooth_temp))
+            grown = jnp.where(iota(piece.shape, 0) < live, grown, 0.0)
+            start = (at * step + p) * tokens
+            shares_out[start : start + tokens, columns] = grown.astype(bf16)
+            summed[at * step + p : at * step + p + 1, columns] = jnp.sum(
+                grown, axis=0, keepdims=True
+            )
+
+
+def near_kernel(dims, lens, hidden, projection, *refs):
+    groups, count, length, passages, tokens, slots, step = dims
+    packed = refs[:near]
+    pre_out, embed_out, shares_out, summed_out = refs[near:]
+    for at in range(passages // step):
+        part = slice(at * step * tokens, (at + 1) * step * tokens)
+        pre = dot(hidden[part, :], projection[...], 1, 0)
+        pre_out[part, :] = pre
+        embed = normalize(pre).astype(bf16)
+        embed_out[part, :] = embed
+        forward_step(dims, at, lens, embed, packed, shares_out, summed_out)
+
+
+def far_kernel(dims, lens, *refs):
     groups, count, length, passages, tokens, slots, step = dims
     packed = refs[:groups]
-    embed, shares_out, inverse_out, stats_out, packet_out, summed, marks = refs[groups:]
+    embed, summed_near, shares_out, inverse_out, stats_out, packet_out, summed, marks = refs[groups:]
     rows = count * length
     me = lax.axis_index("group")
     marks[...] = jnp.full(marks.shape, -1.0, f32)
@@ -137,25 +178,10 @@
         member = jnp.bitwise_xor(me, k)
         start = pl.multiple_of(member * count, count)
         marks[pl.ds(start, count), :] = packed[k][rows:, :].astype(f32)[:count]
-
-    @pl.loop(0, passages // step, unroll=True)
-    def _(at):
-        start = pl.multiple_of(at * (step * tokens), step * tokens)
-        part = embed[pl.ds(start, step * tokens), :]
-        for k in range(groups):
-            similar = dot(part, packed[k][:rows, :], 1, 1)
-            for p in range(step):
-                piece = similar[p * tokens : (p + 1) * tokens, :]
-                alive = iota(piece.shape, 0) < lens[at * step + p]
-                grown = jnp.where(alive, jnp.exp(piece * (1.0 / smooth_temp)), 0.0)
-                shares_out[pl.ds(start + p * tokens, tokens), k * rows : (k + 1) * rows] = (
-                    grown.astype(bf16)
-                )
-                summed[pl.ds(at * step + p, 1), k * rows : (k + 1) * rows] = jnp.sum(
-                    grown, axis=0, keepdims=True
-                )
-
-    total = summed[...]
+    for at in range(passages // step):
+        part = embed[at * step * tokens : (at + 1) * step * tokens, :]
+        forward_step(dims, at, lens, part, packed[near:], shares_out, summed)
+    total = jnp.concatenate([summed_near[...], summed[...]], axis=1)
     inverse_out[...] = 1.0 / total
     width = marks.shape[0]
     scores = exact_dot(
@@ -196,10 +222,18 @@
         packet_out[k] = packet
 
 
-def query_grad_kernel(dims, packets, stats, inverse, shares, embed, *refs):
+def far_grad_kernel(
+    dims,
+    packets,
+    stats,
+    inverse,
+    shares,
+    embed,
+    *refs,
+):
     groups, count, length, passages, tokens, slots, step = dims
-    parts_out = refs[:groups]
-    weights, losses_out, running = refs[groups:]
+    parts_out = refs[: groups - near]
+    weights, losses_out, running = refs[groups - near :]
     rows = count * length
     width = stats.shape[1]
     devices = packets.shape[0]
@@ -225,64 +259,87 @@
     found = (spread * inverse[...]).astype(bf16)
     for p in range(passages):
         weights[p] = found[p : p + 1, :]
-    running[...] = jnp.zeros(running.shape, f32)
-
-    @pl.loop(0, passages // step, unroll=True)
-    def _(at):
-        start = pl.multiple_of(at * (step * tokens), step * tokens)
-        running[...] += dot(
-            embed[pl.ds(start, step * tokens), :].T,
-            coefficients(dims, shares, weights, at),
-            1,
-            0,
-        )
-
-    for k in range(groups):
-        parts_out[k][...] = running[:, k * rows : (k + 1) * rows].astype(bf16)
-
-
-def coefficients(dims, shares, weights, at):
+    query_grads(dims, shares, slice(near * rows, groups * rows), embed, weights, running)
+    for k, out in enumerate(parts_out):
+        out[...] = running[:, k * rows : (k + 1) * rows].astype(bf16)
+
+
+def near_grad_kernel(dims, weights, shares, embed, *refs):
+    rows = dims[1] * dims[2]
+    parts_out, running = refs[:near], refs[near]
+    query_grads(dims, shares, slice(0, near * rows), embed, weights, running)
+    for k, out in enumerate(parts_out):
+        out[...] = running[:, k * rows : (k + 1) * rows].astype(bf16)
+
+
+def query_grads(dims, shares, columns, embed, weights, running):
+    groups, count, length, passages, tokens, slots, step = dims
+    for at in range(passages // step):
+        part = embed[at * step * tokens : (at + 1) * step * tokens, :].T
+        terms = dot(part, coefficients(dims, shares, columns, weights, at), 1, 0)
+        if at == 0:
+            running[...] = terms
+        else:
+            running[...] += terms
+
+
+def halves(dims, shares_near, shares_far):
+    groups, count, length = dims[:3]
+    cut = near * count * length
+    return [(shares_near, slice(0, cut)), (shares_far, slice(cut, groups * count * length))]
+
+
+def coefficients(dims, shares, columns, weights, at):
     passages, tokens, _, step = dims[3:]
-    start = pl.multiple_of(at * (step * tokens), step * tokens)
+    start = at * step * tokens
     return jnp.concatenate(
         [
-            shares[pl.ds(start + p * tokens, tokens), :] * weights[at * step + p]
+            shares[start + p * tokens : start + (p + 1) * tokens, :]
+            * weights[at * step + p, :, columns]
             for p in range(step)
         ],
         axis=0,
     )
 
 
-def passage_grad_kernel(dims, weights, shares, pre, hidden, query_pre, query_hidden, *refs):
+def passage_grad_kernel(
+    dims, weights, shares_near, shares_far, pre, hidden, query_pre, query_hidden, *refs
+):
     groups, count, length, passages, tokens, slots, step = dims
     packed = refs[:groups]
     back_out, weight_out, pre_out, hidden_out, queries, running = refs[groups:]
     rows = count * length
     for k in range(groups):
         queries[k * rows : (k + 1) * rows, :] = packed[k][:rows, :]
-    running[...] = jnp.zeros(running.shape, f32)
-
-    @pl.loop(0, passages // step, unroll=True)
-    def _(at):
-        part = pl.ds(pl.multiple_of(at * (step * tokens), step * tokens), step * tokens)
-        grad = dot(coefficients(dims, shares, weights, at), queries[...], 1, 0)
+    for at in range(passages // step):
+        part = slice(at * step * tokens, (at + 1) * step * tokens)
+        grad = sum(
+            dot(coefficients(dims, shares, columns, weights, at), queries[columns, :], 1, 0)
+            for shares, columns in halves(dims, shares_near, shares_far)
+        )
         back = normalize_back(pre[part, :], grad).astype(bf16)
         back_out[part, :] = back
-        running[...] += dot(back.T, hidden[part, :], 1, 0)
-
+        terms = dot(back.T, hidden[part, :], 1, 0)
+        if at == 0:
+            running[...] = terms
+        else:
+            running[...] += terms
     weight_out[...] = running[...].T
     pre_out[...] = query_pre[...].T
     hidden_out[...] = query_hidden[...].T
+
+
+def normalize_back_columns(projected, grad):
+    inverse = lax.rsqrt(jnp.sum(projected * projected, axis=0, keepdims=True) + norm_eps)
+    along = jnp.sum(projected * grad, axis=0, keepdims=True)
+    return grad * inverse - projected * (inverse * inverse * inverse * along)
 
 
 def query_back_kernel(pre, hidden, weight, *refs):
     parts = refs[:-2]
     back_out, weight_out = refs[-2:]
     grad = sum(part[...].astype(f32) for part in parts)
-    projected = pre[...]
-    inverse = lax.rsqrt(jnp.sum(projected * projected, axis=0, keepdims=True) + norm_eps)
-    along = jnp.sum(projected * grad, axis=0, keepdims=True)
-    back = (grad * inverse - projected * (inverse * inverse * inverse * along)).astype(bf16)
+    back = normalize_back_columns(pre[...], grad).astype(bf16)
     back_out[...] = back
     weight_out[...] = (weight[...] + dot(hidden[...], back, 1, 1)).astype(bf16)
 
@@ -315,80 +372,101 @@
     passage_flat = passage_hidden.reshape(passage_rows, width)
     shape = jax.ShapeDtypeStruct
 
-    query_pre, packed = pl.pallas_call(
+    query_pre, packed, projection_near, lens = pl.pallas_call(
         query_kernel,
-        out_shape=(shape((rows, depth), f32), shape((rows + 16, depth), bf16)),
-        in_specs=[HBM] * 4,
-        out_specs=(VMEM, VMEM),
+        out_shape=(
+            shape((rows, depth), f32),
+            shape((rows + 16, depth), bf16),
+            shape((width, depth), bf16),
+            shape((passages, lanes), jnp.int32),
+        ),
+        in_specs=[HBM] * 5,
+        out_specs=(VMEM,) * 4,
         scratch_shapes=[
             pltpu.VMEM((rows, width), bf16),
-            pltpu.VMEM((width, depth), bf16),
             pltpu.VMEM((count, slots), jnp.int32),
             pltpu.SMEM((count,), jnp.int32),
-            pltpu.SemaphoreType.DMA((4,)),
+            pltpu.SMEM((passages,), jnp.int32),
+            pltpu.SemaphoreType.DMA((5,)),
         ],
         compiler_params=params(16),
-        cost_estimate=cost(2 * rows * width * depth, rows * width * 2),
+        cost_estimate=cost(2e10, rows * width * 2),
         name="query_embed",
-    )(*in_hbm(query_flat, projection, hard_ids, positive))
+    )(*in_hbm(query_flat, projection, hard_ids, positive, passage_len))
 
     def swap(value, k):
         return lax.ppermute(value, "group", [(i, i ^ k) for i in range(groups)])
 
     blocks = [packed] + [swap(packed, k) for k in range(1, groups)]
 
-    passage_pre, passage_embed = pl.pallas_call(
-        functools.partial(passage_kernel, 4 * tokens),
-        out_shape=(shape((passage_rows, depth), f32), shape((passage_rows, depth), bf16)),
-        in_specs=[VMEM, HBM],
-        out_specs=(VMEM, VMEM),
-        scratch_shapes=[pltpu.VMEM((width, depth), bf16), pltpu.SemaphoreType.DMA],
-        compiler_params=params(16),
-        cost_estimate=cost(2 * passage_rows * width * depth, passage_rows * (width * 2 + depth * 6)),
-        name="passage_embed",
-    )(passage_flat, *in_hbm(projection))
-
-    shares, inverse, stats, packets = pl.pallas_call(
-        functools.partial(forward_kernel, dims),
+    passage_pre, passage_embed, shares_near, summed_near = pl.pallas_call(
+        functools.partial(near_kernel, dims),
         out_shape=(
-            shape((passage_rows, all_rows), bf16),
+            shape((passage_rows, depth), f32),
+            shape((passage_rows, depth), bf16),
+            shape((passage_rows, near * rows), bf16),
+            shape((passages, near * rows), f32),
+        ),
+        in_specs=[VMEM] * (near + 3),
+        out_specs=(VMEM,) * 4,
+        compiler_params=params(32),
+        cost_estimate=cost(
+            2 * passage_rows * (width + near * rows) * depth,
+            passage_rows * (width + near * rows + 3 * depth) * 2,
+            passage_rows * near * rows,
+        ),
+        name="forward_near",
+    )(lens, passage_flat, projection_near, *blocks[:near])
+
+    far_rows = all_rows - near * rows
+    shares_far, inverse, stats, packets = pl.pallas_call(
+        functools.partial(far_kernel, dims),
+        out_shape=(
+            shape((passage_rows, far_rows), bf16),
             shape((passages, all_rows), f32),
             shape((3 * passages, pool_width), f32),
             shape((devices, packet_rows, pool_width), f32),
         ),
-        in_specs=[SMEM] + [VMEM] * (groups + 1),
+        in_specs=[VMEM] * (groups + 3),
         out_specs=(VMEM, VMEM, VMEM, VMEM),
         scratch_shapes=[
-            pltpu.VMEM((passages, all_rows), f32),
+            pltpu.VMEM((passages, far_rows), f32),
             pltpu.VMEM((pool_width, lanes), f32),
         ],
         compiler_params=params(32),
         cost_estimate=cost(
-            2 * passage_rows * all_rows * depth,
-            passage_rows * all_rows * 2,
-            passage_rows * all_rows,
-        ),
-        name="forward",
-    )(passage_len, *blocks, passage_embed)
+            2 * passage_rows * far_rows * depth, passage_rows * far_rows * 2, passage_rows * far_rows
+        ),
+        name="forward_far",
+    )(lens, *blocks, passage_embed, summed_near)
 
     packets = lax.all_to_all(packets, axes, 0, 0, tiled=True)
 
-    outs = pl.pallas_call(
-        functools.partial(query_grad_kernel, dims),
+    *far_parts, weights, losses = pl.pallas_call(
+        functools.partial(far_grad_kernel, dims),
         out_shape=(
-            *[shape((depth, rows), bf16)] * groups,
+            *[shape((depth, rows), bf16)] * (groups - near),
             shape((passages, 1, all_rows), bf16),
             shape((8, pool_width), f32),
         ),
         in_specs=[VMEM] * 5,
-        out_specs=(VMEM,) * (groups + 2),
-        scratch_shapes=[pltpu.VMEM((depth, all_rows), f32)],
+        out_specs=(VMEM,) * (groups - near + 2),
+        scratch_shapes=[pltpu.VMEM((depth, far_rows), f32)],
         compiler_params=params(32),
-        cost_estimate=cost(2 * passage_rows * all_rows * depth, passage_rows * all_rows * 2),
-        name="query_grad",
-    )(packets, stats, inverse, shares, passage_embed)
-    parts = outs[:groups]
-    weights, losses = outs[groups:]
+        cost_estimate=cost(2 * passage_rows * far_rows * depth, passage_rows * far_rows * 2),
+        name="query_grad_far",
+    )(packets, stats, inverse, shares_far, passage_embed)
+    near_parts = pl.pallas_call(
+        functools.partial(near_grad_kernel, dims),
+        out_shape=(shape((depth, rows), bf16),) * near,
+        in_specs=[VMEM] * 3,
+        out_specs=(VMEM,) * near,
+        scratch_shapes=[pltpu.VMEM((depth, near * rows), f32)],
+        compiler_params=params(32),
+        cost_estimate=cost(4e9, passage_rows * near * rows * 2),
+        name="query_grad_near",
+    )(weights, shares_near, passage_embed)
+    parts = [*near_parts, *far_parts]
     parts = [parts[0]] + [swap(parts[k], k) for k in range(1, groups)]
 
     passage_back, weight, pre_t, hidden_t = pl.pallas_call(
@@ -399,7 +477,7 @@
             shape((depth, rows), f32),
             shape((width, rows), bf16),
         ),
-        in_specs=[VMEM] * (6 + groups),
+        in_specs=[VMEM] * (7 + groups),
         out_specs=(VMEM,) * 4,
         scratch_shapes=[pltpu.VMEM((all_rows, depth), bf16), pltpu.VMEM((depth, width), f32)],
         compiler_params=params(32),
@@ -408,7 +486,7 @@
             passage_rows * (all_rows * 2 + width * 2 + depth * 6),
         ),
         name="passage_grad",
-    )(weights, shares, passage_pre, passage_flat, query_pre, query_flat, *blocks)
+    )(weights, shares_near, shares_far, passage_pre, passage_flat, query_pre, query_flat, *blocks)
 
     query_back, weight = pl.pallas_call(
         query_back_kernel,
@@ -422,6 +500,8 @@
 
     weight = weight.reshape(devices, width // devices, depth)
     weight = lax.all_to_all(weight, axes, 0, 0, tiled=True)
+    grad_passage = dot(passage_back, projection, 1, 1).astype(bf16).reshape(passage_hidden.shape)
+    weight, grad_passage = lax.optimization_barrier((weight, grad_passage))
     copies = pl.pallas_call(
         sum_kernel,
         out_shape=shape(weight.shape, bf16),
@@ -434,7 +514,6 @@
     grad_proj = copies.reshape(width, depth).astype(f32)
 
     grad_query = dot(query_back, projection, 0, 1).astype(bf16).reshape(query_hidden.shape)
-    grad_passage = dot(passage_back, projection, 1, 1).astype(bf16).reshape(passage_hidden.shape)
     own = lax.axis_index("group") * count
     return (lax.dynamic_slice(losses[0], (own,), (count,)), grad_proj, grad_query, grad_passage)
 

time: 57.9 us -> 56.5 us (0.976)
  local copies, waits for them, and re-layouts: 2.49 us -> 0.6 us
  waiting for transfers between devices: 15.3 us -> 16.1 us
    all_to_all x1, waiting for transfers between devices: 9.36 us -> 6.71 us  [local(): weight = lax.all_to_all(weight, axes, 0, 0, tiled=True)]
    all_to_all x1, waiting for transfers between devices: 4.89 us -> 7.54 us  [local(): copies = lax.all_to_all(copies, axes, 0, 0, tiled=True)]
    unnamed x10 -> x6, local copies, waits for them, and re-layouts: 1.91 us -> 0.01 us
    ppermute x6, waiting for transfers between devices: 1.08 us -> 1.85 us  [swap(): return lax.ppermute(value, 'group', [(i, i ^ k) for i in range(groups)])]
    pallas_call x3 -> x4, Pallas kernels: 6.11 us -> 5.91 us  [the longest x1 3.17 us: local(): pl.pallas_call(functools.partial(near_kernel, dims), out_shape=(shape((pa...]
  transfers between devices with their start and end apart: 8 -> 8, of which waited for: 4 -> 4; matrix products, arithmetic and copies ran while one was open for 7% -> 8% of each run, Pallas kernels for 8% -> 10%
where the time goes in v4:
time: 56.5 us; the launch traced here: 56.2 us
  waiting for transfers between devices  16.1 us (28%)
  blocking collectives  12.5 us (22%)
  Pallas kernels  11.8 us (21%)
  starting transfers between devices  9.99 us (18%)
  matrix products  3.68 us (7%)
  other arithmetic  0.78 us (1%)
  between operations  0.76 us (1%)
  local copies, waits for them, and re-layouts  0.6 us (1%)
    all_to_all x1, blocking collectives, local(): packets = lax.all_to_all(packets, axes, 0, 0, tiled=True)  12.5 us
    all_to_all x1, waiting for transfers between devices, local(): copies = lax.all_to_all(copies, axes, 0, 0, tiled=True)  7.54 us
    all_to_all x1, waiting for transfers between devices, local(): weight = lax.all_to_all(weight, axes, 0, 0, tiled=True)  6.71 us
    ppermute x6, starting transfers between devices, swap(): return lax.ppermute(value, 'group', [(i, i ^ k) for i in range(groups)])  5.25 us
    dot_general x2, matrix products, dot(): lax.dot_general(left, right, (((left_dim,), (right_dim,)), ((), ())), pre...  3.68 us
    pallas_call x1, Pallas kernels, local(): pl.pallas_call(functools.partial(near_kernel, dims), out_shape=(shape((pa...  3.17 us
    pallas_call x1, Pallas kernels, local(): pl.pallas_call(functools.partial(passage_grad_kernel, dims), out_shape=(s...  2.56 us
    all_to_all x1, starting transfers between devices, local(): weight = lax.all_to_all(weight, axes, 0, 0, tiled=True)  2.41 us
  transfers between devices with their start and end apart: 8, of which 4 were waited for; matrix products, arithmetic and copies ran while one was open for 8% of the time, Pallas kernels for 10%

profile of v4, /device:TPU:1, one launch (start us, length us, event | category | flops | bytes accessed | tf_op | source)
XLA Modules:
  0.0 56.2 jit_solution(10389823091517015467)
XLA Ops:
  0.6 1.6 %query_embed.1 = (f32[256,128]{1,0:T(8,128)S(1)}, bf16[272,128]{1,0:T(8,128)(2,1)S(1)}, bf16[768,128]{1,0:T(8,128)(2,1)S(1)}, s32[16,128]{1,0:T(8,128)S(1)}) custom-call(bf16[256,768]{1,0:T(8,128)(2,1)} %bitcast.16, bf16[768,128]{1,0:T(8,128)(2,1)} %projection_hbm.1, s32[8,32]{1,0:T(8,128)} %ids_hbm.1, s32[8]{0:T(128)} %positive_hbm.1, s32[16]{0:T(128)} %lens_hbm.1), custom_call_target="tpu_custom_call" | custom-call | flops 20000000000 | bytes 393216 | tf_op jit(solution)/shard_map/query_embed/pallas_call | solution.py:375
  2.3 0.1 collective-permute-start
  2.4 2.7 %collective-permute-start.1 = (bf16[272,128]{1,0:T(8,128)(2,1)S(1)}, bf16[272,128]{1,0:T(8,128)(2,1)S(1)}, u32[]{:S(2)}, u32[]{:S(2)}) collective-permute-start(bf16[272,128]{1,0:T(8,128)(2,1)S(1)} %get-tuple-element.31.refs_0_), channel_id=1, source_target_pairs={{0,16},{8,24},{16,0},{24,8},{1,17},{9,25},{17,1},{25,9},{2,18},{10... | collective-permute-start | bytes 208904 | tf_op jit(solution)/shard_map/ppermute | solution.py:398
  5.1 3.2 %forward_near.1 = (f32[2048,128]{1,0:T(8,128)S(1)}, bf16[2048,128]{1,0:T(8,128)(2,1)S(1)}, bf16[2048,512]{1,0:T(8,128)(2,1)S(1)}, f32[16,512]{1,0:T(8,128)S(1)}) custom-call(s32[16,128]{1,0:T(8,128)S(1)} %get-tuple-element.30.lens, bf16[2048,768]{1,0:T(8,128)(2,1)S(1)} %bitcast.14, bf16[768,128]{1,0:T(8,128)(2,1)S(1)} %get-tuple-element.32.projection, ...), custom_call_target="tpu_custom_call" | custom-call | flops 671088640 | bytes 6815744 | tf_op jit(solution)/shard_map/forward_near/pallas_call | solution.py:402
  8.3 0.9 %collective-permute-done.2.refs_3_ = bf16[272,128]{1,0:T(8,128)(2,1)S(1)} collective-permute-done((bf16[272,128]{1,0:T(8,128)(2,1)S(1)}, bf16[272,128]{1,0:T(8,128)(2,1)S(1)}, u32[]{:S(2)}, u32[]{:S(2)}) %collective-permute-start.2) | collective-permute-done | bytes 69664 | tf_op jit(solution)/shard_map/ppermute | solution.py:398
  9.2 1.5 %forward_far.1 = (bf16[2048,512]{1,0:T(8,128)(2,1)S(1)}, f32[16,1024]{1,0:T(8,128)S(1)}, f32[48,128]{1,0:T(8,128)S(1)}, f32[32,1,128]{2,1,0:T(1,128)S(1)}) custom-call(s32[16,128]{1,0:T(8,128)S(1)} %get-tuple-element.30.lens, bf16[272,128]{1,0:T(8,128)(2,1)S(1)} %get-tuple-element.31.refs_0_, bf16[272,128]{1,0:T(8,128)(2,1)S(1)} %collective-permute-done.refs_1_, ...), custom_call_target="tpu_custom_call" | custom-call | flops 268435456 | bytes 2097152 | tf_op jit(solution)/shard_map/forward_far/pallas_call | solution.py:422
  10.7 12.5 %all_to_all.15.packets = f32[32,1,128]{2,1,0:T(1,128)S(1)} all-to-all(f32[32,1,128]{2,1,0:T(1,128)S(1)} %get-tuple-element.35), channel_id=1, replica_groups=mesh['group'=4,'dp'=8] {'dp','group'}, dimensions={0} | all-to-all | bytes 32768 | tf_op jit(solution)/shard_map/all_to_all | solution.py:443
  23.1 0.8 %query_grad_far.1 = (bf16[128,256]{1,0:T(8,128)(2,1)S(1)}, bf16[128,256]{1,0:T(8,128)(2,1)S(1)}, bf16[16,1,1024]{2,1,0:T(2,128)(2,1)S(1)}, f32[8,128]{1,0:T(8,128)S(1)}) custom-call(f32[32,1,128]{2,1,0:T(1,128)S(1)} %all_to_all.15.packets, f32[48,128]{1,0:T(8,128)S(1)} %get-tuple-element.36.stats, f32[16,1024]{1,0:T(8,128)S(1)} %get-tuple-element.37.inverse, ...), custom_call_target="tpu_custom_call" | custom-call | flops 268435456 | bytes 2097152 | tf_op jit(solution)/shard_map/query_grad_far/pallas_call | solution.py:445
  24.0 0.5 query_grad_near.1
  24.4 0.7 %collective-permute-start.3 = (bf16[128,256]{1,0:T(8,128)(2,1)S(1)}, bf16[128,256]{1,0:T(8,128)(2,1)S(1)}, u32[]{:S(2)}, u32[]{:S(2)}) collective-permute-start(bf16[128,256]{1,0:T(8,128)(2,1)S(1)} %get-tuple-element.48), channel_id=1, source_target_pairs={{0,8},{8,0},{16,24},{24,16},{1,9},{9,1},{17,25},{25,17},{2,10},{10... | collective-permute-start | bytes 196616 | tf_op jit(solution)/shard_map/ppermute | solution.py:398
  25.1 0.3 collective-permute-start.4
  25.4 1.5 %collective-permute-start.5 = (bf16[128,256]{1,0:T(8,128)(2,1)S(1)}, bf16[128,256]{1,0:T(8,128)(2,1)S(1)}, u32[]{:S(2)}, u32[]{:S(2)}) collective-permute-start(bf16[128,256]{1,0:T(8,128)(2,1)S(1)} %get-tuple-element.50), channel_id=1, source_target_pairs={{0,24},{8,16},{16,8},{24,0},{1,25},{9,17},{17,9},{25,1},{2,26},{10... | collective-permute-start | bytes 196616 | tf_op jit(solution)/shard_map/ppermute | solution.py:398
  26.9 2.6 %passage_grad.1 = (bf16[2048,128]{1,0:T(8,128)(2,1)S(1)}, f32[768,128]{1,0:T(8,128)S(1)}, f32[128,256]{1,0:T(8,128)S(1)}, bf16[768,256]{1,0:T(8,128)(2,1)S(1)}) custom-call(bf16[16,1,1024]{2,1,0:T(2,128)(2,1)S(1)} %get-tuple-element.40.weights, bf16[2048,512]{1,0:T(8,128)(2,1)S(1)} %get-tuple-element.41.shares_near.shares, ...), custom_call_target="tpu_custom_call" | custom-call | flops 939524096 | bytes 8912896 | tf_op jit(solution)/shard_map/passage_grad/pallas_call | solution.py:472
  29.4 0.9 %collective-permute-done.5.refs_3_ = bf16[128,256]{1,0:T(8,128)(2,1)S(1)} collective-permute-done((bf16[128,256]{1,0:T(8,128)(2,1)S(1)}, bf16[128,256]{1,0:T(8,128)(2,1)S(1)}, u32[]{:S(2)}, u32[]{:S(2)}) %collective-permute-start.5) | collective-permute-done | bytes 65568 | tf_op jit(solution)/shard_map/ppermute | solution.py:398
  30.4 1.0 %query_back.1 = (bf16[128,256]{1,0:T(8,128)(2,1)S(1)}, bf16[768,128]{1,0:T(8,128)(2,1)}) custom-call(f32[128,256]{1,0:T(8,128)S(1)} %get-tuple-element.44.pre, bf16[768,256]{1,0:T(8,128)(2,1)S(1)} %get-tuple-element.45.hidden, f32[768,128]{1,0:T(8,128)S(1)} %get-tuple-element.46.weight, bf16[128,256]{1,0:T(8,128)(2,1)S(1)} %get-tuple-element.47.refs_0_, ...), custom_call_target="tpu_custom_call" | custom-call | flops 50331648 | bytes 983040 | tf_op jit(solution)/shard_map/query_back/pallas_call | solution.py:491
  31.4 2.4 %all-to-all-start.1 = ((bf16[32,24,128]{2,1,0:T(8,128)(2,1)}), bf16[32,24,128]{2,1,0:T(8,128)(2,1)S(1)}, u32[]{:S(2)}, u32[]{:S(2)}) async-start(bf16[32,24,128]{2,1,0:T(8,128)(2,1)} %bitcast.3), calls=%async_computation.1 | async-start | bytes 393216 | tf_op jit(solution)/shard_map/all_to_all | solution.py:502
  33.8 2.6 %convolution_convert_fusion = bf16[2048,768]{1,0:T(8,128)(2,1)} fusion(bf16[2048,128]{1,0:T(8,128)(2,1)S(1)} %get-tuple-element.52, bf16[768,128]{1,0:T(8,128)(2,1)S(1)} %copy-done.2), kind=kOutput, calls=%fused_computation | convolution fusion | flops 404226048 | bytes 3866624 | tf_op jit(solution)/shard_map/dot_general | solution.py:21
  36.5 6.7 %all-to-all-done.1.parts = bf16[32,24,128]{2,1,0:T(8,128)(2,1)S(1)} async-done(((bf16[32,24,128]{2,1,0:T(8,128)(2,1)}), bf16[32,24,128]{2,1,0:T(8,128)(2,1)S(1)}, u32[]{:S(2)}, u32[]{:S(2)}) %all-to-all-start.1) | async-done | bytes 196640 | tf_op jit(solution)/shard_map/all_to_all | solution.py:502
  43.2 0.7 %sum_parts.1 = bf16[32,24,128]{2,1,0:T(8,128)(2,1)} custom-call(bf16[32,24,128]{2,1,0:T(8,128)(2,1)S(1)} %all-to-all-done.1.parts), custom_call_target="tpu_custom_call" | custom-call | tf_op jit(solution)/shard_map/sum_parts/pallas_call | solution.py:505
  43.9 2.3 %all-to-all-start.2 = ((bf16[32,24,128]{2,1,0:T(8,128)(2,1)}), bf16[32,24,128]{2,1,0:T(8,128)(2,1)S(1)}, u32[]{:S(2)}, u32[]{:S(2)}) async-start(bf16[32,24,128]{2,1,0:T(8,128)(2,1)} %sum_parts.1), calls=%async_computation.2 | async-start | bytes 393216 | tf_op jit(solution)/shard_map/all_to_all | solution.py:513
  46.3 0.6 %dynamic-slice_bitcast_fusion = f32[8]{0:T(128)} fusion(f32[1,128]{1,0:T(1,128)S(1)} %slice.3, s32[]{:T(128)S(6)} %select_n.3), kind=kLoop, calls=%fused_computation.3 | loop fusion | bytes 68 | tf_op jit(solution)/shard_map/dynamic_slice | solution.py:518
  46.9 1.0 %convolution_convert_fusion.1 = bf16[256,768]{1,0:T(8,128)(2,1)} fusion(bf16[128,256]{1,0:T(8,128)(2,1)S(1)} %get-tuple-element.54, bf16[768,128]{1,0:T(8,128)(2,1)S(1)} %copy-done.2), kind=kOutput, calls=%fused_computation.1 | convolution fusion | flops 50528256 | bytes 655360 | tf_op jit(solution)/shard_map/dot_general | solution.py:21
  47.9 7.5 %all-to-all-done.2 = bf16[32,24,128]{2,1,0:T(8,128)(2,1)S(1)} async-done(((bf16[32,24,128]{2,1,0:T(8,128)(2,1)}), bf16[32,24,128]{2,1,0:T(8,128)(2,1)S(1)}, u32[]{:S(2)}, u32[]{:S(2)}) %all-to-all-start.2) | async-done | bytes 196640 | tf_op jit(solution)/shard_map/all_to_all | solution.py:513
  55.4 0.8 %bitcast_convert_fusion = f32[768,128]{1,0:T(8,128)} fusion(bf16[32,24,128]{2,1,0:T(8,128)(2,1)S(1)} %all-to-all-done.2), kind=kLoop, calls=%fused_computation.2 | loop fusion | flops 98304 | bytes 589824 | tf_op jit(solution)/shard_map/convert_element_type | solution.py:514
  (12 shorter events, 0.1 us)
Async XLA Ops:
  0.6 4.5 %copy-start = (bf16[16,128,768]{2,1,0:T(8,128)(2,1)S(1)}, bf16[16,128,768]{2,1,0:T(8,128)(2,1)}, u32[]{:S(2)}) copy-start(bf16[16,128,768]{2,1,0:T(8,128)(2,1)} %param.7) | copy-start | bytes 9437188
  2.3 2.8 %collective-permute-start = (bf16[272,128]{1,0:T(8,128)(2,1)S(1)}, bf16[272,128]{1,0:T(8,128)(2,1)S(1)}, u32[]{:S(2)}, u32[]{:S(2)}) collective-permute-start(bf16[272,128]{1,0:T(8,128)(2,1)S(1)} %get-tuple-element.31.refs_0_), channel_id=1, source_target_pairs={{0,8},{8,0},{16,24},{24,16},{1,9},{9,1},{17,25},{25,17},{2,10},{10... | collective-permute-start | bytes 208904 | tf_op jit(solution)/shard_map/ppermute | solution.py:398
  2.4 5.9 %collective-permute-start.1 = (bf16[272,128]{1,0:T(8,128)(2,1)S(1)}, bf16[272,128]{1,0:T(8,128)(2,1)S(1)}, u32[]{:S(2)}, u32[]{:S(2)}) collective-permute-start(bf16[272,128]{1,0:T(8,128)(2,1)S(1)} %get-tuple-element.31.refs_0_), channel_id=1, source_target_pairs={{0,16},{8,24},{16,0},{24,8},{1,17},{9,25},{17,1},{25,9},{2,18},{10... | collective-permute-start | bytes 208904 | tf_op jit(solution)/shard_map/ppermute | solution.py:398
  5.1 4.1 %collective-permute-start.2 = (bf16[272,128]{1,0:T(8,128)(2,1)S(1)}, bf16[272,128]{1,0:T(8,128)(2,1)S(1)}, u32[]{:S(2)}, u32[]{:S(2)}) collective-permute-start(bf16[272,128]{1,0:T(8,128)(2,1)S(1)} %get-tuple-element.31.refs_0_), channel_id=1, source_target_pairs={{0,24},{8,16},{16,8},{24,0},{1,25},{9,17},{17,9},{25,1},{2,26},{10... | collective-permute-start | bytes 208904 | tf_op jit(solution)/shard_map/ppermute | solution.py:398
  23.9 2.9 %copy-start.1 = (bf16[8,32,768]{2,1,0:T(8,128)(2,1)S(1)}, bf16[8,32,768]{2,1,0:T(8,128)(2,1)}, u32[]{:S(2)}) copy-start(bf16[8,32,768]{2,1,0:T(8,128)(2,1)} %param.6) | copy-start | bytes 1179652
  24.4 5.0 %collective-permute-start.3 = (bf16[128,256]{1,0:T(8,128)(2,1)S(1)}, bf16[128,256]{1,0:T(8,128)(2,1)S(1)}, u32[]{:S(2)}, u32[]{:S(2)}) collective-permute-start(bf16[128,256]{1,0:T(8,128)(2,1)S(1)} %get-tuple-element.48), channel_id=1, source_target_pairs={{0,8},{8,0},{16,24},{24,16},{1,9},{9,1},{17,25},{25,17},{2,10},{10... | collective-permute-start | bytes 196616 | tf_op jit(solution)/shard_map/ppermute | solution.py:398
  25.1 4.3 %collective-permute-start.4 = (bf16[128,256]{1,0:T(8,128)(2,1)S(1)}, bf16[128,256]{1,0:T(8,128)(2,1)S(1)}, u32[]{:S(2)}, u32[]{:S(2)}) collective-permute-start(bf16[128,256]{1,0:T(8,128)(2,1)S(1)} %get-tuple-element.49), channel_id=1, source_target_pairs={{0,16},{8,24},{16,0},{24,8},{1,17},{9,25},{17,1},{25,9},{2,18},{10... | collective-permute-start | bytes 196616 | tf_op jit(solution)/shard_map/ppermute | solution.py:398
  25.4 5.0 %collective-permute-start.5 = (bf16[128,256]{1,0:T(8,128)(2,1)S(1)}, bf16[128,256]{1,0:T(8,128)(2,1)S(1)}, u32[]{:S(2)}, u32[]{:S(2)}) collective-permute-start(bf16[128,256]{1,0:T(8,128)(2,1)S(1)} %get-tuple-element.50), channel_id=1, source_target_pairs={{0,24},{8,16},{16,8},{24,0},{1,25},{9,17},{17,9},{25,1},{2,26},{10... | collective-permute-start | bytes 196616 | tf_op jit(solution)/shard_map/ppermute | solution.py:398
  26.9 7.0 %copy-start.2 = (bf16[768,128]{1,0:T(8,128)(2,1)S(1)}, bf16[768,128]{1,0:T(8,128)(2,1)}, u32[]{:S(2)}) copy-start(bf16[768,128]{1,0:T(8,128)(2,1)} %projection_hbm.1) | copy-start | bytes 589828
  31.4 11.8 %all-to-all-start.1 = ((bf16[32,24,128]{2,1,0:T(8,128)(2,1)}), bf16[32,24,128]{2,1,0:T(8,128)(2,1)S(1)}, u32[]{:S(2)}, u32[]{:S(2)}) async-start(bf16[32,24,128]{2,1,0:T(8,128)(2,1)} %bitcast.3), calls=%async_computation.1 | async-start | bytes 393216 | tf_op jit(solution)/shard_map/all_to_all | solution.py:502
  43.9 11.5 %all-to-all-start.2 = ((bf16[32,24,128]{2,1,0:T(8,128)(2,1)}), bf16[32,24,128]{2,1,0:T(8,128)(2,1)S(1)}, u32[]{:S(2)}, u32[]{:S(2)}) async-start(bf16[32,24,128]{2,1,0:T(8,128)(2,1)} %sum_parts.1), calls=%async_computation.2 | async-start | bytes 393216 | tf_op jit(solution)/shard_map/all_to_all | solution.py:513

commit v5 on v4

--- a/solution.py
+++ b/solution.py
@@ -23,16 +23,14 @@
     )
 
 
-def split_parts(value):
+def exact_dot(value, picks):
     high = value.astype(bf16)
     rest = value - high.astype(f32)
     middle = rest.astype(bf16)
     low = (rest - middle.astype(f32)).astype(bf16)
-    return (high, middle, low)
-
-
-def exact_dot(value, picks):
-    return sum(dot(part, picks, 1, 0) for part in split_parts(value))
+    rows = value.shape[0]
+    got = dot(jnp.concatenate([high, middle, low], axis=0), picks, 1, 0)
+    return got[:rows] + got[rows : 2 * rows] + got[2 * rows :]
 
 
 def normalize(projected):
@@ -157,7 +155,9 @@
 def near_kernel(dims, lens, hidden, projection, *refs):
     groups, count, length, passages, tokens, slots, step = dims
     packed = refs[:near]
-    pre_out, embed_out, shares_out, summed_out = refs[near:]
+    pre_out, embed_out, shares_out, summed_out, gather_out, spread_out = refs[near:]
+    gather_out[...] = token_picks(groups, count, length, gather_out.shape[1], True)
+    spread_out[...] = token_picks(groups, count, length, gather_out.shape[1], False)
     for at in range(passages // step):
         part = slice(at * step * tokens, (at + 1) * step * tokens)
         pre = dot(hidden[part, :], projection[...], 1, 0)
@@ -170,7 +170,8 @@
 def far_kernel(dims, lens, *refs):
     groups, count, length, passages, tokens, slots, step = dims
     packed = refs[:groups]
-    embed, summed_near, shares_out, inverse_out, stats_out, packet_out, summed, marks = refs[groups:]
+    embed, summed_near, gather, *refs = refs[groups:]
+    shares_out, inverse_out, stats_out, packet_out, summed, marks = refs
     rows = count * length
     me = lax.axis_index("group")
     marks[...] = jnp.full(marks.shape, -1.0, f32)
@@ -184,9 +185,7 @@
     total = jnp.concatenate([summed_near[...], summed[...]], axis=1)
     inverse_out[...] = 1.0 / total
     width = marks.shape[0]
-    scores = exact_dot(
-        smooth_temp * jnp.log(total), token_picks(groups, count, length, width, True)
-    )
+    scores = exact_dot(smooth_temp * jnp.log(total), gather[...])
     marks_t = marks[...].T
     ids = marks_t[:slots, :]
     first = me * passages
@@ -227,6 +226,7 @@
     packets,
     stats,
     inverse,
+    spread,
     shares,
     embed,
     *refs,
@@ -255,8 +255,7 @@
     boosted = stats[passages : 2 * passages, :]
     chosen = stats[2 * passages :, :]
     grad = grown * (1.0 + boosted * grown / hard_mean) / partition - chosen
-    spread = exact_dot(grad, token_picks(groups, count, length, width, False))
-    found = (spread * inverse[...]).astype(bf16)
+    found = (exact_dot(grad, spread[...]) * inverse[...]).astype(bf16)
     for p in range(passages):
         weights[p] = found[p : p + 1, :]
     query_grads(dims, shares, slice(near * rows, groups * rows), embed, weights, running)
@@ -399,16 +398,18 @@
 
     blocks = [packed] + [swap(packed, k) for k in range(1, groups)]
 
-    passage_pre, passage_embed, shares_near, summed_near = pl.pallas_call(
+    passage_pre, passage_embed, shares_near, summed_near, gather, spread = pl.pallas_call(
         functools.partial(near_kernel, dims),
         out_shape=(
             shape((passage_rows, depth), f32),
             shape((passage_rows, depth), bf16),
             shape((passage_rows, near * rows), bf16),
             shape((passages, near * rows), f32),
+            shape((all_rows, pool_width), bf16),
+            shape((pool_width, all_rows), bf16),
         ),
         in_specs=[VMEM] * (near + 3),
-        out_specs=(VMEM,) * 4,
+        out_specs=(VMEM,) * 6,
         compiler_params=params(32),
         cost_estimate=cost(
             2 * passage_rows * (width + near * rows) * depth,
@@ -427,7 +428,7 @@
             shape((3 * passages, pool_width), f32),
             shape((devices, packet_rows, pool_width), f32),
         ),
-        in_specs=[VMEM] * (groups + 3),
+        in_specs=[VMEM] * (groups + 4),
         out_specs=(VMEM, VMEM, VMEM, VMEM),
         scratch_shapes=[
             pltpu.VMEM((passages, far_rows), f32),
@@ -438,7 +439,7 @@
             2 * passage_rows * far_rows * depth, passage_rows * far_rows * 2, passage_rows * far_rows
         ),
         name="forward_far",
-    )(lens, *blocks, passage_embed, summed_near)
+    )(lens, *blocks, passage_embed, summed_near, gather)
 
     packets = lax.all_to_all(packets, axes, 0, 0, tiled=True)
 
@@ -449,13 +450,13 @@
             shape((passages, 1, all_rows), bf16),
             shape((8, pool_width), f32),
         ),
-        in_specs=[VMEM] * 5,
+        in_specs=[VMEM] * 6,
         out_specs=(VMEM,) * (groups - near + 2),
         scratch_shapes=[pltpu.VMEM((depth, far_rows), f32)],
         compiler_params=params(32),
         cost_estimate=cost(2 * passage_rows * far_rows * depth, passage_rows * far_rows * 2),
         name="query_grad_far",
-    )(packets, stats, inverse, shares_far, passage_embed)
+    )(packets, stats, inverse, spread, shares_far, passage_embed)
     near_parts = pl.pallas_call(
         functools.partial(near_grad_kernel, dims),
         out_shape=(shape((depth, rows), bf16),) * near,
@@ -467,7 +468,7 @@
         name="query_grad_near",
     )(weights, shares_near, passage_embed)
     parts = [*near_parts, *far_parts]
-    parts = [parts[0]] + [swap(parts[k], k) for k in range(1, groups)]
+    parts = [swap(parts[k], k) for k in range(groups - 1, 0, -1)] + [parts[0]]
 
     passage_back, weight, pre_t, hidden_t = pl.pallas_call(
         functools.partial(passage_grad_kernel, dims),

time: 56.5 us -> 56.2 us (level)
  waiting for transfers between devices: 16.1 us -> 15.5 us
  transfers between devices with their start and end apart: 8 -> 8, of which waited for: 4 -> 4; matrix products, arithmetic and copies ran while one was open for 8% -> 8% of each run, Pallas kernels for 10% -> 11%
where the time goes in v5:
time: 56.2 us; the launch traced here: 55.9 us
  waiting for transfers between devices  15.5 us (28%)
  blocking collectives  12.4 us (22%)
  Pallas kernels  11.7 us (21%)
  starting transfers between devices  10.1 us (18%)
  matrix products  3.69 us (7%)
  local copies, waits for them, and re-layouts  0.9 us (2%)
  other arithmetic  0.78 us (1%)
  between operations  0.75 us (1%)
    all_to_all x1, blocking collectives, local(): packets = lax.all_to_all(packets, axes, 0, 0, tiled=True)  12.4 us
    all_to_all x1, waiting for transfers between devices, local(): copies = lax.all_to_all(copies, axes, 0, 0, tiled=True)  7.54 us
    all_to_all x1, waiting for transfers between devices, local(): weight = lax.all_to_all(weight, axes, 0, 0, tiled=True)  6.7 us
    ppermute x6, starting transfers between devices, swap(): return lax.ppermute(value, 'group', [(i, i ^ k) for i in range(groups)])  5.11 us
    dot_general x2, matrix products, dot(): lax.dot_general(left, right, (((left_dim,), (right_dim,)), ((), ())), pre...  3.69 us
    pallas_call x1, Pallas kernels, local(): pl.pallas_call(functools.partial(near_kernel, dims), out_shape=(shape((pa...  3.29 us
    all_to_all x1, starting transfers between devices, local(): weight = lax.all_to_all(weight, axes, 0, 0, tiled=True)  2.63 us
    pallas_call x1, Pallas kernels, local(): pl.pallas_call(functools.partial(passage_grad_kernel, dims), out_shape=(s...  2.48 us
  transfers between devices with their start and end apart: 8, of which 4 were waited for; matrix products, arithmetic and copies ran while one was open for 8% of the time, Pallas kernels for 11%

profile of v5, /device:TPU:1, one launch (start us, length us, event | category | flops | bytes accessed | tf_op | source)
XLA Modules:
  0.0 55.9 jit_solution(4958653231029606107)
XLA Ops:
  0.6 1.6 %query_embed.1 = (f32[256,128]{1,0:T(8,128)S(1)}, bf16[272,128]{1,0:T(8,128)(2,1)S(1)}, bf16[768,128]{1,0:T(8,128)(2,1)S(1)}, s32[16,128]{1,0:T(8,128)S(1)}) custom-call(bf16[256,768]{1,0:T(8,128)(2,1)} %bitcast.16, bf16[768,128]{1,0:T(8,128)(2,1)} %projection_hbm.1, s32[8,32]{1,0:T(8,128)} %ids_hbm.1, s32[8]{0:T(128)} %positive_hbm.1, s32[16]{0:T(128)} %lens_hbm.1), custom_call_target="tpu_custom_call" | custom-call | flops 20000000000 | bytes 393216 | tf_op jit(solution)/shard_map/query_embed/pallas_call | solution.py:374
  2.4 2.7 %collective-permute-start.1 = (bf16[272,128]{1,0:T(8,128)(2,1)S(1)}, bf16[272,128]{1,0:T(8,128)(2,1)S(1)}, u32[]{:S(2)}, u32[]{:S(2)}) collective-permute-start(bf16[272,128]{1,0:T(8,128)(2,1)S(1)} %get-tuple-element.33.refs_0_), channel_id=1, source_target_pairs={{0,16},{8,24},{16,0},{24,8},{1,17},{9,25},{17,1},{25,9},{2,18},{10... | collective-permute-start | bytes 208904 | tf_op jit(solution)/shard_map/ppermute | solution.py:397
  5.1 3.3 %forward_near.1 = (f32[2048,128]{1,0:T(8,128)S(1)}, bf16[2048,128]{1,0:T(8,128)(2,1)S(1)}, bf16[2048,512]{1,0:T(8,128)(2,1)S(1)}, f32[16,512]{1,0:T(8,128)S(1)},...) custom-call(s32[16,128]{1,0:T(8,128)S(1)} %get-tuple-element.32.lens, bf16[2048,768]{1,0:T(8,128)(2,1)S(1)} %bitcast.14, ...), custom_call_target="tpu_custom_call" | custom-call | flops 671088640 | bytes 6815744 | tf_op jit(solution)/shard_map/forward_near/pallas_call | solution.py:401
  8.4 0.8 %collective-permute-done.2.refs_3_ = bf16[272,128]{1,0:T(8,128)(2,1)S(1)} collective-permute-done((bf16[272,128]{1,0:T(8,128)(2,1)S(1)}, bf16[272,128]{1,0:T(8,128)(2,1)S(1)}, u32[]{:S(2)}, u32[]{:S(2)}) %collective-permute-start.2) | collective-permute-done | bytes 69664 | tf_op jit(solution)/shard_map/ppermute | solution.py:397
  9.2 1.3 %forward_far.1 = (bf16[2048,512]{1,0:T(8,128)(2,1)S(1)}, f32[16,1024]{1,0:T(8,128)S(1)}, f32[48,128]{1,0:T(8,128)S(1)}, f32[32,1,128]{2,1,0:T(1,128)S(1)}) custom-call(s32[16,128]{1,0:T(8,128)S(1)} %get-tuple-element.32.lens, bf16[272,128]{1,0:T(8,128)(2,1)S(1)} %get-tuple-element.33.refs_0_, bf16[272,128]{1,0:T(8,128)(2,1)S(1)} %collective-permute-done.refs_1_, ...), custom_call_target="tpu_custom_call" | custom-call | flops 268435456 | bytes 2097152 | tf_op jit(solution)/shard_map/forward_far/pallas_call | solution.py:423
  10.5 12.4 %all_to_all.15.packets = f32[32,1,128]{2,1,0:T(1,128)S(1)} all-to-all(f32[32,1,128]{2,1,0:T(1,128)S(1)} %get-tuple-element.38), channel_id=1, replica_groups=mesh['group'=4,'dp'=8] {'dp','group'}, dimensions={0} | all-to-all | bytes 32768 | tf_op jit(solution)/shard_map/all_to_all | solution.py:444
  23.0 0.8 %query_grad_far.1 = (bf16[128,256]{1,0:T(8,128)(2,1)S(1)}, bf16[128,256]{1,0:T(8,128)(2,1)S(1)}, bf16[16,1,1024]{2,1,0:T(2,128)(2,1)S(1)}, f32[8,128]{1,0:T(8,128)S(1)}) custom-call(f32[32,1,128]{2,1,0:T(1,128)S(1)} %all_to_all.15.packets, f32[48,128]{1,0:T(8,128)S(1)} %get-tuple-element.39.stats, f32[16,1024]{1,0:T(8,128)S(1)} %get-tuple-element.40.inverse, ...), custom_call_target="tpu_custom_call" | custom-call | flops 268435456 | bytes 2097152 | tf_op jit(solution)/shard_map/query_grad_far/pallas_call | solution.py:446
  23.8 0.8 %collective-permute-start.3 = (bf16[128,256]{1,0:T(8,128)(2,1)S(1)}, bf16[128,256]{1,0:T(8,128)(2,1)S(1)}, u32[]{:S(2)}, u32[]{:S(2)}) collective-permute-start(bf16[128,256]{1,0:T(8,128)(2,1)S(1)} %get-tuple-element.51), channel_id=1, source_target_pairs={{0,24},{8,16},{16,8},{24,0},{1,25},{9,17},{17,9},{25,1},{2,26},{10... | collective-permute-start | bytes 196616 | tf_op jit(solution)/shard_map/ppermute | solution.py:397
  24.6 1.2 %collective-permute-start.4 = (bf16[128,256]{1,0:T(8,128)(2,1)S(1)}, bf16[128,256]{1,0:T(8,128)(2,1)S(1)}, u32[]{:S(2)}, u32[]{:S(2)}) collective-permute-start(bf16[128,256]{1,0:T(8,128)(2,1)S(1)} %get-tuple-element.52), channel_id=1, source_target_pairs={{0,16},{8,24},{16,0},{24,8},{1,17},{9,25},{17,1},{25,9},{2,18},{10... | collective-permute-start | bytes 196616 | tf_op jit(solution)/shard_map/ppermute | solution.py:397
  25.8 0.5 query_grad_near.1
  26.3 0.2 collective-permute-start.5
  26.5 0.3 copy-done.1
  26.8 2.5 %passage_grad.1 = (bf16[2048,128]{1,0:T(8,128)(2,1)S(1)}, f32[768,128]{1,0:T(8,128)S(1)}, f32[128,256]{1,0:T(8,128)S(1)}, bf16[768,256]{1,0:T(8,128)(2,1)S(1)}) custom-call(bf16[16,1,1024]{2,1,0:T(2,128)(2,1)S(1)} %get-tuple-element.44.weights, bf16[2048,512]{1,0:T(8,128)(2,1)S(1)} %get-tuple-element.45.shares_near.shares, ...), custom_call_target="tpu_custom_call" | custom-call | flops 939524096 | bytes 8912896 | tf_op jit(solution)/shard_map/passage_grad/pallas_call | solution.py:473
  29.3 0.5 collective-permute-done.4.refs_1_
  29.8 1.0 %query_back.1 = (bf16[128,256]{1,0:T(8,128)(2,1)S(1)}, bf16[768,128]{1,0:T(8,128)(2,1)}) custom-call(f32[128,256]{1,0:T(8,128)S(1)} %get-tuple-element.48.pre, bf16[768,256]{1,0:T(8,128)(2,1)S(1)} %get-tuple-element.49.hidden, f32[768,128]{1,0:T(8,128)S(1)} %get-tuple-element.50.weight, bf16[128,256]{1,0:T(8,128)(2,1)S(1)} %collective-permute-done.3.refs_0_, ...), custom_call_target="tpu_custom_call" | custom-call | flops 50331648 | bytes 983040 | tf_op jit(solution)/shard_map/query_back/pallas_call | solution.py:492
  30.8 2.6 %all-to-all-start.1 = ((bf16[32,24,128]{2,1,0:T(8,128)(2,1)}), bf16[32,24,128]{2,1,0:T(8,128)(2,1)S(1)}, u32[]{:S(2)}, u32[]{:S(2)}) async-start(bf16[32,24,128]{2,1,0:T(8,128)(2,1)} %bitcast.3), calls=%async_computation.1 | async-start | bytes 393216 | tf_op jit(solution)/shard_map/all_to_all | solution.py:503
  33.5 2.7 %convolution_convert_fusion = bf16[2048,768]{1,0:T(8,128)(2,1)} fusion(bf16[2048,128]{1,0:T(8,128)(2,1)S(1)} %get-tuple-element.56, bf16[768,128]{1,0:T(8,128)(2,1)S(1)} %copy-done.2), kind=kOutput, calls=%fused_computation | convolution fusion | flops 404226048 | bytes 3866624 | tf_op jit(solution)/shard_map/dot_general | solution.py:21
  36.2 6.7 %all-to-all-done.1.parts = bf16[32,24,128]{2,1,0:T(8,128)(2,1)S(1)} async-done(((bf16[32,24,128]{2,1,0:T(8,128)(2,1)}), bf16[32,24,128]{2,1,0:T(8,128)(2,1)S(1)}, u32[]{:S(2)}, u32[]{:S(2)}) %all-to-all-start.1) | async-done | bytes 196640 | tf_op jit(solution)/shard_map/all_to_all | solution.py:503
  42.9 0.7 %sum_parts.1 = bf16[32,24,128]{2,1,0:T(8,128)(2,1)} custom-call(bf16[32,24,128]{2,1,0:T(8,128)(2,1)S(1)} %all-to-all-done.1.parts), custom_call_target="tpu_custom_call" | custom-call | tf_op jit(solution)/shard_map/sum_parts/pallas_call | solution.py:506
  43.6 2.3 %all-to-all-start.2 = ((bf16[32,24,128]{2,1,0:T(8,128)(2,1)}), bf16[32,24,128]{2,1,0:T(8,128)(2,1)S(1)}, u32[]{:S(2)}, u32[]{:S(2)}) async-start(bf16[32,24,128]{2,1,0:T(8,128)(2,1)} %sum_parts.1), calls=%async_computation.2 | async-start | bytes 393216 | tf_op jit(solution)/shard_map/all_to_all | solution.py:514
  45.9 0.6 %dynamic-slice_bitcast_fusion = f32[8]{0:T(128)} fusion(f32[1,128]{1,0:T(1,128)S(1)} %slice.3, s32[]{:T(128)S(6)} %select_n.3), kind=kLoop, calls=%fused_computation.3 | loop fusion | bytes 68 | tf_op jit(solution)/shard_map/dynamic_slice | solution.py:519
  46.5 1.0 %convolution_convert_fusion.1 = bf16[256,768]{1,0:T(8,128)(2,1)} fusion(bf16[128,256]{1,0:T(8,128)(2,1)S(1)} %get-tuple-element.58, bf16[768,128]{1,0:T(8,128)(2,1)S(1)} %copy-done.2), kind=kOutput, calls=%fused_computation.1 | convolution fusion | flops 50528256 | bytes 655360 | tf_op jit(solution)/shard_map/dot_general | solution.py:21
  47.5 7.5 %all-to-all-done.2 = bf16[32,24,128]{2,1,0:T(8,128)(2,1)S(1)} async-done(((bf16[32,24,128]{2,1,0:T(8,128)(2,1)}), bf16[32,24,128]{2,1,0:T(8,128)(2,1)S(1)}, u32[]{:S(2)}, u32[]{:S(2)}) %all-to-all-start.2) | async-done | bytes 196640 | tf_op jit(solution)/shard_map/all_to_all | solution.py:514
  55.1 0.8 %bitcast_convert_fusion = f32[768,128]{1,0:T(8,128)} fusion(bf16[32,24,128]{2,1,0:T(8,128)(2,1)S(1)} %all-to-all-done.2), kind=kLoop, calls=%fused_computation.2 | loop fusion | flops 98304 | bytes 589824 | tf_op jit(solution)/shard_map/convert_element_type | solution.py:515
  (12 shorter events, 0.2 us)
Async XLA Ops:
  0.6 4.5 %copy-start = (bf16[16,128,768]{2,1,0:T(8,128)(2,1)S(1)}, bf16[16,128,768]{2,1,0:T(8,128)(2,1)}, u32[]{:S(2)}) copy-start(bf16[16,128,768]{2,1,0:T(8,128)(2,1)} %param.7) | copy-start | bytes 9437188
  2.3 2.8 %collective-permute-start = (bf16[272,128]{1,0:T(8,128)(2,1)S(1)}, bf16[272,128]{1,0:T(8,128)(2,1)S(1)}, u32[]{:S(2)}, u32[]{:S(2)}) collective-permute-start(bf16[272,128]{1,0:T(8,128)(2,1)S(1)} %get-tuple-element.33.refs_0_), channel_id=1, source_target_pairs={{0,8},{8,0},{16,24},{24,16},{1,9},{9,1},{17,25},{25,17},{2,10},{10... | collective-permute-start | bytes 208904 | tf_op jit(solution)/shard_map/ppermute | solution.py:397
  2.4 6.0 %collective-permute-start.1 = (bf16[272,128]{1,0:T(8,128)(2,1)S(1)}, bf16[272,128]{1,0:T(8,128)(2,1)S(1)}, u32[]{:S(2)}, u32[]{:S(2)}) collective-permute-start(bf16[272,128]{1,0:T(8,128)(2,1)S(1)} %get-tuple-element.33.refs_0_), channel_id=1, source_target_pairs={{0,16},{8,24},{16,0},{24,8},{1,17},{9,25},{17,1},{25,9},{2,18},{10... | collective-permute-start | bytes 208904 | tf_op jit(solution)/shard_map/ppermute | solution.py:397
  5.1 4.1 %collective-permute-start.2 = (bf16[272,128]{1,0:T(8,128)(2,1)S(1)}, bf16[272,128]{1,0:T(8,128)(2,1)S(1)}, u32[]{:S(2)}, u32[]{:S(2)}) collective-permute-start(bf16[272,128]{1,0:T(8,128)(2,1)S(1)} %get-tuple-element.33.refs_0_), channel_id=1, source_target_pairs={{0,24},{8,16},{16,8},{24,0},{1,25},{9,17},{17,9},{25,1},{2,26},{10... | collective-permute-start | bytes 208904 | tf_op jit(solution)/shard_map/ppermute | solution.py:397
  23.8 5.5 %collective-permute-start.3 = (bf16[128,256]{1,0:T(8,128)(2,1)S(1)}, bf16[128,256]{1,0:T(8,128)(2,1)S(1)}, u32[]{:S(2)}, u32[]{:S(2)}) collective-permute-start(bf16[128,256]{1,0:T(8,128)(2,1)S(1)} %get-tuple-element.51), channel_id=1, source_target_pairs={{0,24},{8,16},{16,8},{24,0},{1,25},{9,17},{17,9},{25,1},{2,26},{10... | collective-permute-start | bytes 196616 | tf_op jit(solution)/shard_map/ppermute | solution.py:397
  24.6 5.2 %collective-permute-start.4 = (bf16[128,256]{1,0:T(8,128)(2,1)S(1)}, bf16[128,256]{1,0:T(8,128)(2,1)S(1)}, u32[]{:S(2)}, u32[]{:S(2)}) collective-permute-start(bf16[128,256]{1,0:T(8,128)(2,1)S(1)} %get-tuple-element.52), channel_id=1, source_target_pairs={{0,16},{8,24},{16,0},{24,8},{1,17},{9,25},{17,1},{25,9},{2,18},{10... | collective-permute-start | bytes 196616 | tf_op jit(solution)/shard_map/ppermute | solution.py:397
  25.8 1.0 %copy-start.1 = (bf16[8,32,768]{2,1,0:T(8,128)(2,1)S(1)}, bf16[8,32,768]{2,1,0:T(8,128)(2,1)}, u32[]{:S(2)}) copy-start(bf16[8,32,768]{2,1,0:T(8,128)(2,1)} %param.6) | copy-start | bytes 1179652
  26.3 3.5 %collective-permute-start.5 = (bf16[128,256]{1,0:T(8,128)(2,1)S(1)}, bf16[128,256]{1,0:T(8,128)(2,1)S(1)}, u32[]{:S(2)}, u32[]{:S(2)}) collective-permute-start(bf16[128,256]{1,0:T(8,128)(2,1)S(1)} %get-tuple-element.53), channel_id=1, source_target_pairs={{0,8},{8,0},{16,24},{24,16},{1,9},{9,1},{17,25},{25,17},{2,10},{10... | collective-permute-start | bytes 196616 | tf_op jit(solution)/shard_map/ppermute | solution.py:397
  26.8 6.7 %copy-start.2 = (bf16[768,128]{1,0:T(8,128)(2,1)S(1)}, bf16[768,128]{1,0:T(8,128)(2,1)}, u32[]{:S(2)}) copy-start(bf16[768,128]{1,0:T(8,128)(2,1)} %projection_hbm.1) | copy-start | bytes 589828
  30.8 12.0 %all-to-all-start.1 = ((bf16[32,24,128]{2,1,0:T(8,128)(2,1)}), bf16[32,24,128]{2,1,0:T(8,128)(2,1)S(1)}, u32[]{:S(2)}, u32[]{:S(2)}) async-start(bf16[32,24,128]{2,1,0:T(8,128)(2,1)} %bitcast.3), calls=%async_computation.1 | async-start | bytes 393216 | tf_op jit(solution)/shard_map/all_to_all | solution.py:503
  43.6 11.5 %all-to-all-start.2 = ((bf16[32,24,128]{2,1,0:T(8,128)(2,1)}), bf16[32,24,128]{2,1,0:T(8,128)(2,1)S(1)}, u32[]{:S(2)}, u32[]{:S(2)}) async-start(bf16[32,24,128]{2,1,0:T(8,128)(2,1)} %sum_parts.1), calls=%async_computation.2 | async-start | bytes 393216 | tf_op jit(solution)/shard_map/all_to_all | solution.py:514

commit v6 on v5

v6 whole, which is shorter than its diff:
```python
import functools

import jax
import jax.numpy as jnp
from jax import lax
from jax.experimental import pallas as pl
from jax.experimental.pallas import tpu as pltpu
from jax.sharding import PartitionSpec as P

smooth_temp = 0.1
norm_eps = 1e-06
center = 0.375
lanes = 128
cores = 2
axes = ("dp", "group")
f32 = jnp.float32
bf16 = jnp.bfloat16


def dot(left, right, left_dim, right_dim):
    return lax.dot_general(
        left, right, (((left_dim,), (right_dim,)), ((), ())), preferred_element_type=f32
    )


def exact_dot(value, picks):
    high = value.astype(bf16)
    rest = value - high.astype(f32)
    middle = rest.astype(bf16)
    low = (rest - middle.astype(f32)).astype(bf16)
    rows = value.shape[0]
    got = dot(jnp.concatenate([high, middle, low], axis=0), picks, 1, 0)
    return got[:rows] + got[rows : 2 * rows] + got[2 * rows :]


def normalize(projected):
    return projected * lax.rsqrt(jnp.sum(projected * projected, axis=-1, keepdims=True) + norm_eps)


def normalize_back(projected, grad):
    inverse = lax.rsqrt(jnp.sum(projected * projected, axis=-1, keepdims=True) + norm_eps)
    along = jnp.sum(projected * grad, axis=-1, keepdims=True)
    return grad * inverse - projected * (inverse * inverse * inverse * along)


def iota(shape, dim):
    return lax.broadcasted_iota(jnp.int32, shape, dim)


def params(megabytes):
    return pltpu.CompilerParams(vmem_limit_bytes=megabytes * 2**20)


def cost(flops, nbytes, exps=0):
    return pl.CostEstimate(flops=int(flops), bytes_accessed=int(nbytes), transcendentals=int(exps))


VMEM = pl.BlockSpec(memory_space=pltpu.VMEM)
HBM = pl.BlockSpec(memory_space=pltpu.HBM)


def in_hbm(*values):
    return [pltpu.with_memory_space_constraint(value, pltpu.HBM) for value in values]


def query_kernel(
    hidden_hbm,
    projection_hbm,
    ids_hbm,
    positive_hbm,
    lens_hbm,
    pre_out,
    packed_out,
    projection,
    lens_out,
    hidden,
    hard_ids,
    positive,
    lens,
    sems,
):
    copies = [
        pltpu.make_async_copy(source, target, sems.at[k])
        for k, (source, target) in enumerate(
            [
                (projection_hbm, projection),
                (hidden_hbm, hidden),
                (ids_hbm, hard_ids),
                (positive_hbm, positive),
                (lens_hbm, lens),
            ]
        )
    ]
    for copy in copies:
        copy.start()
    for copy in copies[2:]:
        copy.wait()
    rows = hidden.shape[0]
    count, slots = hard_ids.shape
    row = iota((count, lanes), 0)
    column = iota((count, lanes), 1)
    marks = jnp.full((count, lanes), -1.0, f32)
    for k in range(count):
        marks = jnp.where((row == k) & (column == slots), positive[k].astype(f32), marks)
    ids = jnp.concatenate(
        [hard_ids[...].astype(f32), jnp.full((count, lanes - slots), -1.0, f32)], axis=1
    )
    marks = jnp.where(column < slots, ids, marks)
    extra = packed_out.shape[0] - rows
    marks = jnp.concatenate([marks, jnp.full((extra - count, lanes), -1.0, f32)], axis=0)
    packed_out[rows:, :] = marks.astype(bf16)
    for p in range(lens_out.shape[0]):
        lens_out[p : p + 1, :] = jnp.full((1, lanes), lens[p], jnp.int32)
    for copy in copies[:2]:
        copy.wait()
    pre = dot(hidden[...], projection[...], 1, 0)
    pre_out[...] = pre
    packed_out[:rows, :] = normalize(pre).astype(bf16)


def parted(index, size):
    if size & (size - 1) == 0:
        return lax.shift_right_logical(index, size.bit_length() - 1)
    return index // size


def token_picks(dims, width, rows_first):
    blocks, count, length = dims[:3]
    chip = lax.axis_index("group") // cores
    tokens = blocks * count * length
    shape = (tokens, width) if rows_first else (width, tokens)
    token = iota(shape, 0 if rows_first else 1)
    query = iota(shape, 1 if rows_first else 0)
    owner = jnp.bitwise_xor(parted(token, length), chip * count)
    return jnp.where(owner == query, 1.0, 0.0).astype(bf16)


def passage_kernel(dims, lens, hidden, projection, pre_out, embed_out, gather_out, spread_out):
    blocks, count, length, passages, tokens, slots, step = dims
    for start in range(0, hidden.shape[0], step * tokens):
        part = slice(start, start + step * tokens)
        pre = dot(hidden[part, :], projection[...], 1, 0)
        pre_out[part, :] = pre
        embed_out[part, :] = normalize(pre).astype(bf16)
    embed_out[hidden.shape[0] :, :] = lens[...].astype(f32).astype(bf16)
    gather_out[...] = token_picks(dims, gather_out.shape[1], True)
    spread_out[...] = token_picks(dims, gather_out.shape[1], False)


def forward_part(dims, embed, queries, shares_out, summed, first):
    blocks, count, length, passages, tokens, slots, step = dims
    rows = count * length
    lens = embed[passages * tokens :, :].astype(f32).astype(jnp.int32)
    for at in range(passages // step):
        part = embed[at * step * tokens : (at + 1) * step * tokens, :]
        for k, block in enumerate(queries):
            columns = slice(k * rows, (k + 1) * rows)
            similar = dot(part, block[:rows, :], 1, 1)
            for p in range(step):
                row = at * step + p
                piece = similar[p * tokens : (p + 1) * tokens, :]
                live = jnp.concatenate([lens[row : row + 1, :]] * (rows // lanes), axis=1)
                grown = jnp.exp(piece * (1.0 / smooth_temp))
                grown = jnp.where(iota(piece.shape, 0) < live, grown, 0.0)
                shares_out[row * tokens : (row + 1) * tokens, columns] = grown.astype(bf16)
                summed[first + row : first + row + 1, columns] = jnp.sum(
                    grown, axis=0, keepdims=True
                )


def forward_kernel(dims, embed, *refs):
    forward_part(dims, embed, refs[:-2], refs[-2], refs[-1], 0)


def far_kernel(dims, *refs):
    blocks, count, length, passages, tokens, slots, step = dims
    packed = refs[:blocks]
    embed_other, summed_near, summed_far, gather, *refs = refs[blocks:]
    shares_other, inverse_out, stats_out, packet_out, summed, marks = refs
    rows = count * length
    me = lax.axis_index("group")
    marks[...] = jnp.full(marks.shape, -1.0, f32)
    for k in range(blocks):
        start = pl.multiple_of(jnp.bitwise_xor(me // cores, k) * count, count)
        marks[pl.ds(start, count), :] = packed[k][rows:, :].astype(f32)[:count]
    forward_part(dims, embed_other, packed, shares_other, summed, passages)
    summed[:passages, :rows] = summed_near[...]
    summed[:passages, rows:] = summed_far[...]
    total = summed[...]
    inverse_out[...] = 1.0 / total
    width = marks.shape[0]
    scores = exact_dot(smooth_temp * jnp.log(total), gather[...])
    marks_t = marks[...].T
    ids = marks_t[:slots, :]
    pair = cores * passages
    first = [me * passages, jnp.bitwise_xor(me, 1) * passages]
    counts = jnp.concatenate(
        [
            jnp.sum(
                jnp.where(ids == (first[p // passages] + p % passages).astype(f32), 1.0, 0.0),
                axis=0,
                keepdims=True,
            )
            for p in range(pair)
        ],
        axis=0,
    )
    row = iota((pair, width), 0)
    here = jnp.where(row < passages, row + first[0], row - passages + first[1])
    chosen = here.astype(f32) == marks_t[slots : slots + 1, :]
    grown = jnp.exp(scores - center * length)
    boost = blocks * pair / slots
    boosted = jnp.where(chosen, 0.0, boost * counts)
    stats_out[:pair, :] = grown
    stats_out[pair : 2 * pair, :] = boosted
    stats_out[2 * pair :, :] = jnp.where(chosen, 1.0, 0.0)
    plain = jnp.sum(grown, axis=0, keepdims=True)
    hard = jnp.sum(boosted * grown * grown, axis=0, keepdims=True)
    kept = jnp.sum(jnp.where(chosen, scores, 0.0), axis=0, keepdims=True)
    sums = jnp.sum(counts * grown, axis=0, keepdims=True)
    sums = jnp.broadcast_to(jnp.sum(sums, axis=1, keepdims=True), sums.shape)
    queries = blocks * count
    if packet_out.shape[1] == 1:
        lane = iota(plain.shape, 1)
        packet = jnp.where(lane < queries, plain, sums)
        packet = jnp.where(lane // queries == 1, pltpu.roll(hard, queries, 1), packet)
        packet = jnp.where(lane // queries == 2, pltpu.roll(kept, 2 * queries, 1), packet)
    else:
        packet = jnp.concatenate([plain, hard, kept, sums] * 2, axis=0)
    for k in range(packet_out.shape[0]):
        packet_out[k] = packet


def coefficients(dims, shares, columns, weights, first, at):
    passages, tokens, _, step = dims[3:]
    parts = []
    for p in range(at * step, (at + 1) * step):
        parts.append(shares[p * tokens : (p + 1) * tokens, :] * weights[first + p, :, columns])
    return jnp.concatenate(parts, axis=0)


def query_grads(dims, sources, weights, running):
    blocks, count, length, passages, tokens, slots, step = dims
    for k, (embed, shares, columns, first) in enumerate(sources):
        for at in range(passages // step):
            part = embed[at * step * tokens : (at + 1) * step * tokens, :].T
            terms = dot(part, coefficients(dims, shares, columns, weights, first, at), 1, 0)
            if k == 0 and at == 0:
                running[...] = terms
            else:
                running[...] += terms


class Columns:
    def __init__(self, ref, columns):
        self.ref, self.columns = ref, columns

    def __getitem__(self, index):
        return self.ref[index[0], self.columns]


def far_grad_kernel(
    dims,
    packets,
    stats,
    inverse,
    spread,
    shares_far,
    shares_other,
    embed,
    embed_other,
    *refs,
):
    blocks, count, length, passages, tokens, slots, step = dims
    parts_out = refs[: blocks - 1]
    weights, losses_out, running = refs[blocks - 1 :]
    rows = count * length
    pair = cores * passages
    width = stats.shape[1]
    devices = packets.shape[0]
    groups = cores * blocks
    core = lax.axis_index("group") % cores
    pool = packets[pl.ds(lax.axis_index("dp") * groups, groups)]
    pool = jnp.where(iota(pool.shape, 0) % cores == core, pool, 0.0).sum(axis=0)
    every = packets[...].sum(axis=0)
    queries = blocks * count
    if packets.shape[1] == 1:
        plain = pool
        hard = pltpu.roll(pool, width - queries, 1)
        kept = pltpu.roll(pool, width - 2 * queries, 1)
        sums = every[:, 3 * queries : 3 * queries + 1]
    else:
        plain, hard, kept, sums = pool[0:1, :], pool[1:2, :], pool[2:3, :], every[3:4, 0:1]
    hard_mean = sums * (1.0 / (devices * count * slots))
    partition = jnp.where(iota(plain.shape, 1) < queries, plain + hard / hard_mean, 1.0)
    losses_out[...] = jnp.broadcast_to(
        jnp.log(partition) - (kept - center * length), losses_out.shape
    )
    grown = stats[:pair, :]
    boosted = stats[pair : 2 * pair, :]
    chosen = stats[2 * pair :, :]
    grad = grown * (1.0 + boosted * grown / hard_mean) / partition - chosen
    found = (exact_dot(grad, spread[...]) * inverse[...]).astype(bf16)
    for p in range(pair):
        weights[p] = found[p : p + 1, :]
    columns = slice(rows, blocks * rows)
    sources = [
        (embed, shares_far, columns, 0),
        (embed_other, Columns(shares_other, columns), columns, passages),
    ]
    query_grads(dims, sources, weights, running)
    for k, out in enumerate(parts_out):
        out[...] = running[:, k * rows : (k + 1) * rows].astype(bf16)


def other_grad_kernel(dims, weights, shares_other, *refs):
    blocks, count, length, passages, tokens, slots, step = dims
    packed = refs[:blocks]
    grad_out, queries = refs[blocks:]
    rows = count * length
    for k in range(blocks):
        queries[k * rows : (k + 1) * rows, :] = packed[k][:rows, :]
    columns = slice(0, blocks * rows)
    for at in range(passages // step):
        coefficient = coefficients(dims, shares_other, columns, weights, passages, at)
        grad = dot(coefficient, queries[...], 1, 0)
        grad_out[at * step * tokens : (at + 1) * step * tokens, :] = grad.astype(bf16)


def own_grad_kernel(
    dims,
    weights,
    shares_near,
    shares_far,
    shares_other,
    embed,
    embed_other,
    query_pre,
    query_hidden,
    *refs,
):
    blocks, count, length, passages, tokens, slots, step = dims
    packed = refs[:blocks]
    part_out, grad_out, pre_out, hidden_out, queries = refs[blocks:]
    rows = count * length
    for k in range(1, blocks):
        queries[(k - 1) * rows : k * rows, :] = packed[k][:rows, :]
    own, far = slice(0, rows), slice(rows, blocks * rows)
    for at in range(passages // step):
        part = slice(at * step * tokens, (at + 1) * step * tokens)
        near = coefficients(dims, shares_near, own, weights, 0, at)
        other = coefficients(dims, Columns(shares_other, own), own, weights, passages, at)
        terms = dot(embed[part, :].T, near, 1, 0) + dot(embed_other[part, :].T, other, 1, 0)
        if at == 0:
            part_out[...] = terms
        else:
            part_out[...] += terms
        grad_out[part, :] = dot(near, packed[0][:rows, :], 1, 0) + dot(
            coefficients(dims, shares_far, far, weights, 0, at), queries[...], 1, 0
        )
    pre_out[...] = query_pre[...].T
    hidden_out[...] = query_hidden[...].T


def passage_back_kernel(dims, grad, grad_other, pre, hidden, back_out, weight_out, running):
    blocks, count, length, passages, tokens, slots, step = dims
    for at in range(passages // step):
        part = slice(at * step * tokens, (at + 1) * step * tokens)
        total = grad[part, :] + grad_other[part, :].astype(f32)
        back = normalize_back(pre[part, :], total).astype(bf16)
        back_out[part, :] = back
        terms = dot(back.T, hidden[part, :], 1, 0)
        if at == 0:
            running[...] = terms
        else:
            running[...] += terms
    weight_out[...] = running[...].T


def normalize_back_columns(projected, grad):
    inverse = lax.rsqrt(jnp.sum(projected * projected, axis=0, keepdims=True) + norm_eps)
    along = jnp.sum(projected * grad, axis=0, keepdims=True)
    return grad * inverse - projected * (inverse * inverse * inverse * along)


def query_back_kernel(pre, hidden, weight, *refs):
    parts = refs[:-2]
    back_out, weight_out = refs[-2:]
    grad = sum(part[...].astype(f32) for part in parts)
    back = normalize_back_columns(pre[...], grad).astype(bf16)
    back_out[...] = back
    weight_out[...] = (weight[...] + dot(hidden[...], back, 1, 1)).astype(bf16)


def sum_kernel(parts, copies_out):
    devices = copies_out.shape[0]
    total = parts[0].astype(f32)
    for k in range(1, devices):
        total += parts[k].astype(f32)
    total = total.astype(bf16)
    for k in range(devices):
        copies_out[k] = total


def local(query_hidden, passage_hidden, projection, positive, hard_ids, passage_len):
    count, length, width = query_hidden.shape
    passages, tokens, _ = passage_hidden.shape
    depth = projection.shape[1]
    slots = hard_ids.shape[1]
    groups = lax.axis_size("group")
    devices = lax.axis_size(axes)
    blocks = groups // cores
    rows = count * length
    all_rows = blocks * rows
    far_rows = all_rows - rows
    passage_rows = passages * tokens
    pair = cores * passages
    pool_width = -(-blocks * count // lanes) * lanes
    packet_rows = 1 if 3 * blocks * count < lanes else 8
    step = 4 if blocks <= 2 else 1
    dims = (blocks, count, length, passages, tokens, slots, step)
    query_flat = query_hidden.reshape(rows, width)
    passage_flat = passage_hidden.reshape(passage_rows, width)
    shape = jax.ShapeDtypeStruct

    query_pre, packed, projection_near, lens = pl.pallas_call(
        query_kernel,
        out_shape=(
            shape((rows, depth), f32),
            shape((rows + 16, depth), bf16),
            shape((width, depth), bf16),
            shape((passages, lanes), jnp.int32),
        ),
        in_specs=[HBM] * 5,
        out_specs=(VMEM,) * 4,
        scratch_shapes=[
            pltpu.VMEM((rows, width), bf16),
            pltpu.VMEM((count, slots), jnp.int32),
            pltpu.SMEM((count,), jnp.int32),
            pltpu.SMEM((passages,), jnp.int32),
            pltpu.SemaphoreType.DMA((5,)),
        ],
        compiler_params=params(16),
        cost_estimate=cost(2e10, rows * width * 2),
        name="query_embed",
    )(*in_hbm(query_flat, projection, hard_ids, positive, passage_len))

    def swap(value, k):
        return lax.ppermute(value, "group", [(i, i ^ k) for i in range(groups)])

    queries = [packed] + [swap(packed, cores * k) for k in range(1, blocks)]

    passage_pre, embed, gather, spread = pl.pallas_call(
        functools.partial(passage_kernel, dims),
        out_shape=(
            shape((passage_rows, depth), f32),
            shape((passage_rows + passages, depth), bf16),
            shape((all_rows, pool_width), bf16),
            shape((pool_width, all_rows), bf16),
        ),
        in_specs=[VMEM] * 3,
        out_specs=(VMEM,) * 4,
        compiler_params=params(16),
        cost_estimate=cost(2 * passage_rows * width * depth, passage_rows * (width * 2 + depth * 6)),
        name="passage_embed",
    )(lens, passage_flat, projection_near)
    embed_other = swap(embed, 1)

    def forward_cost(passage_count, query_rows):
        pairs = passage_count * tokens * query_rows
        return cost(2 * pairs * depth, pairs * 2, pairs)

    def forward(name, blocks_of_queries, estimate):
        query_rows = len(blocks_of_queries) * rows
        return pl.pallas_call(
            functools.partial(forward_kernel, dims),
            out_shape=(shape((passage_rows, query_rows), bf16), shape((passages, query_rows), f32)),
            in_specs=[VMEM] * (1 + len(blocks_of_queries)),
            out_specs=(VMEM,) * 2,
            compiler_params=params(16),
            cost_estimate=estimate,
            name=name,
        )(embed, *blocks_of_queries)

    shares_near, summed_near = forward("forward_near", queries[:1], forward_cost(passages, rows))
    shares_far, summed_far = forward("forward_far", queries[1:], cost(1e10, 1e6))
    shares_other, inverse, stats, packets = pl.pallas_call(
        functools.partial(far_kernel, dims),
        out_shape=(
            shape((passage_rows, all_rows), bf16),
            shape((pair, all_rows), f32),
            shape((3 * pair, pool_width), f32),
            shape((devices, packet_rows, pool_width), f32),
        ),
        in_specs=[VMEM] * (blocks + 4),
        out_specs=(VMEM,) * 4,
        scratch_shapes=[
            pltpu.VMEM((pair, all_rows), f32),
            pltpu.VMEM((pool_width, lanes), f32),
        ],
        compiler_params=params(32),
        cost_estimate=forward_cost(passages, all_rows),
        name="forward_other",
    )(*queries, embed_other, summed_near, summed_far, gather)

    packets = lax.all_to_all(packets, axes, 0, 0, tiled=True)

    *far_parts, weights, losses = pl.pallas_call(
        functools.partial(far_grad_kernel, dims),
        out_shape=(
            *[shape((depth, rows), bf16)] * (blocks - 1),
            shape((pair, 1, all_rows), bf16),
            shape((8, pool_width), f32),
        ),
        in_specs=[VMEM] * 8,
        out_specs=(VMEM,) * (blocks + 1),
        scratch_shapes=[pltpu.VMEM((depth, far_rows), f32)],
        compiler_params=params(32),
        cost_estimate=forward_cost(pair, far_rows),
        name="query_grad_far",
    )(packets, stats, inverse, spread, shares_far, shares_other, embed, embed_other)
    far_parts = [swap(part, cores * (k + 1)) for k, part in enumerate(far_parts)]

    grad_other = pl.pallas_call(
        functools.partial(other_grad_kernel, dims),
        out_shape=shape((passage_rows, depth), bf16),
        in_specs=[VMEM] * (2 + blocks),
        out_specs=VMEM,
        scratch_shapes=[pltpu.VMEM((all_rows, depth), bf16)],
        compiler_params=params(32),
        cost_estimate=forward_cost(passages, all_rows),
        name="passage_grad_other",
    )(weights, shares_other, *queries)
    grad_other = swap(grad_other, 1)

    own_part, grad_own, pre_t, hidden_t = pl.pallas_call(
        functools.partial(own_grad_kernel, dims),
        out_shape=(
            shape((depth, rows), f32),
            shape((passage_rows, depth), f32),
            shape((depth, rows), f32),
            shape((width, rows), bf16),
        ),
        in_specs=[VMEM] * (8 + blocks),
        out_specs=(VMEM,) * 4,
        scratch_shapes=[pltpu.VMEM((far_rows, depth), bf16)],
        compiler_params=params(32),
        cost_estimate=forward_cost(pair, all_rows),
        name="own_grads",
    )(
        weights,
        shares_near,
        shares_far,
        shares_other,
        embed,
        embed_other,
        query_pre,
        query_flat,
        *queries,
    )

    passage_back, weight = pl.pallas_call(
        functools.partial(passage_back_kernel, dims),
        out_shape=(shape((passage_rows, depth), bf16), shape((width, depth), f32)),
        in_specs=[VMEM] * 4,
        out_specs=(VMEM,) * 2,
        scratch_shapes=[pltpu.VMEM((depth, width), f32)],
        compiler_params=params(32),
        cost_estimate=cost(2 * passage_rows * width * depth, passage_rows * width * 2),
        name="passage_back",
    )(grad_own, grad_other, passage_pre, passage_flat)

    parts = [*far_parts, own_part]
    query_back, weight = pl.pallas_call(
        query_back_kernel,
        out_shape=(shape((depth, rows), bf16), shape((width, depth), bf16)),
        in_specs=[VMEM] * (3 + blocks),
        out_specs=(VMEM, VMEM),
        compiler_params=params(16),
        cost_estimate=cost(2 * rows * width * depth, width * depth * 6 + rows * width * 2),
        name="query_back",
    )(pre_t, hidden_t, weight, *parts)

    weight = weight.reshape(devices, width // devices, depth)
    weight = lax.all_to_all(weight, axes, 0, 0, tiled=True)
    grad_passage = dot(passage_back, projection, 1, 1).astype(bf16).reshape(passage_hidden.shape)
    weight, grad_passage = lax.optimization_barrier((weight, grad_passage))
    copies = pl.pallas_call(
        sum_kernel,
        out_shape=shape(weight.shape, bf16),
        in_specs=[VMEM],
        out_specs=VMEM,
        compiler_params=params(16),
        name="sum_parts",
    )(weight)
    copies = lax.all_to_all(copies, axes, 0, 0, tiled=True)
    grad_proj = copies.reshape(width, depth).astype(f32)

    grad_query = dot(query_back, projection, 0, 1).astype(bf16).reshape(query_hidden.shape)
    own = lax.axis_index("group") // cores * count
    return (lax.dynamic_slice(losses[0], (own,), (count,)), grad_proj, grad_query, grad_passage)


def solution(mesh):
    in_specs = (
        P(axes, None, None),
        P(axes, None, None),
        P(),
        P(axes),
        P(axes, None),
        P(axes),
    )
    out_specs = (P(axes), P(), P(axes, None, None), P(axes, None, None))
    return jax.shard_map(local, mesh=mesh, in_specs=in_specs, out_specs=out_specs, check_vma=False)
```

time: 56.2 us -> 55 us (0.979)
  starting transfers between devices: 10.1 us -> 9.45 us
    ppermute x6 -> x4, starting transfers between devices: 5.11 us -> 4.1 us  [swap(): return lax.ppermute(value, 'group', [(i, i ^ k) for i in range(groups)])]
    pallas_call x3 -> x6, Pallas kernels: 6.24 us -> 5.64 us  [the longest x1 1.46 us: local(): pl.pallas_call(functools.partial(passage_back_kernel, dims), out_shape=(s...]
    ppermute x6 -> x4, waiting for transfers between devices: 1.28 us -> 1.16 us  [swap(): return lax.ppermute(value, 'group', [(i, i ^ k) for i in range(groups)])]
  transfers between devices with their start and end apart: 8 -> 6, of which waited for: 4 -> 5; matrix products, arithmetic and copies ran while one was open for 8% -> 8% of each run, Pallas kernels for 11% -> 9%
where the time goes in v6:
time: 55 us; the launch traced here: 54.7 us
  waiting for transfers between devices  15.4 us (28%)
  blocking collectives  12.9 us (23%)
  Pallas kernels  11.2 us (20%)
  starting transfers between devices  9.45 us (17%)
  matrix products  3.69 us (7%)
  other arithmetic  0.78 us (1%)
  between operations  0.77 us (1%)
  local copies, waits for them, and re-layouts  0.6 us (1%)
    all_to_all x1, blocking collectives, local(): packets = lax.all_to_all(packets, axes, 0, 0, tiled=True)  12.9 us
    all_to_all x1, waiting for transfers between devices, local(): copies = lax.all_to_all(copies, axes, 0, 0, tiled=True)  7.53 us
    all_to_all x1, waiting for transfers between devices, local(): weight = lax.all_to_all(weight, axes, 0, 0, tiled=True)  6.7 us
    ppermute x4, starting transfers between devices, swap(): return lax.ppermute(value, 'group', [(i, i ^ k) for i in range(groups)])  4.1 us
    dot_general x2, matrix products, dot(): lax.dot_general(left, right, (((left_dim,), (right_dim,)), ((), ())), pre...  3.69 us
    all_to_all x1, starting transfers between devices, local(): weight = lax.all_to_all(weight, axes, 0, 0, tiled=True)  3.03 us
    all_to_all x1, starting transfers between devices, local(): copies = lax.all_to_all(copies, axes, 0, 0, tiled=True)  2.32 us
    pallas_call x1, Pallas kernels, local(): pl.pallas_call(query_kernel, out_shape=(shape((rows, depth), f32), shape(...  1.63 us
  transfers between devices with their start and end apart: 6, of which 5 were waited for; matrix products, arithmetic and copies ran while one was open for 8% of the time, Pallas kernels for 9%

profile of v6, /device:TPU:1, one launch (start us, length us, event | category | flops | bytes accessed | tf_op | source)
XLA Modules:
  0.0 54.7 jit_solution(3585209802796958655)
XLA Ops:
  0.6 1.6 %query_embed.1 = (f32[256,128]{1,0:T(8,128)S(1)}, bf16[272,128]{1,0:T(8,128)(2,1)S(1)}, bf16[768,128]{1,0:T(8,128)(2,1)S(1)}, s32[16,128]{1,0:T(8,128)S(1)}) custom-call(bf16[256,768]{1,0:T(8,128)(2,1)} %bitcast.16, bf16[768,128]{1,0:T(8,128)(2,1)} %projection_hbm.1, s32[8,32]{1,0:T(8,128)} %ids_hbm.1, s32[8]{0:T(128)} %positive_hbm.1, s32[16]{0:T(128)} %lens_hbm.1), custom_call_target="tpu_custom_call" | custom-call | flops 20000000000 | bytes 393216 | tf_op jit(solution)/shard_map/query_embed/pallas_call | solution.py:426
  2.3 2.1 %collective-permute-start = (bf16[272,128]{1,0:T(8,128)(2,1)S(1)}, bf16[272,128]{1,0:T(8,128)(2,1)S(1)}, u32[]{:S(2)}, u32[]{:S(2)}) collective-permute-start(bf16[272,128]{1,0:T(8,128)(2,1)S(1)} %get-tuple-element.33.refs_0_), channel_id=1, source_target_pairs={{0,16},{8,24},{16,0},{24,8},{1,17},{9,25},{17,1},{25,9},{2,18},{10... | collective-permute-start | bytes 208904 | tf_op jit(solution)/shard_map/ppermute | solution.py:449
  4.4 1.2 %passage_embed.1 = (f32[2048,128]{1,0:T(8,128)S(1)}, bf16[2064,128]{1,0:T(8,128)(2,1)S(1)}, bf16[512,128]{1,0:T(8,128)(2,1)S(1)}, bf16[128,512]{1,0:T(8,128)(2,1)S(1)}) custom-call(s32[16,128]{1,0:T(8,128)S(1)} %get-tuple-element.34.lens, bf16[2048,768]{1,0:T(8,128)(2,1)S(1)} %bitcast.14, bf16[768,128]{1,0:T(8,128)(2,1)S(1)} %get-tuple-element.35.projection), custom_call_target="tpu_custom_call" | custom-call | flops 402653184 | bytes 4718592 | tf_op jit(solution)/shard_map/passage_embed/pallas_call | solution.py:453
  5.6 1.0 %collective-permute-start.1 = (bf16[2064,128]{1,0:T(8,128)(2,1)S(1)}, bf16[2064,128]{1,0:T(8,128)(2,1)S(1)}, u32[]{:S(2)}, u32[]{:S(2)}) collective-permute-start(bf16[2064,128]{1,0:T(8,128)(2,1)S(1)} %get-tuple-element.36.embed), channel_id=1, source_target_pairs={{0,8},{8,0},{16,24},{24,16},{1,9},{9,1},{17,25},{25,17},{2,10},{10... | collective-permute-start | bytes 1585160 | tf_op jit(solution)/shard_map/ppermute | solution.py:449
  6.6 0.6 %forward_near.1 = (bf16[2048,256]{1,0:T(8,128)(2,1)S(1)}, f32[16,256]{1,0:T(8,128)S(1)}) custom-call(bf16[2064,128]{1,0:T(8,128)(2,1)S(1)} %get-tuple-element.36.embed, bf16[272,128]{1,0:T(8,128)(2,1)S(1)} %get-tuple-element.33.refs_0_), custom_call_target="tpu_custom_call" | custom-call | flops 134217728 | bytes 1048576 | tf_op jit(solution)/shard_map/forward_near/pallas_call | solution.py:475
  7.2 0.6 %forward_far.1 = (bf16[2048,256]{1,0:T(8,128)(2,1)S(1)}, f32[16,256]{1,0:T(8,128)S(1)}) custom-call(bf16[2064,128]{1,0:T(8,128)(2,1)S(1)} %get-tuple-element.36.embed, bf16[272,128]{1,0:T(8,128)(2,1)S(1)} %collective-permute-done.refs_0_.refs_1_), custom_call_target="tpu_custom_call" | custom-call | flops 10000000000 | bytes 1000000 | tf_op jit(solution)/shard_map/forward_far/pallas_call | solution.py:475
  8.1 1.3 %forward_other.1 = (bf16[2048,512]{1,0:T(8,128)(2,1)S(1)}, f32[32,512]{1,0:T(8,128)S(1)}, f32[96,128]{1,0:T(8,128)S(1)}, f32[32,1,128]{2,1,0:T(1,128)S(1)}) custom-call(bf16[272,128]{1,0:T(8,128)(2,1)S(1)} %get-tuple-element.33.refs_0_, bf16[272,128]{1,0:T(8,128)(2,1)S(1)} %collective-permute-done.refs_0_.refs_1_, ...), custom_call_target="tpu_custom_call" | custom-call | flops 268435456 | bytes 2097152 | tf_op jit(solution)/shard_map/forward_other/pallas_call | solution.py:487
  9.5 12.9 %all_to_all.15.packets = f32[32,1,128]{2,1,0:T(1,128)S(1)} all-to-all(f32[32,1,128]{2,1,0:T(1,128)S(1)} %get-tuple-element.40), channel_id=1, replica_groups=mesh['group'=4,'dp'=8] {'dp','group'}, dimensions={0} | all-to-all | bytes 32768 | tf_op jit(solution)/shard_map/all_to_all | solution.py:506
  22.3 0.8 %query_grad_far.1 = (bf16[128,256]{1,0:T(8,128)(2,1)S(1)}, bf16[32,1,512]{2,1,0:T(2,128)(2,1)S(1)}, f32[8,128]{1,0:T(8,128)S(1)}) custom-call(f32[32,1,128]{2,1,0:T(1,128)S(1)} %all_to_all.15.packets, f32[96,128]{1,0:T(8,128)S(1)} %get-tuple-element.41.stats, f32[32,512]{1,0:T(8,128)S(1)} %get-tuple-element.42.inverse, ...), custom_call_target="tpu_custom_call" | custom-call | flops 268435456 | bytes 2097152 | tf_op jit(solution)/shard_map/query_grad_far/pallas_call | solution.py:508
  23.2 0.7 %passage_grad_other.1 = bf16[2048,128]{1,0:T(8,128)(2,1)S(1)} custom-call(bf16[32,1,512]{2,1,0:T(2,128)(2,1)S(1)} %get-tuple-element.47.weights, bf16[2048,512]{1,0:T(8,128)(2,1)S(1)} %get-tuple-element.45.shares_other, bf16[272,128]{1,0:T(8,128)(2,1)S(1)} %get-tuple-element.33.refs_0_, bf16[272,128]{1,0:T(8,128)(2,1)S(1)} %collective-permute-done.refs_0_.refs_1_), custom_call_target="tpu_custom_call" | custom-call | flops 268435456 | bytes 2097152 | tf_op jit(solution)/shard_map/passage_grad_other/pallas_call | solution.py:524
  23.9 0.7 %collective-permute-start.2 = (bf16[2048,128]{1,0:T(8,128)(2,1)S(1)}, bf16[2048,128]{1,0:T(8,128)(2,1)S(1)}, u32[]{:S(2)}, u32[]{:S(2)}) collective-permute-start(bf16[2048,128]{1,0:T(8,128)(2,1)S(1)} %passage_grad_other.1), channel_id=1, source_target_pairs={{0,8},{8,0},{16,24},{24,16},{1,9},{9,1},{17,25},{25,17},{2,10},{10... | collective-permute-start | bytes 1572872 | tf_op jit(solution)/shard_map/ppermute | solution.py:449
  24.9 1.0 %own_grads.1 = (f32[128,256]{1,0:T(8,128)S(1)}, f32[2048,128]{1,0:T(8,128)S(1)}, f32[128,256]{1,0:T(8,128)S(1)}, bf16[768,256]{1,0:T(8,128)(2,1)S(1)}) custom-call(bf16[32,1,512]{2,1,0:T(2,128)(2,1)S(1)} %get-tuple-element.47.weights, bf16[2048,256]{1,0:T(8,128)(2,1)S(1)} %get-tuple-element.48.shares_near, ...), custom_call_target="tpu_custom_call" | custom-call | flops 536870912 | bytes 4194304 | tf_op jit(solution)/shard_map/own_grads/pallas_call | solution.py:536
  26.1 1.5 %passage_back.1 = (bf16[2048,128]{1,0:T(8,128)(2,1)S(1)}, f32[768,128]{1,0:T(8,128)S(1)}) custom-call(f32[2048,128]{1,0:T(8,128)S(1)} %get-tuple-element.52.grad, bf16[2048,128]{1,0:T(8,128)(2,1)S(1)} %collective-permute-done.2.grad_other, f32[2048,128]{1,0:T(8,128)S(1)} %get-tuple-element.53.pre, bf16[2048,768]{1,0:T(8,128)(2,1)S(1)} %bitcast.15), custom_call_target="tpu_custom_call" | custom-call | flops 402653184 | bytes 3145728 | tf_op jit(solution)/shard_map/passage_back/pallas_call | solution.py:562
  27.6 0.7 %collective-permute-done.3.refs_0_ = bf16[128,256]{1,0:T(8,128)(2,1)S(1)} collective-permute-done((bf16[128,256]{1,0:T(8,128)(2,1)S(1)}, bf16[128,256]{1,0:T(8,128)(2,1)S(1)}, u32[]{:S(2)}, u32[]{:S(2)}) %collective-permute-start.3) | collective-permute-done | bytes 65568 | tf_op jit(solution)/shard_map/ppermute | solution.py:449
  28.3 1.0 %query_back.1 = (bf16[128,256]{1,0:T(8,128)(2,1)S(1)}, bf16[768,128]{1,0:T(8,128)(2,1)}) custom-call(f32[128,256]{1,0:T(8,128)S(1)} %get-tuple-element.50.pre, bf16[768,256]{1,0:T(8,128)(2,1)S(1)} %get-tuple-element.51.hidden, f32[768,128]{1,0:T(8,128)S(1)} %get-tuple-element.54.weight, bf16[128,256]{1,0:T(8,128)(2,1)S(1)} %collective-permute-done.3.refs_0_, ...), custom_call_target="tpu_custom_call" | custom-call | flops 50331648 | bytes 983040 | tf_op jit(solution)/shard_map/query_back/pallas_call | solution.py:574
  29.3 3.0 %all-to-all-start.1 = ((bf16[32,24,128]{2,1,0:T(8,128)(2,1)}), bf16[32,24,128]{2,1,0:T(8,128)(2,1)S(1)}, u32[]{:S(2)}, u32[]{:S(2)}) async-start(bf16[32,24,128]{2,1,0:T(8,128)(2,1)} %bitcast.3), calls=%async_computation.1 | async-start | bytes 393216 | tf_op jit(solution)/shard_map/all_to_all | solution.py:585
  32.3 2.7 %convolution_convert_fusion = bf16[2048,768]{1,0:T(8,128)(2,1)} fusion(bf16[2048,128]{1,0:T(8,128)(2,1)S(1)} %get-tuple-element.58, bf16[768,128]{1,0:T(8,128)(2,1)S(1)} %copy-done.2), kind=kOutput, calls=%fused_computation | convolution fusion | flops 404226048 | bytes 3866624 | tf_op jit(solution)/shard_map/dot_general | solution.py:21
  35.0 6.7 %all-to-all-done.1.parts = bf16[32,24,128]{2,1,0:T(8,128)(2,1)S(1)} async-done(((bf16[32,24,128]{2,1,0:T(8,128)(2,1)}), bf16[32,24,128]{2,1,0:T(8,128)(2,1)S(1)}, u32[]{:S(2)}, u32[]{:S(2)}) %all-to-all-start.1) | async-done | bytes 196640 | tf_op jit(solution)/shard_map/all_to_all | solution.py:585
  41.7 0.7 %sum_parts.1 = bf16[32,24,128]{2,1,0:T(8,128)(2,1)} custom-call(bf16[32,24,128]{2,1,0:T(8,128)(2,1)S(1)} %all-to-all-done.1.parts), custom_call_target="tpu_custom_call" | custom-call | tf_op jit(solution)/shard_map/sum_parts/pallas_call | solution.py:588
  42.4 2.3 %all-to-all-start.2 = ((bf16[32,24,128]{2,1,0:T(8,128)(2,1)}), bf16[32,24,128]{2,1,0:T(8,128)(2,1)S(1)}, u32[]{:S(2)}, u32[]{:S(2)}) async-start(bf16[32,24,128]{2,1,0:T(8,128)(2,1)} %sum_parts.1), calls=%async_computation.2 | async-start | bytes 393216 | tf_op jit(solution)/shard_map/all_to_all | solution.py:596
  44.8 0.6 %dynamic-slice_bitcast_fusion = f32[8]{0:T(128)} fusion(f32[1,128]{1,0:T(1,128)S(1)} %slice.3, s32[]{:T(128)S(6)} %select_n.9), kind=kLoop, calls=%fused_computation.3 | loop fusion | bytes 68 | tf_op jit(solution)/shard_map/dynamic_slice | solution.py:601
  45.3 1.0 %convolution_convert_fusion.1 = bf16[256,768]{1,0:T(8,128)(2,1)} fusion(bf16[128,256]{1,0:T(8,128)(2,1)S(1)} %get-tuple-element.60, bf16[768,128]{1,0:T(8,128)(2,1)S(1)} %copy-done.2), kind=kOutput, calls=%fused_computation.1 | convolution fusion | flops 50528256 | bytes 655360 | tf_op jit(solution)/shard_map/dot_general | solution.py:21
  46.4 7.5 %all-to-all-done.2 = bf16[32,24,128]{2,1,0:T(8,128)(2,1)S(1)} async-done(((bf16[32,24,128]{2,1,0:T(8,128)(2,1)}), bf16[32,24,128]{2,1,0:T(8,128)(2,1)S(1)}, u32[]{:S(2)}, u32[]{:S(2)}) %all-to-all-start.2) | async-done | bytes 196640 | tf_op jit(solution)/shard_map/all_to_all | solution.py:596
  53.9 0.8 %bitcast_convert_fusion = f32[768,128]{1,0:T(8,128)} fusion(bf16[32,24,128]{2,1,0:T(8,128)(2,1)S(1)} %all-to-all-done.2), kind=kLoop, calls=%fused_computation.2 | loop fusion | flops 98304 | bytes 589824 | tf_op jit(solution)/shard_map/convert_element_type | solution.py:597
  (11 shorter events, 0.8 us)
Async XLA Ops:
  0.6 3.8 %copy-start = (bf16[16,128,768]{2,1,0:T(8,128)(2,1)S(1)}, bf16[16,128,768]{2,1,0:T(8,128)(2,1)}, u32[]{:S(2)}) copy-start(bf16[16,128,768]{2,1,0:T(8,128)(2,1)} %param.7) | copy-start | bytes 9437188
  2.3 4.9 %collective-permute-start = (bf16[272,128]{1,0:T(8,128)(2,1)S(1)}, bf16[272,128]{1,0:T(8,128)(2,1)S(1)}, u32[]{:S(2)}, u32[]{:S(2)}) collective-permute-start(bf16[272,128]{1,0:T(8,128)(2,1)S(1)} %get-tuple-element.33.refs_0_), channel_id=1, source_target_pairs={{0,16},{8,24},{16,0},{24,8},{1,17},{9,25},{17,1},{25,9},{2,18},{10... | collective-permute-start | bytes 208904 | tf_op jit(solution)/shard_map/ppermute | solution.py:449
  5.6 2.6 %collective-permute-start.1 = (bf16[2064,128]{1,0:T(8,128)(2,1)S(1)}, bf16[2064,128]{1,0:T(8,128)(2,1)S(1)}, u32[]{:S(2)}, u32[]{:S(2)}) collective-permute-start(bf16[2064,128]{1,0:T(8,128)(2,1)S(1)} %get-tuple-element.36.embed), channel_id=1, source_target_pairs={{0,8},{8,0},{16,24},{24,16},{1,9},{9,1},{17,25},{25,17},{2,10},{10... | collective-permute-start | bytes 1585160 | tf_op jit(solution)/shard_map/ppermute | solution.py:449
  22.3 2.5 %copy-start.1 = (bf16[8,32,768]{2,1,0:T(8,128)(2,1)S(1)}, bf16[8,32,768]{2,1,0:T(8,128)(2,1)}, u32[]{:S(2)}) copy-start(bf16[8,32,768]{2,1,0:T(8,128)(2,1)} %param.6) | copy-start | bytes 1179652
  23.9 2.2 %collective-permute-start.2 = (bf16[2048,128]{1,0:T(8,128)(2,1)S(1)}, bf16[2048,128]{1,0:T(8,128)(2,1)S(1)}, u32[]{:S(2)}, u32[]{:S(2)}) collective-permute-start(bf16[2048,128]{1,0:T(8,128)(2,1)S(1)} %passage_grad_other.1), channel_id=1, source_target_pairs={{0,8},{8,0},{16,24},{24,16},{1,9},{9,1},{17,25},{25,17},{2,10},{10... | collective-permute-start | bytes 1572872 | tf_op jit(solution)/shard_map/ppermute | solution.py:449
  24.6 3.7 %collective-permute-start.3 = (bf16[128,256]{1,0:T(8,128)(2,1)S(1)}, bf16[128,256]{1,0:T(8,128)(2,1)S(1)}, u32[]{:S(2)}, u32[]{:S(2)}) collective-permute-start(bf16[128,256]{1,0:T(8,128)(2,1)S(1)} %get-tuple-element.55), channel_id=1, source_target_pairs={{0,16},{8,24},{16,0},{24,8},{1,17},{9,25},{17,1},{25,9},{2,18},{10... | collective-permute-start | bytes 196616 | tf_op jit(solution)/shard_map/ppermute | solution.py:449
  26.1 6.2 %copy-start.2 = (bf16[768,128]{1,0:T(8,128)(2,1)S(1)}, bf16[768,128]{1,0:T(8,128)(2,1)}, u32[]{:S(2)}) copy-start(bf16[768,128]{1,0:T(8,128)(2,1)} %projection_hbm.1) | copy-start | bytes 589828
  29.3 12.4 %all-to-all-start.1 = ((bf16[32,24,128]{2,1,0:T(8,128)(2,1)}), bf16[32,24,128]{2,1,0:T(8,128)(2,1)S(1)}, u32[]{:S(2)}, u32[]{:S(2)}) async-start(bf16[32,24,128]{2,1,0:T(8,128)(2,1)} %bitcast.3), calls=%async_computation.1 | async-start | bytes 393216 | tf_op jit(solution)/shard_map/all_to_all | solution.py:585
  42.4 11.5 %all-to-all-start.2 = ((bf16[32,24,128]{2,1,0:T(8,128)(2,1)}), bf16[32,24,128]{2,1,0:T(8,128)(2,1)S(1)}, u32[]{:S(2)}, u32[]{:S(2)}) async-start(bf16[32,24,128]{2,1,0:T(8,128)(2,1)} %sum_parts.1), calls=%async_computation.2 | async-start | bytes 393216 | tf_op jit(solution)/shard_map/all_to_all | solution.py:596

commit v7 on v6

--- a/solution.py
+++ b/solution.py
@@ -239,18 +239,6 @@
     return jnp.concatenate(parts, axis=0)
 
 
-def query_grads(dims, sources, weights, running):
-    blocks, count, length, passages, tokens, slots, step = dims
-    for k, (embed, shares, columns, first) in enumerate(sources):
-        for at in range(passages // step):
-            part = embed[at * step * tokens : (at + 1) * step * tokens, :].T
-            terms = dot(part, coefficients(dims, shares, columns, weights, first, at), 1, 0)
-            if k == 0 and at == 0:
-                running[...] = terms
-            else:
-                running[...] += terms
-
-
 class Columns:
     def __init__(self, ref, columns):
         self.ref, self.columns = ref, columns
@@ -272,8 +260,9 @@
     *refs,
 ):
     blocks, count, length, passages, tokens, slots, step = dims
+    packed, refs = refs[:blocks], refs[blocks:]
     parts_out = refs[: blocks - 1]
-    weights, losses_out, running = refs[blocks - 1 :]
+    weights, losses_out, grad_out, running, all_queries = refs[blocks - 1 :]
     rows = count * length
     pair = cores * passages
     width = stats.shape[1]
@@ -293,9 +282,11 @@
         plain, hard, kept, sums = pool[0:1, :], pool[1:2, :], pool[2:3, :], every[3:4, 0:1]
     hard_mean = sums * (1.0 / (devices * count * slots))
     partition = jnp.where(iota(plain.shape, 1) < queries, plain + hard / hard_mean, 1.0)
-    losses_out[...] = jnp.broadcast_to(
+    losses = jnp.broadcast_to(
         jnp.log(partition) - (kept - center * length), losses_out.shape
     )
+    chip = lax.axis_index("group") // cores
+    losses_out[...] = pltpu.roll(losses, width - chip * count, 1)
     grown = stats[:pair, :]
     boosted = stats[pair : 2 * pair, :]
     chosen = stats[2 * pair :, :]
@@ -303,28 +294,22 @@
     found = (exact_dot(grad, spread[...]) * inverse[...]).astype(bf16)
     for p in range(pair):
         weights[p] = found[p : p + 1, :]
-    columns = slice(rows, blocks * rows)
-    sources = [
-        (embed, shares_far, columns, 0),
-        (embed_other, Columns(shares_other, columns), columns, passages),
-    ]
-    query_grads(dims, sources, weights, running)
+    for k in range(blocks):
+        all_queries[k * rows : (k + 1) * rows, :] = packed[k][:rows, :]
+    everything, far = slice(0, blocks * rows), slice(rows, blocks * rows)
+    for at in range(passages // step):
+        part = slice(at * step * tokens, (at + 1) * step * tokens)
+        other = coefficients(dims, shares_other, everything, weights, passages, at)
+        own = coefficients(dims, shares_far, far, weights, 0, at)
+        terms = dot(embed_other[part, :].T, other[:, rows:], 1, 0)
+        terms += dot(embed[part, :].T, own, 1, 0)
+        if at == 0:
+            running[...] = terms
+        else:
+            running[...] += terms
+        grad_out[part, :] = dot(other, all_queries[...], 1, 0).astype(bf16)
     for k, out in enumerate(parts_out):
         out[...] = running[:, k * rows : (k + 1) * rows].astype(bf16)
-
-
-def other_grad_kernel(dims, weights, shares_other, *refs):
-    blocks, count, length, passages, tokens, slots, step = dims
-    packed = refs[:blocks]
-    grad_out, queries = refs[blocks:]
-    rows = count * length
-    for k in range(blocks):
-        queries[k * rows : (k + 1) * rows, :] = packed[k][:rows, :]
-    columns = slice(0, blocks * rows)
-    for at in range(passages // step):
-        coefficient = coefficients(dims, shares_other, columns, weights, passages, at)
-        grad = dot(coefficient, queries[...], 1, 0)
-        grad_out[at * step * tokens : (at + 1) * step * tokens, :] = grad.astype(bf16)
 
 
 def own_grad_kernel(
@@ -362,19 +347,38 @@
     hidden_out[...] = query_hidden[...].T
 
 
-def passage_back_kernel(dims, grad, grad_other, pre, hidden, back_out, weight_out, running):
+def passage_back_kernel(
+    dims,
+    grad,
+    grad_other,
+    pre,
+    hidden,
+    projection,
+    weight_out,
+    grad_hidden_hbm,
+    running,
+    grad_hidden,
+    sems,
+):
     blocks, count, length, passages, tokens, slots, step = dims
+    copies = []
     for at in range(passages // step):
         part = slice(at * step * tokens, (at + 1) * step * tokens)
         total = grad[part, :] + grad_other[part, :].astype(f32)
         back = normalize_back(pre[part, :], total).astype(bf16)
-        back_out[part, :] = back
+        grad_hidden[part, :] = dot(back, projection[...], 1, 1).astype(bf16)
+        rows = pl.ds(at * step * tokens, step * tokens)
+        copy = pltpu.make_async_copy(grad_hidden.at[rows], grad_hidden_hbm.at[rows], sems.at[at])
+        copy.start()
+        copies.append(copy)
         terms = dot(back.T, hidden[part, :], 1, 0)
         if at == 0:
             running[...] = terms
         else:
             running[...] += terms
     weight_out[...] = running[...].T
+    for copy in copies:
+        copy.wait()
 
 
 def normalize_back_columns(projected, grad):
@@ -400,6 +404,12 @@
     total = total.astype(bf16)
     for k in range(devices):
         copies_out[k] = total
+
+
+def final_kernel(copies, back, projection, losses, grad_proj_out, grad_query_out, losses_out):
+    grad_proj_out[...] = copies[...].astype(f32)
+    grad_query_out[...] = dot(back[...].T, projection[...], 1, 1).astype(bf16)
+    losses_out[...] = losses[0, : losses_out.shape[0]]
 
 
 def local(query_hidden, passage_hidden, projection, positive, hard_ids, passage_len):
@@ -505,33 +515,26 @@
 
     packets = lax.all_to_all(packets, axes, 0, 0, tiled=True)
 
-    *far_parts, weights, losses = pl.pallas_call(
+    *far_parts, weights, losses, grad_other = pl.pallas_call(
         functools.partial(far_grad_kernel, dims),
         out_shape=(
             *[shape((depth, rows), bf16)] * (blocks - 1),
             shape((pair, 1, all_rows), bf16),
             shape((8, pool_width), f32),
+            shape((passage_rows, depth), bf16),
         ),
-        in_specs=[VMEM] * 8,
-        out_specs=(VMEM,) * (blocks + 1),
-        scratch_shapes=[pltpu.VMEM((depth, far_rows), f32)],
+        in_specs=[VMEM] * (8 + blocks),
+        out_specs=(VMEM,) * (blocks + 2),
+        scratch_shapes=[
+            pltpu.VMEM((depth, far_rows), f32),
+            pltpu.VMEM((all_rows, depth), bf16),
+        ],
         compiler_params=params(32),
-        cost_estimate=forward_cost(pair, far_rows),
-        name="query_grad_far",
-    )(packets, stats, inverse, spread, shares_far, shares_other, embed, embed_other)
+        cost_estimate=forward_cost(pair, all_rows),
+        name="far_grads",
+    )(packets, stats, inverse, spread, shares_far, shares_other, embed, embed_other, *queries)
+    grad_other = swap(grad_other, 1)
     far_parts = [swap(part, cores * (k + 1)) for k, part in enumerate(far_parts)]
-
-    grad_other = pl.pallas_call(
-        functools.partial(other_grad_kernel, dims),
-        out_shape=shape((passage_rows, depth), bf16),
-        in_specs=[VMEM] * (2 + blocks),
-        out_specs=VMEM,
-        scratch_shapes=[pltpu.VMEM((all_rows, depth), bf16)],
-        compiler_params=params(32),
-        cost_estimate=forward_cost(passages, all_rows),
-        name="passage_grad_other",
-    )(weights, shares_other, *queries)
-    grad_other = swap(grad_other, 1)
 
     own_part, grad_own, pre_t, hidden_t = pl.pallas_call(
         functools.partial(own_grad_kernel, dims),
@@ -559,16 +562,20 @@
         *queries,
     )
 
-    passage_back, weight = pl.pallas_call(
+    weight, grad_passage = pl.pallas_call(
         functools.partial(passage_back_kernel, dims),
-        out_shape=(shape((passage_rows, depth), bf16), shape((width, depth), f32)),
-        in_specs=[VMEM] * 4,
-        out_specs=(VMEM,) * 2,
-        scratch_shapes=[pltpu.VMEM((depth, width), f32)],
+        out_shape=(shape((width, depth), f32), shape((passage_rows, width), bf16)),
+        in_specs=[VMEM] * 5,
+        out_specs=(VMEM, HBM),
+        scratch_shapes=[
+            pltpu.VMEM((depth, width), f32),
+            pltpu.VMEM((passage_rows, width), bf16),
+            pltpu.SemaphoreType.DMA((passages // step,)),
+        ],
         compiler_params=params(32),
-        cost_estimate=cost(2 * passage_rows * width * depth, passage_rows * width * 2),
+        cost_estimate=cost(4 * passage_rows * width * depth, passage_rows * width * 4),
         name="passage_back",
-    )(grad_own, grad_other, passage_pre, passage_flat)
+    )(grad_own, grad_other, passage_pre, passage_flat, projection_near)
 
     parts = [*far_parts, own_part]
     query_back, weight = pl.pallas_call(
@@ -583,8 +590,6 @@
 
     weight = weight.reshape(devices, width // devices, depth)
     weight = lax.all_to_all(weight, axes, 0, 0, tiled=True)
-    grad_passage = dot(passage_back, projection, 1, 1).astype(bf16).reshape(passage_hidden.shape)
-    weight, grad_passage = lax.optimization_barrier((weight, grad_passage))
     copies = pl.pallas_call(
         sum_kernel,
         out_shape=shape(weight.shape, bf16),
@@ -594,11 +599,21 @@
         name="sum_parts",
     )(weight)
     copies = lax.all_to_all(copies, axes, 0, 0, tiled=True)
-    grad_proj = copies.reshape(width, depth).astype(f32)
-
-    grad_query = dot(query_back, projection, 0, 1).astype(bf16).reshape(query_hidden.shape)
-    own = lax.axis_index("group") // cores * count
-    return (lax.dynamic_slice(losses[0], (own,), (count,)), grad_proj, grad_query, grad_passage)
+    grad_proj, grad_query, losses = pl.pallas_call(
+        final_kernel,
+        out_shape=(shape((width, depth), f32), shape((rows, width), bf16), shape((count,), f32)),
+        in_specs=[VMEM] * 4,
+        out_specs=(VMEM,) * 3,
+        compiler_params=params(16),
+        cost_estimate=cost(2 * rows * width * depth, rows * width * 4),
+        name="outputs",
+    )(copies.reshape(width, depth), query_back, projection_near, losses)
+    return (
+        losses,
+        grad_proj,
+        grad_query.reshape(query_hidden.shape),
+        grad_passage.reshape(passage_hidden.shape),
+    )
 
 
 def solution(mesh):

time: 55 us -> 52.6 us (0.956)
  blocking collectives: 12.9 us -> 35.4 us
  waiting for transfers between devices: 15.4 us -> 0.5 us
  starting transfers between devices: 9.45 us -> 4.1 us
  matrix products: 3.69 us -> 0 us
  other arithmetic: 0.78 us -> 0 us
  local copies, waits for them, and re-layouts: 0.6 us -> 0.01 us
    all_to_all x0 -> x2, blocking collectives: none -> 22.6 us  [the longest x1 11.3 us: local(): copies = lax.all_to_all(copies, axes, 0, 0, tiled=True)]
    all_to_all x2 -> x0, waiting for transfers between devices: 14.2 us -> none  [the longest x1 7.53 us: local(): copies = lax.all_to_all(copies, axes, 0, 0, tiled=True)]
    all_to_all x2 -> x0, starting transfers between devices: 5.35 us -> none  [the longest x1 3.03 us: local(): weight = lax.all_to_all(weight, axes, 0, 0, tiled=True)]
    dot_general x2 -> x0, matrix products: 3.69 us -> none  [dot(): lax.dot_general(left, right, (((left_dim,), (right_dim,)), ((), ())), pre...]
    pallas_call x1, Pallas kernels: 1.46 us -> 2.38 us  [local(): pl.pallas_call(functools.partial(passage_back_kernel, dims), out_shape=(s...]
    convert_element_type x1 -> x0, other arithmetic: 0.78 us -> none  [local(): grad_proj = copies.reshape(width, depth).astype(f32)]
    pallas_call x1, Pallas kernels: 1 us -> 0.31 us  [local(): pl.pallas_call(query_back_kernel, out_shape=(shape((depth, rows), bf16),...]
    pallas_call x1, Pallas kernels: 0.73 us -> 0.05 us  [local(): pl.pallas_call(sum_kernel, out_shape=shape(weight.shape, bf16), in_specs=...]
  transfers between devices with their start and end apart: 6 -> 4, of which waited for: 5 -> 2; matrix products, arithmetic and copies ran while one was open for 8% -> 0% of each run, Pallas kernels for 9% -> 11%
where the time goes in v7:
time: 52.6 us; the launch traced here: 52.4 us
  blocking collectives  35.4 us (67%)
  Pallas kernels  11.6 us (22%)
  starting transfers between devices  4.1 us (8%)
  between operations  0.73 us (1%)
    all_to_all x1, blocking collectives, local(): packets = lax.all_to_all(packets, axes, 0, 0, tiled=True)  12.9 us
    all_to_all x1, blocking collectives, local(): copies = lax.all_to_all(copies, axes, 0, 0, tiled=True)  11.3 us
    all_to_all x1, blocking collectives, local(): weight = lax.all_to_all(weight, axes, 0, 0, tiled=True)  11.3 us
    ppermute x4, starting transfers between devices, swap(): return lax.ppermute(value, 'group', [(i, i ^ k) for i in range(groups)])  4.1 us
    pallas_call x1, Pallas kernels, local(): pl.pallas_call(functools.partial(passage_back_kernel, dims), out_shape=(s...  2.38 us
    pallas_call x1, Pallas kernels, local(): pl.pallas_call(query_kernel, out_shape=(shape((rows, depth), f32), shape(...  1.62 us
    pallas_call x1, Pallas kernels, local(): pl.pallas_call(functools.partial(far_grad_kernel, dims), out_shape=(*[sha...  1.36 us
    pallas_call x1, Pallas kernels, local(): pl.pallas_call(functools.partial(far_kernel, dims), out_shape=(shape((pas...  1.35 us
  transfers between devices with their start and end apart: 4, of which 2 were waited for; matrix products, arithmetic and copies ran while one was open for 0% of the time, Pallas kernels for 11%

profile of v7, /device:TPU:1, one launch (start us, length us, event | category | flops | bytes accessed | tf_op | source)
XLA Modules:
  0.0 52.4 jit_solution(12734170067209698694)
XLA Ops:
  0.6 0.0 copy-start
  0.6 1.6 %query_embed.1 = (f32[256,128]{1,0:T(8,128)S(1)}, bf16[272,128]{1,0:T(8,128)(2,1)S(1)}, bf16[768,128]{1,0:T(8,128)(2,1)S(1)}, s32[16,128]{1,0:T(8,128)S(1)}) custom-call(bf16[256,768]{1,0:T(8,128)(2,1)} %bitcast.9, bf16[768,128]{1,0:T(8,128)(2,1)} %projection_hbm.1, s32[8,32]{1,0:T(8,128)} %ids_hbm.1, s32[8]{0:T(128)} %positive_hbm.1, s32[16]{0:T(128)} %lens_hbm.1), custom_call_target="tpu_custom_call" | custom-call | flops 20000000000 | bytes 393216 | tf_op jit(solution)/shard_map/query_embed/pallas_call | solution.py:436
  2.3 2.1 %collective-permute-start = (bf16[272,128]{1,0:T(8,128)(2,1)S(1)}, bf16[272,128]{1,0:T(8,128)(2,1)S(1)}, u32[]{:S(2)}, u32[]{:S(2)}) collective-permute-start(bf16[272,128]{1,0:T(8,128)(2,1)S(1)} %get-tuple-element.35.refs_0_), channel_id=1, source_target_pairs={{0,16},{8,24},{16,0},{24,8},{1,17},{9,25},{17,1},{25,9},{2,18},{10... | collective-permute-start | bytes 208904 | tf_op jit(solution)/shard_map/ppermute | solution.py:459
  4.4 0.0 copy-done
  4.4 1.2 %passage_embed.1 = (f32[2048,128]{1,0:T(8,128)S(1)}, bf16[2064,128]{1,0:T(8,128)(2,1)S(1)}, bf16[512,128]{1,0:T(8,128)(2,1)S(1)}, bf16[128,512]{1,0:T(8,128)(2,1)S(1)}) custom-call(s32[16,128]{1,0:T(8,128)S(1)} %get-tuple-element.36.lens, bf16[2048,768]{1,0:T(8,128)(2,1)S(1)} %bitcast.6, bf16[768,128]{1,0:T(8,128)(2,1)S(1)} %get-tuple-element.37.projection), custom_call_target="tpu_custom_call" | custom-call | flops 402653184 | bytes 4718592 | tf_op jit(solution)/shard_map/passage_embed/pallas_call | solution.py:463
  5.6 1.0 %collective-permute-start.1 = (bf16[2064,128]{1,0:T(8,128)(2,1)S(1)}, bf16[2064,128]{1,0:T(8,128)(2,1)S(1)}, u32[]{:S(2)}, u32[]{:S(2)}) collective-permute-start(bf16[2064,128]{1,0:T(8,128)(2,1)S(1)} %get-tuple-element.38.embed), channel_id=1, source_target_pairs={{0,8},{8,0},{16,24},{24,16},{1,9},{9,1},{17,25},{25,17},{2,10},{10... | collective-permute-start | bytes 1585160 | tf_op jit(solution)/shard_map/ppermute | solution.py:459
  6.6 0.6 %forward_near.1 = (bf16[2048,256]{1,0:T(8,128)(2,1)S(1)}, f32[16,256]{1,0:T(8,128)S(1)}) custom-call(bf16[2064,128]{1,0:T(8,128)(2,1)S(1)} %get-tuple-element.38.embed, bf16[272,128]{1,0:T(8,128)(2,1)S(1)} %get-tuple-element.35.refs_0_), custom_call_target="tpu_custom_call" | custom-call | flops 134217728 | bytes 1048576 | tf_op jit(solution)/shard_map/forward_near/pallas_call | solution.py:485
  7.2 0.0 collective-permute-done.refs_0_.refs_1_
  7.2 0.6 %forward_far.1 = (bf16[2048,256]{1,0:T(8,128)(2,1)S(1)}, f32[16,256]{1,0:T(8,128)S(1)}) custom-call(bf16[2064,128]{1,0:T(8,128)(2,1)S(1)} %get-tuple-element.38.embed, bf16[272,128]{1,0:T(8,128)(2,1)S(1)} %collective-permute-done.refs_0_.refs_1_), custom_call_target="tpu_custom_call" | custom-call | flops 10000000000 | bytes 1000000 | tf_op jit(solution)/shard_map/forward_far/pallas_call | solution.py:485
  7.9 0.2 collective-permute-done.1.refs_2_.embed_other
  8.1 1.3 %forward_other.1 = (bf16[2048,512]{1,0:T(8,128)(2,1)S(1)}, f32[32,512]{1,0:T(8,128)S(1)}, f32[96,128]{1,0:T(8,128)S(1)}, f32[32,1,128]{2,1,0:T(1,128)S(1)}) custom-call(bf16[272,128]{1,0:T(8,128)(2,1)S(1)} %get-tuple-element.35.refs_0_, bf16[272,128]{1,0:T(8,128)(2,1)S(1)} %collective-permute-done.refs_0_.refs_1_, ...), custom_call_target="tpu_custom_call" | custom-call | flops 268435456 | bytes 2097152 | tf_op jit(solution)/shard_map/forward_other/pallas_call | solution.py:497
  9.5 12.9 %all_to_all.15.packets = f32[32,1,128]{2,1,0:T(1,128)S(1)} all-to-all(f32[32,1,128]{2,1,0:T(1,128)S(1)} %get-tuple-element.42), channel_id=1, replica_groups=mesh['group'=4,'dp'=8] {'dp','group'}, dimensions={0} | all-to-all | bytes 32768 | tf_op jit(solution)/shard_map/all_to_all | solution.py:516
  22.3 1.4 %far_grads.1 = (bf16[128,256]{1,0:T(8,128)(2,1)S(1)}, bf16[32,1,512]{2,1,0:T(2,128)(2,1)S(1)}, f32[8,128]{1,0:T(8,128)S(1)}, bf16[2048,128]{1,0:T(8,128)(2,1)S(1)}) custom-call(f32[32,1,128]{2,1,0:T(1,128)S(1)} %all_to_all.15.packets, f32[96,128]{1,0:T(8,128)S(1)} %get-tuple-element.43.stats, f32[32,512]{1,0:T(8,128)S(1)} %get-tuple-element.44.inverse, ...), custom_call_target="tpu_custom_call" | custom-call | flops 536870912 | bytes 4194304 | tf_op jit(solution)/shard_map/far_grads/pallas_call | solution.py:518
  23.7 0.7 %collective-permute-start.2 = (bf16[2048,128]{1,0:T(8,128)(2,1)S(1)}, bf16[2048,128]{1,0:T(8,128)(2,1)S(1)}, u32[]{:S(2)}, u32[]{:S(2)}) collective-permute-start(bf16[2048,128]{1,0:T(8,128)(2,1)S(1)} %get-tuple-element.54), channel_id=1, source_target_pairs={{0,8},{8,0},{16,24},{24,16},{1,9},{9,1},{17,25},{25,17},{2,10},{10... | collective-permute-start | bytes 1572872 | tf_op jit(solution)/shard_map/ppermute | solution.py:459
  24.4 0.3 collective-permute-start.3
  24.7 0.0 copy-done.1
  24.7 1.0 %own_grads.1 = (f32[128,256]{1,0:T(8,128)S(1)}, f32[2048,128]{1,0:T(8,128)S(1)}, f32[128,256]{1,0:T(8,128)S(1)}, bf16[768,256]{1,0:T(8,128)(2,1)S(1)}) custom-call(bf16[32,1,512]{2,1,0:T(2,128)(2,1)S(1)} %get-tuple-element.48.weights, bf16[2048,256]{1,0:T(8,128)(2,1)S(1)} %get-tuple-element.49.shares_near, ...), custom_call_target="tpu_custom_call" | custom-call | flops 536870912 | bytes 4194304 | tf_op jit(solution)/shard_map/own_grads/pallas_call | solution.py:539
  25.7 0.2 collective-permute-done.2.grad_other
  25.9 2.4 %passage_back.1 = (f32[768,128]{1,0:T(8,128)S(1)}, bf16[2048,768]{1,0:T(8,128)(2,1)}) custom-call(f32[2048,128]{1,0:T(8,128)S(1)} %get-tuple-element.53.grad, bf16[2048,128]{1,0:T(8,128)(2,1)S(1)} %collective-permute-done.2.grad_other, f32[2048,128]{1,0:T(8,128)S(1)} %get-tuple-element.55.pre, bf16[2048,768]{1,0:T(8,128)(2,1)S(1)} %bitcast.7, ...), custom_call_target="tpu_custom_call" | custom-call | flops 805306368 | bytes 6291456 | tf_op jit(solution)/shard_map/passage_back/pallas_call | solution.py:565
  28.3 0.0 collective-permute-done.3.refs_0_
  28.3 0.3 query_back.1
  28.7 11.3 %all_to_all.16.parts = bf16[32,24,128]{2,1,0:T(8,128)(2,1)S(1)} all-to-all(bf16[32,24,128]{2,1,0:T(8,128)(2,1)S(1)} %bitcast.11), channel_id=1, replica_groups=mesh['group'=4,'dp'=8] {'dp','group'}, dimensions={0} | all-to-all | bytes 393216 | tf_op jit(solution)/shard_map/all_to_all | solution.py:592
  40.0 11.3 %all_to_all.17 = bf16[32,24,128]{2,1,0:T(8,128)(2,1)S(1)} all-to-all(bf16[32,24,128]{2,1,0:T(8,128)(2,1)S(1)} %sum_parts.1), channel_id=1, replica_groups=mesh['group'=4,'dp'=8] {'dp','group'}, dimensions={0} | all-to-all | bytes 393216 | tf_op jit(solution)/shard_map/all_to_all | solution.py:601
  51.3 1.1 %outputs.1 = (f32[768,128]{1,0:T(8,128)}, bf16[256,768]{1,0:T(8,128)(2,1)}, f32[8]{0:T(128)}) custom-call(bf16[768,128]{1,0:T(8,128)(2,1)S(1)} %bitcast.8, bf16[128,256]{1,0:T(8,128)(2,1)S(1)} %get-tuple-element.60.back, bf16[768,128]{1,0:T(8,128)(2,1)S(1)} %get-tuple-element.37.projection, f32[8,128]{1,0:T(8,128)S(1)} %get-tuple-element.61.losses), custom_call_target="tpu_custom_call" | custom-call | flops 50331648 | bytes 786432 | tf_op jit(solution)/shard_map/outputs/pallas_call | solution.py:602
  (2 shorter events, 0.1 us)
Async XLA Ops:
  0.6 3.8 %copy-start = (bf16[16,128,768]{2,1,0:T(8,128)(2,1)S(1)}, bf16[16,128,768]{2,1,0:T(8,128)(2,1)}, u32[]{:S(2)}) copy-start(bf16[16,128,768]{2,1,0:T(8,128)(2,1)} %param.7) | copy-start | bytes 9437188
  2.3 4.9 %collective-permute-start = (bf16[272,128]{1,0:T(8,128)(2,1)S(1)}, bf16[272,128]{1,0:T(8,128)(2,1)S(1)}, u32[]{:S(2)}, u32[]{:S(2)}) collective-permute-start(bf16[272,128]{1,0:T(8,128)(2,1)S(1)} %get-tuple-element.35.refs_0_), channel_id=1, source_target_pairs={{0,16},{8,24},{16,0},{24,8},{1,17},{9,25},{17,1},{25,9},{2,18},{10... | collective-permute-start | bytes 208904 | tf_op jit(solution)/shard_map/ppermute | solution.py:459
  5.6 2.6 %collective-permute-start.1 = (bf16[2064,128]{1,0:T(8,128)(2,1)S(1)}, bf16[2064,128]{1,0:T(8,128)(2,1)S(1)}, u32[]{:S(2)}, u32[]{:S(2)}) collective-permute-start(bf16[2064,128]{1,0:T(8,128)(2,1)S(1)} %get-tuple-element.38.embed), channel_id=1, source_target_pairs={{0,8},{8,0},{16,24},{24,16},{1,9},{9,1},{17,25},{25,17},{2,10},{10... | collective-permute-start | bytes 1585160 | tf_op jit(solution)/shard_map/ppermute | solution.py:459
  8.1 16.6 %copy-start.1 = (bf16[8,32,768]{2,1,0:T(8,128)(2,1)S(1)}, bf16[8,32,768]{2,1,0:T(8,128)(2,1)}, u32[]{:S(2)}) copy-start(bf16[8,32,768]{2,1,0:T(8,128)(2,1)} %param.6) | copy-start | bytes 1179652
  23.7 2.2 %collective-permute-start.2 = (bf16[2048,128]{1,0:T(8,128)(2,1)S(1)}, bf16[2048,128]{1,0:T(8,128)(2,1)S(1)}, u32[]{:S(2)}, u32[]{:S(2)}) collective-permute-start(bf16[2048,128]{1,0:T(8,128)(2,1)S(1)} %get-tuple-element.54), channel_id=1, source_target_pairs={{0,8},{8,0},{16,24},{24,16},{1,9},{9,1},{17,25},{25,17},{2,10},{10... | collective-permute-start | bytes 1572872 | tf_op jit(solution)/shard_map/ppermute | solution.py:459
  24.4 3.9 %collective-permute-start.3 = (bf16[128,256]{1,0:T(8,128)(2,1)S(1)}, bf16[128,256]{1,0:T(8,128)(2,1)S(1)}, u32[]{:S(2)}, u32[]{:S(2)}) collective-permute-start(bf16[128,256]{1,0:T(8,128)(2,1)S(1)} %get-tuple-element.57), channel_id=1, source_target_pairs={{0,16},{8,24},{16,0},{24,8},{1,17},{9,25},{17,1},{25,9},{2,18},{10... | collective-permute-start | bytes 196616 | tf_op jit(solution)/shard_map/ppermute | solution.py:459

commit v8 on v7

--- a/solution.py
+++ b/solution.py
@@ -68,15 +68,12 @@
     projection_hbm,
     ids_hbm,
     positive_hbm,
-    lens_hbm,
     pre_out,
     packed_out,
     projection,
-    lens_out,
     hidden,
     hard_ids,
     positive,
-    lens,
     sems,
 ):
     copies = [
@@ -87,7 +84,6 @@
                 (hidden_hbm, hidden),
                 (ids_hbm, hard_ids),
                 (positive_hbm, positive),
-                (lens_hbm, lens),
             ]
         )
     ]
@@ -109,8 +105,6 @@
     extra = packed_out.shape[0] - rows
     marks = jnp.concatenate([marks, jnp.full((extra - count, lanes), -1.0, f32)], axis=0)
     packed_out[rows:, :] = marks.astype(bf16)
-    for p in range(lens_out.shape[0]):
-        lens_out[p : p + 1, :] = jnp.full((1, lanes), lens[p], jnp.int32)
     for copy in copies[:2]:
         copy.wait()
     pre = dot(hidden[...], projection[...], 1, 0)
@@ -135,16 +129,17 @@
     return jnp.where(owner == query, 1.0, 0.0).astype(bf16)
 
 
-def passage_kernel(dims, lens, hidden, projection, pre_out, embed_out, gather_out, spread_out):
+def passage_kernel(dims, lens, hidden, projection, pre_out, embed_out):
     blocks, count, length, passages, tokens, slots, step = dims
     for start in range(0, hidden.shape[0], step * tokens):
         part = slice(start, start + step * tokens)
         pre = dot(hidden[part, :], projection[...], 1, 0)
         pre_out[part, :] = pre
         embed_out[part, :] = normalize(pre).astype(bf16)
-    embed_out[hidden.shape[0] :, :] = lens[...].astype(f32).astype(bf16)
-    gather_out[...] = token_picks(dims, gather_out.shape[1], True)
-    spread_out[...] = token_picks(dims, gather_out.shape[1], False)
+    row = jnp.broadcast_to(lens[...].astype(f32).reshape(1, passages), (passages, passages))
+    own = iota(row.shape, 0) == iota(row.shape, 1)
+    column = jnp.sum(jnp.where(own, row, 0.0), axis=1, keepdims=True)
+    embed_out[hidden.shape[0] :, :] = jnp.broadcast_to(column, (passages, lanes)).astype(bf16)
 
 
 def forward_part(dims, embed, queries, shares_out, summed, first):
@@ -168,46 +163,46 @@
                 )
 
 
-def forward_kernel(dims, embed, *refs):
-    forward_part(dims, embed, refs[:-2], refs[-2], refs[-1], 0)
+def near_kernel(dims, embed, packed, shares_out, summed_out, gather_out, spread_out):
+    forward_part(dims, embed, [packed], shares_out, summed_out, 0)
+    gather_out[...] = token_picks(dims, gather_out.shape[1], True)
+    spread_out[...] = token_picks(dims, gather_out.shape[1], False)
+
+
+def other_kernel(dims, embed, packed, shares_out, summed_out):
+    forward_part(dims, embed, [packed], shares_out, summed_out, 0)
 
 
 def far_kernel(dims, *refs):
     blocks, count, length, passages, tokens, slots, step = dims
     packed = refs[:blocks]
-    embed_other, summed_near, summed_far, gather, *refs = refs[blocks:]
-    shares_other, inverse_out, stats_out, packet_out, summed, marks = refs
+    embed, embed_other, summed_near, summed_other, gather, *refs = refs[blocks:]
+    shares_far, shares_other, inverse_out, stats_out, packet_out, summed, summed_far, marks = refs
     rows = count * length
     me = lax.axis_index("group")
     marks[...] = jnp.full(marks.shape, -1.0, f32)
     for k in range(blocks):
         start = pl.multiple_of(jnp.bitwise_xor(me // cores, k) * count, count)
         marks[pl.ds(start, count), :] = packed[k][rows:, :].astype(f32)[:count]
-    forward_part(dims, embed_other, packed, shares_other, summed, passages)
+    forward_part(dims, embed, packed[1:], shares_far, summed_far, 0)
+    forward_part(dims, embed_other, packed[1:], shares_other, summed_far, passages)
     summed[:passages, :rows] = summed_near[...]
-    summed[:passages, rows:] = summed_far[...]
+    summed[passages:, :rows] = summed_other[...]
+    summed[:, rows:] = summed_far[...]
     total = summed[...]
     inverse_out[...] = 1.0 / total
     width = marks.shape[0]
     scores = exact_dot(smooth_temp * jnp.log(total), gather[...])
     marks_t = marks[...].T
-    ids = marks_t[:slots, :]
     pair = cores * passages
-    first = [me * passages, jnp.bitwise_xor(me, 1) * passages]
-    counts = jnp.concatenate(
-        [
-            jnp.sum(
-                jnp.where(ids == (first[p // passages] + p % passages).astype(f32), 1.0, 0.0),
-                axis=0,
-                keepdims=True,
-            )
-            for p in range(pair)
-        ],
-        axis=0,
-    )
     row = iota((pair, width), 0)
-    here = jnp.where(row < passages, row + first[0], row - passages + first[1])
-    chosen = here.astype(f32) == marks_t[slots : slots + 1, :]
+    other = jnp.bitwise_xor(me, 1)
+    here = jnp.where(row < passages, row + me * passages, row + (other - 1) * passages)
+    here = here.astype(f32)
+    chosen = here == marks_t[slots : slots + 1, :]
+    counts = jnp.zeros((pair, width), f32)
+    for k in range(slots):
+        counts += jnp.where(here == marks_t[k : k + 1, :], 1.0, 0.0)
     grown = jnp.exp(scores - center * length)
     boost = blocks * pair / slots
     boosted = jnp.where(chosen, 0.0, boost * counts)
@@ -235,16 +230,10 @@
     passages, tokens, _, step = dims[3:]
     parts = []
     for p in range(at * step, (at + 1) * step):
-        parts.append(shares[p * tokens : (p + 1) * tokens, :] * weights[first + p, :, columns])
+        weight = weights[first + p : first + p + 1, columns]
+        weight = jnp.broadcast_to(weight, (tokens, weight.shape[1])).astype(bf16)
+        parts.append(shares[p * tokens : (p + 1) * tokens, :] * weight)
     return jnp.concatenate(parts, axis=0)
-
-
-class Columns:
-    def __init__(self, ref, columns):
-        self.ref, self.columns = ref, columns
-
-    def __getitem__(self, index):
-        return self.ref[index[0], self.columns]
 
 
 def far_grad_kernel(
@@ -254,7 +243,8 @@
     inverse,
     spread,
     shares_far,
-    shares_other,
+    shares_other_near,
+    shares_other_far,
     embed,
     embed_other,
     *refs,
@@ -262,7 +252,7 @@
     blocks, count, length, passages, tokens, slots, step = dims
     packed, refs = refs[:blocks], refs[blocks:]
     parts_out = refs[: blocks - 1]
-    weights, losses_out, grad_out, running, all_queries = refs[blocks - 1 :]
+    weights, losses_out, grad_out, running, far_queries = refs[blocks - 1 :]
     rows = count * length
     pair = cores * passages
     width = stats.shape[1]
@@ -291,23 +281,23 @@
     boosted = stats[pair : 2 * pair, :]
     chosen = stats[2 * pair :, :]
     grad = grown * (1.0 + boosted * grown / hard_mean) / partition - chosen
-    found = (exact_dot(grad, spread[...]) * inverse[...]).astype(bf16)
-    for p in range(pair):
-        weights[p] = found[p : p + 1, :]
-    for k in range(blocks):
-        all_queries[k * rows : (k + 1) * rows, :] = packed[k][:rows, :]
-    everything, far = slice(0, blocks * rows), slice(rows, blocks * rows)
+    found = exact_dot(grad, spread[...]) * inverse[...]
+    weights[...] = found
+    for k in range(1, blocks):
+        far_queries[(k - 1) * rows : k * rows, :] = packed[k][:rows, :]
+    near, far = slice(0, rows), slice(rows, blocks * rows)
     for at in range(passages // step):
         part = slice(at * step * tokens, (at + 1) * step * tokens)
-        other = coefficients(dims, shares_other, everything, weights, passages, at)
         own = coefficients(dims, shares_far, far, weights, 0, at)
-        terms = dot(embed_other[part, :].T, other[:, rows:], 1, 0)
-        terms += dot(embed[part, :].T, own, 1, 0)
+        other_near = coefficients(dims, shares_other_near, near, weights, passages, at)
+        other_far = coefficients(dims, shares_other_far, far, weights, passages, at)
+        terms = dot(embed[part, :].T, own, 1, 0) + dot(embed_other[part, :].T, other_far, 1, 0)
         if at == 0:
             running[...] = terms
         else:
             running[...] += terms
-        grad_out[part, :] = dot(other, all_queries[...], 1, 0).astype(bf16)
+        grad = dot(other_near, packed[0][:rows, :], 1, 0) + dot(other_far, far_queries[...], 1, 0)
+        grad_out[part, :] = grad.astype(bf16)
     for k, out in enumerate(parts_out):
         out[...] = running[:, k * rows : (k + 1) * rows].astype(bf16)
 
@@ -334,7 +324,7 @@
     for at in range(passages // step):
         part = slice(at * step * tokens, (at + 1) * step * tokens)
         near = coefficients(dims, shares_near, own, weights, 0, at)
-        other = coefficients(dims, Columns(shares_other, own), own, weights, passages, at)
+        other = coefficients(dims, shares_other, own, weights, passages, at)
         terms = dot(embed[part, :].T, near, 1, 0) + dot(embed_other[part, :].T, other, 1, 0)
         if at == 0:
             part_out[...] = terms
@@ -433,85 +423,92 @@
     passage_flat = passage_hidden.reshape(passage_rows, width)
     shape = jax.ShapeDtypeStruct
 
-    query_pre, packed, projection_near, lens = pl.pallas_call(
+    query_pre, packed, projection_near = pl.pallas_call(
         query_kernel,
         out_shape=(
             shape((rows, depth), f32),
             shape((rows + 16, depth), bf16),
             shape((width, depth), bf16),
-            shape((passages, lanes), jnp.int32),
         ),
-        in_specs=[HBM] * 5,
-        out_specs=(VMEM,) * 4,
+        in_specs=[HBM] * 4,
+        out_specs=(VMEM,) * 3,
         scratch_shapes=[
             pltpu.VMEM((rows, width), bf16),
             pltpu.VMEM((count, slots), jnp.int32),
             pltpu.SMEM((count,), jnp.int32),
-            pltpu.SMEM((passages,), jnp.int32),
-            pltpu.SemaphoreType.DMA((5,)),
+            pltpu.SemaphoreType.DMA((4,)),
         ],
         compiler_params=params(16),
         cost_estimate=cost(2e10, rows * width * 2),
         name="query_embed",
-    )(*in_hbm(query_flat, projection, hard_ids, positive, passage_len))
+    )(*in_hbm(query_flat, projection, hard_ids, positive))
 
     def swap(value, k):
         return lax.ppermute(value, "group", [(i, i ^ k) for i in range(groups)])
 
     queries = [packed] + [swap(packed, cores * k) for k in range(1, blocks)]
 
-    passage_pre, embed, gather, spread = pl.pallas_call(
+    passage_pre, embed = pl.pallas_call(
         functools.partial(passage_kernel, dims),
         out_shape=(
             shape((passage_rows, depth), f32),
             shape((passage_rows + passages, depth), bf16),
+        ),
+        in_specs=[VMEM] * 3,
+        out_specs=(VMEM,) * 2,
+        compiler_params=params(16),
+        cost_estimate=cost(2 * passage_rows * width * depth, passage_rows * (width * 2 + depth * 6)),
+        name="passage_embed",
+    )(passage_len, passage_flat, projection_near)
+    embed_other = swap(embed, 1)
+
+    def forward_cost(passage_count, query_rows):
+        pairs = passage_count * tokens * query_rows
+        return cost(2 * pairs * depth, pairs * 2, pairs)
+
+    shares_near, summed_near, gather, spread = pl.pallas_call(
+        functools.partial(near_kernel, dims),
+        out_shape=(
+            shape((passage_rows, rows), bf16),
+            shape((passages, rows), f32),
             shape((all_rows, pool_width), bf16),
             shape((pool_width, all_rows), bf16),
         ),
-        in_specs=[VMEM] * 3,
+        in_specs=[VMEM] * 2,
         out_specs=(VMEM,) * 4,
         compiler_params=params(16),
-        cost_estimate=cost(2 * passage_rows * width * depth, passage_rows * (width * 2 + depth * 6)),
-        name="passage_embed",
-    )(lens, passage_flat, projection_near)
-    embed_other = swap(embed, 1)
-
-    def forward_cost(passage_count, query_rows):
-        pairs = passage_count * tokens * query_rows
-        return cost(2 * pairs * depth, pairs * 2, pairs)
-
-    def forward(name, blocks_of_queries, estimate):
-        query_rows = len(blocks_of_queries) * rows
-        return pl.pallas_call(
-            functools.partial(forward_kernel, dims),
-            out_shape=(shape((passage_rows, query_rows), bf16), shape((passages, query_rows), f32)),
-            in_specs=[VMEM] * (1 + len(blocks_of_queries)),
-            out_specs=(VMEM,) * 2,
-            compiler_params=params(16),
-            cost_estimate=estimate,
-            name=name,
-        )(embed, *blocks_of_queries)
-
-    shares_near, summed_near = forward("forward_near", queries[:1], forward_cost(passages, rows))
-    shares_far, summed_far = forward("forward_far", queries[1:], cost(1e10, 1e6))
-    shares_other, inverse, stats, packets = pl.pallas_call(
+        cost_estimate=cost(5e10, 1e6),
+        name="forward_near",
+    )(embed, packed)
+    shares_other_near, summed_other = pl.pallas_call(
+        functools.partial(other_kernel, dims),
+        out_shape=(shape((passage_rows, rows), bf16), shape((passages, rows), f32)),
+        in_specs=[VMEM] * 2,
+        out_specs=(VMEM,) * 2,
+        compiler_params=params(16),
+        cost_estimate=forward_cost(passages, rows),
+        name="forward_other",
+    )(embed_other, packed)
+    shares_far, shares_other_far, inverse, stats, packets = pl.pallas_call(
         functools.partial(far_kernel, dims),
         out_shape=(
-            shape((passage_rows, all_rows), bf16),
+            shape((passage_rows, far_rows), bf16),
+            shape((passage_rows, far_rows), bf16),
             shape((pair, all_rows), f32),
             shape((3 * pair, pool_width), f32),
             shape((devices, packet_rows, pool_width), f32),
         ),
-        in_specs=[VMEM] * (blocks + 4),
-        out_specs=(VMEM,) * 4,
+        in_specs=[VMEM] * (blocks + 5),
+        out_specs=(VMEM,) * 5,
         scratch_shapes=[
             pltpu.VMEM((pair, all_rows), f32),
+            pltpu.VMEM((pair, far_rows), f32),
             pltpu.VMEM((pool_width, lanes), f32),
         ],
         compiler_params=params(32),
-        cost_estimate=forward_cost(passages, all_rows),
-        name="forward_other",
-    )(*queries, embed_other, summed_near, summed_far, gather)
+        cost_estimate=forward_cost(pair, far_rows),
+        name="forward_far",
+    )(*queries, embed, embed_other, summed_near, summed_other, gather)
 
     packets = lax.all_to_all(packets, axes, 0, 0, tiled=True)
 
@@ -519,20 +516,31 @@
         functools.partial(far_grad_kernel, dims),
         out_shape=(
             *[shape((depth, rows), bf16)] * (blocks - 1),
-            shape((pair, 1, all_rows), bf16),
+            shape((pair, all_rows), f32),
             shape((8, pool_width), f32),
             shape((passage_rows, depth), bf16),
         ),
-        in_specs=[VMEM] * (8 + blocks),
+        in_specs=[VMEM] * (9 + blocks),
         out_specs=(VMEM,) * (blocks + 2),
         scratch_shapes=[
             pltpu.VMEM((depth, far_rows), f32),
-            pltpu.VMEM((all_rows, depth), bf16),
+            pltpu.VMEM((far_rows, depth), bf16),
         ],
         compiler_params=params(32),
         cost_estimate=forward_cost(pair, all_rows),
         name="far_grads",
-    )(packets, stats, inverse, spread, shares_far, shares_other, embed, embed_other, *queries)
+    )(
+        packets,
+        stats,
+        inverse,
+        spread,
+        shares_far,
+        shares_other_near,
+        shares_other_far,
+        embed,
+        embed_other,
+        *queries,
+    )
     grad_other = swap(grad_other, 1)
     far_parts = [swap(part, cores * (k + 1)) for k, part in enumerate(far_parts)]
 
@@ -554,7 +562,7 @@
         weights,
         shares_near,
         shares_far,
-        shares_other,
+        shares_other_near,
         embed,
         embed_other,
         query_pre,

time: 52.6 us -> 51.9 us (0.987)
  blocking collectives: 35.4 us -> 34.2 us
  waiting for transfers between devices: 0.5 us -> 1.05 us
    all_to_all x1, blocking collectives: 12.9 us -> 11.6 us  [local(): packets = lax.all_to_all(packets, axes, 0, 0, tiled=True)]
    ppermute x4, waiting for transfers between devices: 0.5 us -> 1.05 us  [swap(): return lax.ppermute(value, 'group', [(i, i ^ k) for i in range(groups)])]
where the time goes in v8:
time: 51.9 us; the launch traced here: 51.7 us
  blocking collectives  34.2 us (66%)
  Pallas kernels  11.7 us (23%)
  starting transfers between devices  4.09 us (8%)
  waiting for transfers between devices  1.05 us (2%)
  between operations  0.74 us (1%)
    all_to_all x1, blocking collectives, local(): packets = lax.all_to_all(packets, axes, 0, 0, tiled=True)  11.6 us
    all_to_all x1, blocking collectives, local(): copies = lax.all_to_all(copies, axes, 0, 0, tiled=True)  11.3 us
    all_to_all x1, blocking collectives, local(): weight = lax.all_to_all(weight, axes, 0, 0, tiled=True)  11.2 us
    ppermute x4, starting transfers between devices, swap(): return lax.ppermute(value, 'group', [(i, i ^ k) for i in range(groups)])  4.09 us
    pallas_call x1, Pallas kernels, local(): pl.pallas_call(functools.partial(passage_back_kernel, dims), out_shape=(s...  2.41 us
    pallas_call x1, Pallas kernels, local(): pl.pallas_call(query_kernel, out_shape=(shape((rows, depth), f32), shape(...  1.61 us
    pallas_call x1, Pallas kernels, local(): pl.pallas_call(functools.partial(far_kernel, dims), out_shape=(shape((pas...  1.4 us
    pallas_call x1, Pallas kernels, local(): pl.pallas_call(functools.partial(far_grad_kernel, dims), out_shape=(*[sha...  1.32 us
  transfers between devices with their start and end apart: 4, of which 2 were waited for; matrix products, arithmetic and copies ran while one was open for 0% of the time, Pallas kernels for 11%

profile of v8, /device:TPU:1, one launch (start us, length us, event | category | flops | bytes accessed | tf_op | source)
XLA Modules:
  0.0 51.7 jit_solution(9977721384903402604)
XLA Ops:
  0.7 1.6 %query_embed.1 = (f32[256,128]{1,0:T(8,128)S(1)}, bf16[272,128]{1,0:T(8,128)(2,1)S(1)}, bf16[768,128]{1,0:T(8,128)(2,1)S(1)}) custom-call(bf16[256,768]{1,0:T(8,128)(2,1)} %bitcast.9, bf16[768,128]{1,0:T(8,128)(2,1)} %projection_hbm.1, s32[8,32]{1,0:T(8,128)} %ids_hbm.1, s32[8]{0:T(128)} %positive_hbm.1), custom_call_target="tpu_custom_call" | custom-call | flops 20000000000 | bytes 393216 | tf_op jit(solution)/shard_map/query_embed/pallas_call | solution.py:426
  2.3 2.1 %collective-permute-start = (bf16[272,128]{1,0:T(8,128)(2,1)S(1)}, bf16[272,128]{1,0:T(8,128)(2,1)S(1)}, u32[]{:S(2)}, u32[]{:S(2)}) collective-permute-start(bf16[272,128]{1,0:T(8,128)(2,1)S(1)} %get-tuple-element.35.packed.refs_0_), channel_id=1, source_target_pairs={{0,16},{8,24},{16,0},{24,8},{1,17},{9,25},{17,1},{25,9},{2,18},{10... | collective-permute-start | bytes 208904 | tf_op jit(solution)/shard_map/ppermute | solution.py:447
  4.4 0.0 copy-done
  4.4 1.1 %passage_embed.1 = (f32[2048,128]{1,0:T(8,128)S(1)}, bf16[2064,128]{1,0:T(8,128)(2,1)S(1)}) custom-call(s32[16]{0:T(128)S(1)} %copy-done.2, bf16[2048,768]{1,0:T(8,128)(2,1)S(1)} %bitcast.6, bf16[768,128]{1,0:T(8,128)(2,1)S(1)} %get-tuple-element.36.projection), custom_call_target="tpu_custom_call" | custom-call | flops 402653184 | bytes 4718592 | tf_op jit(solution)/shard_map/passage_embed/pallas_call | solution.py:451
  5.5 1.0 %collective-permute-start.1 = (bf16[2064,128]{1,0:T(8,128)(2,1)S(1)}, bf16[2064,128]{1,0:T(8,128)(2,1)S(1)}, u32[]{:S(2)}, u32[]{:S(2)}) collective-permute-start(bf16[2064,128]{1,0:T(8,128)(2,1)S(1)} %get-tuple-element.37.embed.refs_2_), channel_id=1, source_target_pairs={{0,8},{8,0},{16,24},{24,16},{1,9},{9,1},{17,25},{25,17},{2,10},{10... | collective-permute-start | bytes 1585160 | tf_op jit(solution)/shard_map/ppermute | solution.py:447
  6.5 0.7 %forward_near.1 = (bf16[2048,256]{1,0:T(8,128)(2,1)S(1)}, f32[16,256]{1,0:T(8,128)S(1)}, bf16[512,128]{1,0:T(8,128)(2,1)S(1)}, bf16[128,512]{1,0:T(8,128)(2,1)S(1)}) custom-call(bf16[2064,128]{1,0:T(8,128)(2,1)S(1)} %get-tuple-element.37.embed.refs_2_, bf16[272,128]{1,0:T(8,128)(2,1)S(1)} %get-tuple-element.35.packed.refs_0_), custom_call_target="tpu_custom_call" | custom-call | flops 49999998976 | bytes 1000000 | tf_op jit(solution)/shard_map/forward_near/pallas_call | solution.py:469
  7.2 0.8 %collective-permute-done.1.embed.refs_3_.embed_other = bf16[2064,128]{1,0:T(8,128)(2,1)S(1)} collective-permute-done((bf16[2064,128]{1,0:T(8,128)(2,1)S(1)}, bf16[2064,128]{1,0:T(8,128)(2,1)S(1)}, u32[]{:S(2)}, u32[]{:S(2)}) %collective-permute-start.1) | collective-permute-done | bytes 528416 | tf_op jit(solution)/shard_map/ppermute | solution.py:447
  8.0 0.6 %forward_other.1 = (bf16[2048,256]{1,0:T(8,128)(2,1)S(1)}, f32[16,256]{1,0:T(8,128)S(1)}) custom-call(bf16[2064,128]{1,0:T(8,128)(2,1)S(1)} %collective-permute-done.1.embed.refs_3_.embed_other, bf16[272,128]{1,0:T(8,128)(2,1)S(1)} %get-tuple-element.35.packed.refs_0_), custom_call_target="tpu_custom_call" | custom-call | flops 134217728 | bytes 1048576 | tf_op jit(solution)/shard_map/forward_other/pallas_call | solution.py:483
  8.7 0.0 collective-permute-done.refs_1_
  8.7 0.0 copy-start.1
  8.7 1.4 %forward_far.1 = (bf16[2048,256]{1,0:T(8,128)(2,1)S(1)}, bf16[2048,256]{1,0:T(8,128)(2,1)S(1)}, f32[32,512]{1,0:T(8,128)S(1)}, f32[96,128]{1,0:T(8,128)S(1)}, f32[32,1,128]{2,1,0:T(1,128)S(1)}) custom-call(bf16[272,128]{1,0:T(8,128)(2,1)S(1)} %get-tuple-element.35.packed.refs_0_, bf16[272,128]{1,0:T(8,128)(2,1)S(1)} %collective-permute-done.refs_1_, ...), custom_call_target="tpu_custom_call" | custom-call | flops 268435456 | bytes 2097152 | tf_op jit(solution)/shard_map/forward_far/pallas_call | solution.py:492
  10.1 11.6 %all_to_all.15.packets = f32[32,1,128]{2,1,0:T(1,128)S(1)} all-to-all(f32[32,1,128]{2,1,0:T(1,128)S(1)} %get-tuple-element.41), channel_id=1, replica_groups=mesh['group'=4,'dp'=8] {'dp','group'}, dimensions={0} | all-to-all | bytes 32768 | tf_op jit(solution)/shard_map/all_to_all | solution.py:513
  21.7 1.3 %far_grads.1 = (bf16[128,256]{1,0:T(8,128)(2,1)S(1)}, f32[32,512]{1,0:T(8,128)S(1)}, f32[8,128]{1,0:T(8,128)S(1)}, bf16[2048,128]{1,0:T(8,128)(2,1)S(1)}) custom-call(f32[32,1,128]{2,1,0:T(1,128)S(1)} %all_to_all.15.packets, f32[96,128]{1,0:T(8,128)S(1)} %get-tuple-element.42.stats, f32[32,512]{1,0:T(8,128)S(1)} %get-tuple-element.43.inverse, ...), custom_call_target="tpu_custom_call" | custom-call | flops 536870912 | bytes 4194304 | tf_op jit(solution)/shard_map/far_grads/pallas_call | solution.py:515
  23.0 0.7 %collective-permute-start.2 = (bf16[2048,128]{1,0:T(8,128)(2,1)S(1)}, bf16[2048,128]{1,0:T(8,128)(2,1)S(1)}, u32[]{:S(2)}, u32[]{:S(2)}) collective-permute-start(bf16[2048,128]{1,0:T(8,128)(2,1)S(1)} %get-tuple-element.54), channel_id=1, source_target_pairs={{0,8},{8,0},{16,24},{24,16},{1,9},{9,1},{17,25},{25,17},{2,10},{10... | collective-permute-start | bytes 1572872 | tf_op jit(solution)/shard_map/ppermute | solution.py:447
  23.7 0.3 collective-permute-start.3
  24.0 0.0 copy-done.1
  24.0 1.0 %own_grads.1 = (f32[128,256]{1,0:T(8,128)S(1)}, f32[2048,128]{1,0:T(8,128)S(1)}, f32[128,256]{1,0:T(8,128)S(1)}, bf16[768,256]{1,0:T(8,128)(2,1)S(1)}) custom-call(f32[32,512]{1,0:T(8,128)S(1)} %get-tuple-element.48.weights, bf16[2048,256]{1,0:T(8,128)(2,1)S(1)} %get-tuple-element.49.shares_near, bf16[2048,256]{1,0:T(8,128)(2,1)S(1)} %get-tuple-element.45.shares_far, ...), custom_call_target="tpu_custom_call" | custom-call | flops 536870912 | bytes 4194304 | tf_op jit(solution)/shard_map/own_grads/pallas_call | solution.py:547
  25.0 0.2 collective-permute-done.2.grad_other
  25.3 2.4 %passage_back.1 = (f32[768,128]{1,0:T(8,128)S(1)}, bf16[2048,768]{1,0:T(8,128)(2,1)}) custom-call(f32[2048,128]{1,0:T(8,128)S(1)} %get-tuple-element.53.grad, bf16[2048,128]{1,0:T(8,128)(2,1)S(1)} %collective-permute-done.2.grad_other, f32[2048,128]{1,0:T(8,128)S(1)} %get-tuple-element.55.pre, bf16[2048,768]{1,0:T(8,128)(2,1)S(1)} %bitcast.7, ...), custom_call_target="tpu_custom_call" | custom-call | flops 805306368 | bytes 6291456 | tf_op jit(solution)/shard_map/passage_back/pallas_call | solution.py:573
  27.7 0.0 collective-permute-done.3.refs_0_
  27.7 0.3 query_back.1
  28.0 11.2 %all_to_all.16.parts = bf16[32,24,128]{2,1,0:T(8,128)(2,1)S(1)} all-to-all(bf16[32,24,128]{2,1,0:T(8,128)(2,1)S(1)} %bitcast.11), channel_id=1, replica_groups=mesh['group'=4,'dp'=8] {'dp','group'}, dimensions={0} | all-to-all | bytes 393216 | tf_op jit(solution)/shard_map/all_to_all | solution.py:600
  39.3 11.3 %all_to_all.17 = bf16[32,24,128]{2,1,0:T(8,128)(2,1)S(1)} all-to-all(bf16[32,24,128]{2,1,0:T(8,128)(2,1)S(1)} %sum_parts.1), channel_id=1, replica_groups=mesh['group'=4,'dp'=8] {'dp','group'}, dimensions={0} | all-to-all | bytes 393216 | tf_op jit(solution)/shard_map/all_to_all | solution.py:609
  50.6 1.1 %outputs.1 = (f32[768,128]{1,0:T(8,128)}, bf16[256,768]{1,0:T(8,128)(2,1)}, f32[8]{0:T(128)}) custom-call(bf16[768,128]{1,0:T(8,128)(2,1)S(1)} %bitcast.8, bf16[128,256]{1,0:T(8,128)(2,1)S(1)} %get-tuple-element.60.back, bf16[768,128]{1,0:T(8,128)(2,1)S(1)} %get-tuple-element.36.projection, f32[8,128]{1,0:T(8,128)S(1)} %get-tuple-element.61.losses), custom_call_target="tpu_custom_call" | custom-call | flops 50331648 | bytes 786432 | tf_op jit(solution)/shard_map/outputs/pallas_call | solution.py:610
  (4 shorter events, 0.1 us)
Async XLA Ops:
  0.6 3.8 %copy-start = (bf16[16,128,768]{2,1,0:T(8,128)(2,1)S(1)}, bf16[16,128,768]{2,1,0:T(8,128)(2,1)}, u32[]{:S(2)}) copy-start(bf16[16,128,768]{2,1,0:T(8,128)(2,1)} %param.7) | copy-start | bytes 9437188
  0.6 3.7 %copy-start.2 = (s32[16]{0:T(128)S(1)}, s32[16]{0:T(128)}, u32[]{:S(2)}) copy-start(s32[16]{0:T(128)} %lens.1) | copy-start | bytes 196
  2.3 6.4 %collective-permute-start = (bf16[272,128]{1,0:T(8,128)(2,1)S(1)}, bf16[272,128]{1,0:T(8,128)(2,1)S(1)}, u32[]{:S(2)}, u32[]{:S(2)}) collective-permute-start(bf16[272,128]{1,0:T(8,128)(2,1)S(1)} %get-tuple-element.35.packed.refs_0_), channel_id=1, source_target_pairs={{0,16},{8,24},{16,0},{24,8},{1,17},{9,25},{17,1},{25,9},{2,18},{10... | collective-permute-start | bytes 208904 | tf_op jit(solution)/shard_map/ppermute | solution.py:447
  5.5 2.6 %collective-permute-start.1 = (bf16[2064,128]{1,0:T(8,128)(2,1)S(1)}, bf16[2064,128]{1,0:T(8,128)(2,1)S(1)}, u32[]{:S(2)}, u32[]{:S(2)}) collective-permute-start(bf16[2064,128]{1,0:T(8,128)(2,1)S(1)} %get-tuple-element.37.embed.refs_2_), channel_id=1, source_target_pairs={{0,8},{8,0},{16,24},{24,16},{1,9},{9,1},{17,25},{25,17},{2,10},{10... | collective-permute-start | bytes 1585160 | tf_op jit(solution)/shard_map/ppermute | solution.py:447
  8.7 15.3 %copy-start.1 = (bf16[8,32,768]{2,1,0:T(8,128)(2,1)S(1)}, bf16[8,32,768]{2,1,0:T(8,128)(2,1)}, u32[]{:S(2)}) copy-start(bf16[8,32,768]{2,1,0:T(8,128)(2,1)} %param.6) | copy-start | bytes 1179652
  23.0 2.2 %collective-permute-start.2 = (bf16[2048,128]{1,0:T(8,128)(2,1)S(1)}, bf16[2048,128]{1,0:T(8,128)(2,1)S(1)}, u32[]{:S(2)}, u32[]{:S(2)}) collective-permute-start(bf16[2048,128]{1,0:T(8,128)(2,1)S(1)} %get-tuple-element.54), channel_id=1, source_target_pairs={{0,8},{8,0},{16,24},{24,16},{1,9},{9,1},{17,25},{25,17},{2,10},{10... | collective-permute-start | bytes 1572872 | tf_op jit(solution)/shard_map/ppermute | solution.py:447
  23.7 4.0 %collective-permute-start.3 = (bf16[128,256]{1,0:T(8,128)(2,1)S(1)}, bf16[128,256]{1,0:T(8,128)(2,1)S(1)}, u32[]{:S(2)}, u32[]{:S(2)}) collective-permute-start(bf16[128,256]{1,0:T(8,128)(2,1)S(1)} %get-tuple-element.57), channel_id=1, source_target_pairs={{0,16},{8,24},{16,0},{24,8},{1,17},{9,25},{17,1},{25,9},{2,18},{10... | collective-permute-start | bytes 196616 | tf_op jit(solution)/shard_map/ppermute | solution.py:447

commit v9 on v8

--- a/solution.py
+++ b/solution.py
@@ -12,6 +12,7 @@
 center = 0.375
 lanes = 128
 cores = 2
+padding = -30.0
 axes = ("dp", "group")
 f32 = jnp.float32
 bf16 = jnp.bfloat16
@@ -118,15 +119,15 @@
     return index // size
 
 
-def token_picks(dims, width, rows_first):
+def owners(dims, token):
+    chip = lax.axis_index("group") // cores
+    return jnp.bitwise_xor(parted(token, dims[2]), chip * dims[1])
+
+
+def token_picks(dims, width):
     blocks, count, length = dims[:3]
-    chip = lax.axis_index("group") // cores
-    tokens = blocks * count * length
-    shape = (tokens, width) if rows_first else (width, tokens)
-    token = iota(shape, 0 if rows_first else 1)
-    query = iota(shape, 1 if rows_first else 0)
-    owner = jnp.bitwise_xor(parted(token, length), chip * count)
-    return jnp.where(owner == query, 1.0, 0.0).astype(bf16)
+    shape = (blocks * count * length, width)
+    return jnp.where(owners(dims, iota(shape, 0)) == iota(shape, 1), 1.0, 0.0).astype(bf16)
 
 
 def passage_kernel(dims, lens, hidden, projection, pre_out, embed_out):
@@ -142,41 +143,50 @@
     embed_out[hidden.shape[0] :, :] = jnp.broadcast_to(column, (passages, lanes)).astype(bf16)
 
 
-def forward_part(dims, embed, queries, shares_out, summed, first):
+def fill_bias(dims, embed, bias_out):
+    passages, tokens = dims[3:5]
+    lens = embed[passages * tokens :, :].astype(f32).astype(jnp.int32)
+    for p in range(passages):
+        live = iota((tokens, lanes), 0) < lens[p : p + 1, :]
+        bias_out[p * tokens : (p + 1) * tokens, :] = jnp.where(live, 0.0, padding).astype(bf16)
+
+
+def forward_part(dims, embed, bias, queries, shares_out, summed, first):
     blocks, count, length, passages, tokens, slots, step = dims
     rows = count * length
-    lens = embed[passages * tokens :, :].astype(f32).astype(jnp.int32)
+    once = jnp.where(iota((rows, lanes), 1) == 0, 1.0, 0.0).astype(bf16)
     for at in range(passages // step):
-        part = embed[at * step * tokens : (at + 1) * step * tokens, :]
+        part = slice(at * step * tokens, (at + 1) * step * tokens)
+        left = jnp.concatenate([embed[part, :], bias[part, :]], axis=1)
         for k, block in enumerate(queries):
             columns = slice(k * rows, (k + 1) * rows)
-            similar = dot(part, block[:rows, :], 1, 1)
+            similar = dot(left, jnp.concatenate([block[:rows, :], once], axis=1), 1, 1)
             for p in range(step):
                 row = at * step + p
-                piece = similar[p * tokens : (p + 1) * tokens, :]
-                live = jnp.concatenate([lens[row : row + 1, :]] * (rows // lanes), axis=1)
-                grown = jnp.exp(piece * (1.0 / smooth_temp))
-                grown = jnp.where(iota(piece.shape, 0) < live, grown, 0.0)
+                grown = jnp.exp(similar[p * tokens : (p + 1) * tokens, :] * (1.0 / smooth_temp))
                 shares_out[row * tokens : (row + 1) * tokens, columns] = grown.astype(bf16)
                 summed[first + row : first + row + 1, columns] = jnp.sum(
                     grown, axis=0, keepdims=True
                 )
 
 
-def near_kernel(dims, embed, packed, shares_out, summed_out, gather_out, spread_out):
-    forward_part(dims, embed, [packed], shares_out, summed_out, 0)
-    gather_out[...] = token_picks(dims, gather_out.shape[1], True)
-    spread_out[...] = token_picks(dims, gather_out.shape[1], False)
-
-
-def other_kernel(dims, embed, packed, shares_out, summed_out):
-    forward_part(dims, embed, [packed], shares_out, summed_out, 0)
+def near_kernel(dims, embed, packed, shares_out, summed_out, turned_out, bias_out, gather_out):
+    fill_bias(dims, embed, bias_out)
+    forward_part(dims, embed, bias_out, [packed], shares_out, summed_out, 0)
+    turned_out[...] = embed[: turned_out.shape[1], :].T
+    gather_out[...] = token_picks(dims, gather_out.shape[1])
+
+
+def other_kernel(dims, embed, packed, shares_out, summed_out, turned_out, bias_out):
+    fill_bias(dims, embed, bias_out)
+    forward_part(dims, embed, bias_out, [packed], shares_out, summed_out, 0)
+    turned_out[...] = embed[: turned_out.shape[1], :].T
 
 
 def far_kernel(dims, *refs):
     blocks, count, length, passages, tokens, slots, step = dims
     packed = refs[:blocks]
-    embed, embed_other, summed_near, summed_other, gather, *refs = refs[blocks:]
+    embed, embed_other, bias, bias_other, summed_near, summed_other, gather, *refs = refs[blocks:]
     shares_far, shares_other, inverse_out, stats_out, packet_out, summed, summed_far, marks = refs
     rows = count * length
     me = lax.axis_index("group")
@@ -184,8 +194,8 @@
     for k in range(blocks):
         start = pl.multiple_of(jnp.bitwise_xor(me // cores, k) * count, count)
         marks[pl.ds(start, count), :] = packed[k][rows:, :].astype(f32)[:count]
-    forward_part(dims, embed, packed[1:], shares_far, summed_far, 0)
-    forward_part(dims, embed_other, packed[1:], shares_other, summed_far, passages)
+    forward_part(dims, embed, bias, packed[1:], shares_far, summed_far, 0)
+    forward_part(dims, embed_other, bias_other, packed[1:], shares_other, summed_far, passages)
     summed[:passages, :rows] = summed_near[...]
     summed[passages:, :rows] = summed_other[...]
     summed[:, rows:] = summed_far[...]
@@ -241,12 +251,11 @@
     packets,
     stats,
     inverse,
-    spread,
     shares_far,
     shares_other_near,
     shares_other_far,
-    embed,
-    embed_other,
+    embed_t,
+    embed_other_t,
     *refs,
 ):
     blocks, count, length, passages, tokens, slots, step = dims
@@ -281,7 +290,11 @@
     boosted = stats[pair : 2 * pair, :]
     chosen = stats[2 * pair :, :]
     grad = grown * (1.0 + boosted * grown / hard_mean) / partition - chosen
-    found = exact_dot(grad, spread[...]) * inverse[...]
+    spreaded = []
+    for start in range(0, blocks * rows, lanes):
+        owner = owners(dims, iota(grad.shape, 1) + start)
+        spreaded.append(jnp.take_along_axis(grad, owner, axis=1))
+    found = jnp.concatenate(spreaded, axis=1) * inverse[...]
     weights[...] = found
     for k in range(1, blocks):
         far_queries[(k - 1) * rows : k * rows, :] = packed[k][:rows, :]
@@ -291,7 +304,7 @@
         own = coefficients(dims, shares_far, far, weights, 0, at)
         other_near = coefficients(dims, shares_other_near, near, weights, passages, at)
         other_far = coefficients(dims, shares_other_far, far, weights, passages, at)
-        terms = dot(embed[part, :].T, own, 1, 0) + dot(embed_other[part, :].T, other_far, 1, 0)
+        terms = dot(embed_t[:, part], own, 1, 0) + dot(embed_other_t[:, part], other_far, 1, 0)
         if at == 0:
             running[...] = terms
         else:
@@ -308,8 +321,8 @@
     shares_near,
     shares_far,
     shares_other,
-    embed,
-    embed_other,
+    embed_t,
+    embed_other_t,
     query_pre,
     query_hidden,
     *refs,
@@ -325,7 +338,7 @@
         part = slice(at * step * tokens, (at + 1) * step * tokens)
         near = coefficients(dims, shares_near, own, weights, 0, at)
         other = coefficients(dims, shares_other, own, weights, passages, at)
-        terms = dot(embed[part, :].T, near, 1, 0) + dot(embed_other[part, :].T, other, 1, 0)
+        terms = dot(embed_t[:, part], near, 1, 0) + dot(embed_other_t[:, part], other, 1, 0)
         if at == 0:
             part_out[...] = terms
         else:
@@ -346,7 +359,7 @@
     projection,
     weight_out,
     grad_hidden_hbm,
-    running,
+    backs,
     grad_hidden,
     sems,
 ):
@@ -361,12 +374,8 @@
         copy = pltpu.make_async_copy(grad_hidden.at[rows], grad_hidden_hbm.at[rows], sems.at[at])
         copy.start()
         copies.append(copy)
-        terms = dot(back.T, hidden[part, :], 1, 0)
-        if at == 0:
-            running[...] = terms
-        else:
-            running[...] += terms
-    weight_out[...] = running[...].T
+        backs[:, part] = back.T
+    weight_out[...] = dot(backs[...], hidden[...], 1, 0).T
     for copy in copies:
         copy.wait()
 
@@ -466,25 +475,31 @@
         pairs = passage_count * tokens * query_rows
         return cost(2 * pairs * depth, pairs * 2, pairs)
 
-    shares_near, summed_near, gather, spread = pl.pallas_call(
+    shares_near, summed_near, embed_t, bias, gather = pl.pallas_call(
         functools.partial(near_kernel, dims),
         out_shape=(
             shape((passage_rows, rows), bf16),
             shape((passages, rows), f32),
+            shape((depth, passage_rows), bf16),
+            shape((passage_rows, lanes), bf16),
             shape((all_rows, pool_width), bf16),
-            shape((pool_width, all_rows), bf16),
         ),
         in_specs=[VMEM] * 2,
-        out_specs=(VMEM,) * 4,
+        out_specs=(VMEM,) * 5,
         compiler_params=params(16),
         cost_estimate=cost(5e10, 1e6),
         name="forward_near",
     )(embed, packed)
-    shares_other_near, summed_other = pl.pallas_call(
+    shares_other_near, summed_other, embed_other_t, bias_other = pl.pallas_call(
         functools.partial(other_kernel, dims),
-        out_shape=(shape((passage_rows, rows), bf16), shape((passages, rows), f32)),
+        out_shape=(
+            shape((passage_rows, rows), bf16),
+            shape((passages, rows), f32),
+            shape((depth, passage_rows), bf16),
+            shape((passage_rows, lanes), bf16),
+        ),
         in_specs=[VMEM] * 2,
-        out_specs=(VMEM,) * 2,
+        out_specs=(VMEM,) * 4,
         compiler_params=params(16),
         cost_estimate=forward_cost(passages, rows),
         name="forward_other",
@@ -498,7 +513,7 @@
             shape((3 * pair, pool_width), f32),
             shape((devices, packet_rows, pool_width), f32),
         ),
-        in_specs=[VMEM] * (blocks + 5),
+        in_specs=[VMEM] * (blocks + 7),
         out_specs=(VMEM,) * 5,
         scratch_shapes=[
             pltpu.VMEM((pair, all_rows), f32),
@@ -508,7 +523,16 @@
         compiler_params=params(32),
         cost_estimate=forward_cost(pair, far_rows),
         name="forward_far",
-    )(*queries, embed, embed_other, summed_near, summed_other, gather)
+    )(
+        *queries,
+        embed,
+        embed_other,
+        bias,
+        bias_other,
+        summed_near,
+        summed_other,
+        gather,
+    )
 
     packets = lax.all_to_all(packets, axes, 0, 0, tiled=True)
 
@@ -520,7 +544,7 @@
             shape((8, pool_width), f32),
             shape((passage_rows, depth), bf16),
         ),
-        in_specs=[VMEM] * (9 + blocks),
+        in_specs=[VMEM] * (8 + blocks),
         out_specs=(VMEM,) * (blocks + 2),
         scratch_shapes=[
             pltpu.VMEM((depth, far_rows), f32),
@@ -533,12 +557,11 @@
         packets,
         stats,
         inverse,
-        spread,
         shares_far,
         shares_other_near,
         shares_other_far,
-        embed,
-        embed_other,
+        embed_t,
+        embed_other_t,
         *queries,
     )
     grad_other = swap(grad_other, 1)
@@ -563,8 +586,8 @@
         shares_near,
         shares_far,
         shares_other_near,
-        embed,
-        embed_other,
+        embed_t,
+        embed_other_t,
         query_pre,
         query_flat,
         *queries,
@@ -576,7 +599,7 @@
         in_specs=[VMEM] * 5,
         out_specs=(VMEM, HBM),
         scratch_shapes=[
-            pltpu.VMEM((depth, width), f32),
+            pltpu.VMEM((depth, passage_rows), bf16),
             pltpu.VMEM((passage_rows, width), bf16),
             pltpu.SemaphoreType.DMA((passages // step,)),
         ],

time: 51.9 us -> 51.7 us (level)
  no operation moved by 1% of the time
where the time goes in v9:
time: 51.7 us; the launch traced here: 51.5 us
  blocking collectives  34.3 us (66%)
  Pallas kernels  11.3 us (22%)
  starting transfers between devices  4.09 us (8%)
  waiting for transfers between devices  1.1 us (2%)
  between operations  0.75 us (1%)
    all_to_all x1, blocking collectives, local(): packets = lax.all_to_all(packets, axes, 0, 0, tiled=True)  11.6 us
    all_to_all x1, blocking collectives, local(): weight = lax.all_to_all(weight, axes, 0, 0, tiled=True)  11.3 us
    all_to_all x1, blocking collectives, local(): copies = lax.all_to_all(copies, axes, 0, 0, tiled=True)  11.3 us
    ppermute x4, starting transfers between devices, swap(): return lax.ppermute(value, 'group', [(i, i ^ k) for i in range(groups)])  4.09 us
    pallas_call x1, Pallas kernels, local(): pl.pallas_call(functools.partial(passage_back_kernel, dims), out_shape=(s...  2.31 us
    pallas_call x1, Pallas kernels, local(): pl.pallas_call(query_kernel, out_shape=(shape((rows, depth), f32), shape(...  1.61 us
    pallas_call x1, Pallas kernels, local(): pl.pallas_call(functools.partial(far_grad_kernel, dims), out_shape=(*[sha...  1.23 us
    pallas_call x1, Pallas kernels, local(): pl.pallas_call(functools.partial(far_kernel, dims), out_shape=(shape((pas...  1.2 us
  transfers between devices with their start and end apart: 4, of which 2 were waited for; matrix products, arithmetic and copies ran while one was open for 0% of the time, Pallas kernels for 11%

profile of v9, /device:TPU:1, one launch (start us, length us, event | category | flops | bytes accessed | tf_op | source)
XLA Modules:
  0.0 51.5 jit_solution(318696846614102212)
XLA Ops:
  0.6 0.0 copy-start
  0.7 1.6 %query_embed.1 = (f32[256,128]{1,0:T(8,128)S(1)}, bf16[272,128]{1,0:T(8,128)(2,1)S(1)}, bf16[768,128]{1,0:T(8,128)(2,1)S(1)}) custom-call(bf16[256,768]{1,0:T(8,128)(2,1)} %bitcast.9, bf16[768,128]{1,0:T(8,128)(2,1)} %projection_hbm.1, s32[8,32]{1,0:T(8,128)} %ids_hbm.1, s32[8]{0:T(128)} %positive_hbm.1), custom_call_target="tpu_custom_call" | custom-call | flops 20000000000 | bytes 393216 | tf_op jit(solution)/shard_map/query_embed/pallas_call | solution.py:435
  2.3 2.1 %collective-permute-start = (bf16[272,128]{1,0:T(8,128)(2,1)S(1)}, bf16[272,128]{1,0:T(8,128)(2,1)S(1)}, u32[]{:S(2)}, u32[]{:S(2)}) collective-permute-start(bf16[272,128]{1,0:T(8,128)(2,1)S(1)} %get-tuple-element.38.packed.refs_0_), channel_id=1, source_target_pairs={{0,16},{8,24},{16,0},{24,8},{1,17},{9,25},{17,1},{25,9},{2,18},{10... | collective-permute-start | bytes 208904 | tf_op jit(solution)/shard_map/ppermute | solution.py:456
  4.4 0.0 copy-done.2
  4.4 1.1 %passage_embed.1 = (f32[2048,128]{1,0:T(8,128)S(1)}, bf16[2064,128]{1,0:T(8,128)(2,1)S(1)}) custom-call(s32[16]{0:T(128)S(1)} %copy-done.2, bf16[2048,768]{1,0:T(8,128)(2,1)S(1)} %bitcast.6, bf16[768,128]{1,0:T(8,128)(2,1)S(1)} %get-tuple-element.39.projection), custom_call_target="tpu_custom_call" | custom-call | flops 402653184 | bytes 4718592 | tf_op jit(solution)/shard_map/passage_embed/pallas_call | solution.py:460
  5.5 1.0 %collective-permute-start.1 = (bf16[2064,128]{1,0:T(8,128)(2,1)S(1)}, bf16[2064,128]{1,0:T(8,128)(2,1)S(1)}, u32[]{:S(2)}, u32[]{:S(2)}) collective-permute-start(bf16[2064,128]{1,0:T(8,128)(2,1)S(1)} %get-tuple-element.40.embed.refs_2_), channel_id=1, source_target_pairs={{0,8},{8,0},{16,24},{24,16},{1,9},{9,1},{17,25},{25,17},{2,10},{10... | collective-permute-start | bytes 1585160 | tf_op jit(solution)/shard_map/ppermute | solution.py:456
  6.5 0.7 %forward_near.1 = (bf16[2048,256]{1,0:T(8,128)(2,1)S(1)}, f32[16,256]{1,0:T(8,128)S(1)}, bf16[128,2048]{1,0:T(8,128)(2,1)S(1)}, bf16[2048,128]{1,0:T(8,128)(2,1)S(1)}, bf16[512,128]{1,0:T(8,128)(2,1)S(1)}) custom-call(bf16[2064,128]{1,0:T(8,128)(2,1)S(1)} %get-tuple-element.40.embed.refs_2_, bf16[272,128]{1,0:T(8,128)(2,1)S(1)} %get-tuple-element.38.packed.refs_0_), custom_call_target="tpu_custom_call" | custom-call | flops 49999998976 | bytes 1000000 | tf_op jit(solution)/shard_map/forward_near/pallas_call | solution.py:478
  7.2 0.9 %collective-permute-done.1.embed.refs_3_ = bf16[2064,128]{1,0:T(8,128)(2,1)S(1)} collective-permute-done((bf16[2064,128]{1,0:T(8,128)(2,1)S(1)}, bf16[2064,128]{1,0:T(8,128)(2,1)S(1)}, u32[]{:S(2)}, u32[]{:S(2)}) %collective-permute-start.1) | collective-permute-done | bytes 528416 | tf_op jit(solution)/shard_map/ppermute | solution.py:456
  8.0 0.7 %forward_other.1 = (bf16[2048,256]{1,0:T(8,128)(2,1)S(1)}, f32[16,256]{1,0:T(8,128)S(1)}, bf16[128,2048]{1,0:T(8,128)(2,1)S(1)}, bf16[2048,128]{1,0:T(8,128)(2,1)S(1)}) custom-call(bf16[2064,128]{1,0:T(8,128)(2,1)S(1)} %collective-permute-done.1.embed.refs_3_, bf16[272,128]{1,0:T(8,128)(2,1)S(1)} %get-tuple-element.38.packed.refs_0_), custom_call_target="tpu_custom_call" | custom-call | flops 134217728 | bytes 1048576 | tf_op jit(solution)/shard_map/forward_other/pallas_call | solution.py:493
  8.7 0.0 collective-permute-done.refs_1_
  8.7 0.0 copy-start.1
  8.7 1.2 %forward_far.1 = (bf16[2048,256]{1,0:T(8,128)(2,1)S(1)}, bf16[2048,256]{1,0:T(8,128)(2,1)S(1)}, f32[32,512]{1,0:T(8,128)S(1)}, f32[96,128]{1,0:T(8,128)S(1)}, f32[32,1,128]{2,1,0:T(1,128)S(1)}) custom-call(bf16[272,128]{1,0:T(8,128)(2,1)S(1)} %get-tuple-element.38.packed.refs_0_, bf16[272,128]{1,0:T(8,128)(2,1)S(1)} %collective-permute-done.refs_1_, ...), custom_call_target="tpu_custom_call" | custom-call | flops 268435456 | bytes 2097152 | tf_op jit(solution)/shard_map/forward_far/pallas_call | solution.py:507
  9.9 11.6 %all_to_all.15.packets = f32[32,1,128]{2,1,0:T(1,128)S(1)} all-to-all(f32[32,1,128]{2,1,0:T(1,128)S(1)} %get-tuple-element.46), channel_id=1, replica_groups=mesh['group'=4,'dp'=8] {'dp','group'}, dimensions={0} | all-to-all | bytes 32768 | tf_op jit(solution)/shard_map/all_to_all | solution.py:537
  21.5 1.2 %far_grads.1 = (bf16[128,256]{1,0:T(8,128)(2,1)S(1)}, f32[32,512]{1,0:T(8,128)S(1)}, f32[8,128]{1,0:T(8,128)S(1)}, bf16[2048,128]{1,0:T(8,128)(2,1)S(1)}) custom-call(f32[32,1,128]{2,1,0:T(1,128)S(1)} %all_to_all.15.packets, f32[96,128]{1,0:T(8,128)S(1)} %get-tuple-element.47.stats, f32[32,512]{1,0:T(8,128)S(1)} %get-tuple-element.48.inverse, ...), custom_call_target="tpu_custom_call" | custom-call | flops 536870912 | bytes 4194304 | tf_op jit(solution)/shard_map/far_grads/pallas_call | solution.py:539
  22.8 0.7 %collective-permute-start.2 = (bf16[2048,128]{1,0:T(8,128)(2,1)S(1)}, bf16[2048,128]{1,0:T(8,128)(2,1)S(1)}, u32[]{:S(2)}, u32[]{:S(2)}) collective-permute-start(bf16[2048,128]{1,0:T(8,128)(2,1)S(1)} %get-tuple-element.60), channel_id=1, source_target_pairs={{0,8},{8,0},{16,24},{24,16},{1,9},{9,1},{17,25},{25,17},{2,10},{10... | collective-permute-start | bytes 1572872 | tf_op jit(solution)/shard_map/ppermute | solution.py:456
  23.5 0.3 collective-permute-start.3
  23.7 1.0 %own_grads.1 = (f32[128,256]{1,0:T(8,128)S(1)}, f32[2048,128]{1,0:T(8,128)S(1)}, f32[128,256]{1,0:T(8,128)S(1)}, bf16[768,256]{1,0:T(8,128)(2,1)S(1)}) custom-call(f32[32,512]{1,0:T(8,128)S(1)} %get-tuple-element.54.weights, bf16[2048,256]{1,0:T(8,128)(2,1)S(1)} %get-tuple-element.55.shares_near, bf16[2048,256]{1,0:T(8,128)(2,1)S(1)} %get-tuple-element.49.shares_far, ...), custom_call_target="tpu_custom_call" | custom-call | flops 536870912 | bytes 4194304 | tf_op jit(solution)/shard_map/own_grads/pallas_call | solution.py:570
  24.8 0.2 collective-permute-done.2.grad_other
  25.0 2.3 %passage_back.1 = (f32[768,128]{1,0:T(8,128)S(1)}, bf16[2048,768]{1,0:T(8,128)(2,1)}) custom-call(f32[2048,128]{1,0:T(8,128)S(1)} %get-tuple-element.59.grad, bf16[2048,128]{1,0:T(8,128)(2,1)S(1)} %collective-permute-done.2.grad_other, f32[2048,128]{1,0:T(8,128)S(1)} %get-tuple-element.61.pre, bf16[2048,768]{1,0:T(8,128)(2,1)S(1)} %bitcast.7, ...), custom_call_target="tpu_custom_call" | custom-call | flops 805306368 | bytes 6291456 | tf_op jit(solution)/shard_map/passage_back/pallas_call | solution.py:596
  27.3 0.0 collective-permute-done.3.refs_0_
  27.3 0.3 query_back.1
  27.7 11.3 %all_to_all.16.parts = bf16[32,24,128]{2,1,0:T(8,128)(2,1)S(1)} all-to-all(bf16[32,24,128]{2,1,0:T(8,128)(2,1)S(1)} %bitcast.11), channel_id=1, replica_groups=mesh['group'=4,'dp'=8] {'dp','group'}, dimensions={0} | all-to-all | bytes 393216 | tf_op jit(solution)/shard_map/all_to_all | solution.py:623
  39.0 11.3 %all_to_all.17 = bf16[32,24,128]{2,1,0:T(8,128)(2,1)S(1)} all-to-all(bf16[32,24,128]{2,1,0:T(8,128)(2,1)S(1)} %sum_parts.1), channel_id=1, replica_groups=mesh['group'=4,'dp'=8] {'dp','group'}, dimensions={0} | all-to-all | bytes 393216 | tf_op jit(solution)/shard_map/all_to_all | solution.py:632
  50.3 1.1 %outputs.1 = (f32[768,128]{1,0:T(8,128)}, bf16[256,768]{1,0:T(8,128)(2,1)}, f32[8]{0:T(128)}) custom-call(bf16[768,128]{1,0:T(8,128)(2,1)S(1)} %bitcast.8, bf16[128,256]{1,0:T(8,128)(2,1)S(1)} %get-tuple-element.66.back, bf16[768,128]{1,0:T(8,128)(2,1)S(1)} %get-tuple-element.39.projection, f32[8,128]{1,0:T(8,128)S(1)} %get-tuple-element.67.losses), custom_call_target="tpu_custom_call" | custom-call | flops 50331648 | bytes 786432 | tf_op jit(solution)/shard_map/outputs/pallas_call | solution.py:633
  (4 shorter events, 0.1 us)
Async XLA Ops:
  0.6 3.7 %copy-start = (bf16[16,128,768]{2,1,0:T(8,128)(2,1)S(1)}, bf16[16,128,768]{2,1,0:T(8,128)(2,1)}, u32[]{:S(2)}) copy-start(bf16[16,128,768]{2,1,0:T(8,128)(2,1)} %param.7) | copy-start | bytes 9437188
  0.6 3.7 %copy-start.2 = (s32[16]{0:T(128)S(1)}, s32[16]{0:T(128)}, u32[]{:S(2)}) copy-start(s32[16]{0:T(128)} %lens.1) | copy-start | bytes 196
  2.3 6.4 %collective-permute-start = (bf16[272,128]{1,0:T(8,128)(2,1)S(1)}, bf16[272,128]{1,0:T(8,128)(2,1)S(1)}, u32[]{:S(2)}, u32[]{:S(2)}) collective-permute-start(bf16[272,128]{1,0:T(8,128)(2,1)S(1)} %get-tuple-element.38.packed.refs_0_), channel_id=1, source_target_pairs={{0,16},{8,24},{16,0},{24,8},{1,17},{9,25},{17,1},{25,9},{2,18},{10... | collective-permute-start | bytes 208904 | tf_op jit(solution)/shard_map/ppermute | solution.py:456
  5.5 2.6 %collective-permute-start.1 = (bf16[2064,128]{1,0:T(8,128)(2,1)S(1)}, bf16[2064,128]{1,0:T(8,128)(2,1)S(1)}, u32[]{:S(2)}, u32[]{:S(2)}) collective-permute-start(bf16[2064,128]{1,0:T(8,128)(2,1)S(1)} %get-tuple-element.40.embed.refs_2_), channel_id=1, source_target_pairs={{0,8},{8,0},{16,24},{24,16},{1,9},{9,1},{17,25},{25,17},{2,10},{10... | collective-permute-start | bytes 1585160 | tf_op jit(solution)/shard_map/ppermute | solution.py:456
  8.7 15.0 %copy-start.1 = (bf16[8,32,768]{2,1,0:T(8,128)(2,1)S(1)}, bf16[8,32,768]{2,1,0:T(8,128)(2,1)}, u32[]{:S(2)}) copy-start(bf16[8,32,768]{2,1,0:T(8,128)(2,1)} %param.6) | copy-start | bytes 1179652
  22.8 2.2 %collective-permute-start.2 = (bf16[2048,128]{1,0:T(8,128)(2,1)S(1)}, bf16[2048,128]{1,0:T(8,128)(2,1)S(1)}, u32[]{:S(2)}, u32[]{:S(2)}) collective-permute-start(bf16[2048,128]{1,0:T(8,128)(2,1)S(1)} %get-tuple-element.60), channel_id=1, source_target_pairs={{0,8},{8,0},{16,24},{24,16},{1,9},{9,1},{17,25},{25,17},{2,10},{10... | collective-permute-start | bytes 1572872 | tf_op jit(solution)/shard_map/ppermute | solution.py:456
  23.5 3.9 %collective-permute-start.3 = (bf16[128,256]{1,0:T(8,128)(2,1)S(1)}, bf16[128,256]{1,0:T(8,128)(2,1)S(1)}, u32[]{:S(2)}, u32[]{:S(2)}) collective-permute-start(bf16[128,256]{1,0:T(8,128)(2,1)S(1)} %get-tuple-element.63), channel_id=1, source_target_pairs={{0,16},{8,24},{16,0},{24,8},{1,17},{9,25},{17,1},{25,9},{2,18},{10... | collective-permute-start | bytes 196616 | tf_op jit(solution)/shard_map/ppermute | solution.py:456

commit v10 on v9

--- a/solution.py
+++ b/solution.py
@@ -170,7 +170,22 @@
                 )
 
 
-def near_kernel(dims, embed, packed, shares_out, summed_out, turned_out, bias_out, gather_out):
+def near_kernel(
+    dims,
+    embed,
+    packed,
+    query_pre,
+    query_hidden,
+    shares_out,
+    summed_out,
+    turned_out,
+    bias_out,
+    gather_out,
+    pre_out,
+    hidden_out,
+):
+    pre_out[...] = query_pre[...].T
+    hidden_out[...] = query_hidden[...].T
     fill_bias(dims, embed, bias_out)
     forward_part(dims, embed, bias_out, [packed], shares_out, summed_out, 0)
     turned_out[...] = embed[: turned_out.shape[1], :].T
@@ -323,13 +338,11 @@
     shares_other,
     embed_t,
     embed_other_t,
-    query_pre,
-    query_hidden,
     *refs,
 ):
     blocks, count, length, passages, tokens, slots, step = dims
     packed = refs[:blocks]
-    part_out, grad_out, pre_out, hidden_out, queries = refs[blocks:]
+    part_out, grad_out, queries = refs[blocks:]
     rows = count * length
     for k in range(1, blocks):
         queries[(k - 1) * rows : k * rows, :] = packed[k][:rows, :]
@@ -346,8 +359,6 @@
         grad_out[part, :] = dot(near, packed[0][:rows, :], 1, 0) + dot(
             coefficients(dims, shares_far, far, weights, 0, at), queries[...], 1, 0
         )
-    pre_out[...] = query_pre[...].T
-    hidden_out[...] = query_hidden[...].T
 
 
 def passage_back_kernel(
@@ -432,17 +443,17 @@
     passage_flat = passage_hidden.reshape(passage_rows, width)
     shape = jax.ShapeDtypeStruct
 
-    query_pre, packed, projection_near = pl.pallas_call(
+    query_pre, packed, projection_near, query_rows = pl.pallas_call(
         query_kernel,
         out_shape=(
             shape((rows, depth), f32),
             shape((rows + 16, depth), bf16),
             shape((width, depth), bf16),
+            shape((rows, width), bf16),
         ),
         in_specs=[HBM] * 4,
-        out_specs=(VMEM,) * 3,
+        out_specs=(VMEM,) * 4,
         scratch_shapes=[
-            pltpu.VMEM((rows, width), bf16),
             pltpu.VMEM((count, slots), jnp.int32),
             pltpu.SMEM((count,), jnp.int32),
             pltpu.SemaphoreType.DMA((4,)),
@@ -475,7 +486,7 @@
         pairs = passage_count * tokens * query_rows
         return cost(2 * pairs * depth, pairs * 2, pairs)
 
-    shares_near, summed_near, embed_t, bias, gather = pl.pallas_call(
+    shares_near, summed_near, embed_t, bias, gather, pre_t, hidden_t = pl.pallas_call(
         functools.partial(near_kernel, dims),
         out_shape=(
             shape((passage_rows, rows), bf16),
@@ -483,13 +494,15 @@
             shape((depth, passage_rows), bf16),
             shape((passage_rows, lanes), bf16),
             shape((all_rows, pool_width), bf16),
+            shape((depth, rows), f32),
+            shape((width, rows), bf16),
         ),
-        in_specs=[VMEM] * 2,
-        out_specs=(VMEM,) * 5,
+        in_specs=[VMEM] * 4,
+        out_specs=(VMEM,) * 7,
         compiler_params=params(16),
         cost_estimate=cost(5e10, 1e6),
         name="forward_near",
-    )(embed, packed)
+    )(embed, packed, query_pre, query_rows)
     shares_other_near, summed_other, embed_other_t, bias_other = pl.pallas_call(
         functools.partial(other_kernel, dims),
         out_shape=(
@@ -567,16 +580,14 @@
     grad_other = swap(grad_other, 1)
     far_parts = [swap(part, cores * (k + 1)) for k, part in enumerate(far_parts)]
 
-    own_part, grad_own, pre_t, hidden_t = pl.pallas_call(
+    own_part, grad_own = pl.pallas_call(
         functools.partial(own_grad_kernel, dims),
         out_shape=(
             shape((depth, rows), f32),
             shape((passage_rows, depth), f32),
-            shape((depth, rows), f32),
-            shape((width, rows), bf16),
         ),
-        in_specs=[VMEM] * (8 + blocks),
-        out_specs=(VMEM,) * 4,
+        in_specs=[VMEM] * (6 + blocks),
+        out_specs=(VMEM,) * 2,
         scratch_shapes=[pltpu.VMEM((far_rows, depth), bf16)],
         compiler_params=params(32),
         cost_estimate=forward_cost(pair, all_rows),
@@ -588,8 +599,6 @@
         shares_other_near,
         embed_t,
         embed_other_t,
-        query_pre,
-        query_flat,
         *queries,
     )
 

time: 51.7 us -> 51.7 us (level)
  no operation moved by 1% of the time
where the time goes in v10:
time: 51.7 us; the launch traced here: 51.5 us
  blocking collectives  34.3 us (66%)
  Pallas kernels  11.2 us (22%)
  starting transfers between devices  4.09 us (8%)
  waiting for transfers between devices  1.1 us (2%)
  between operations  0.74 us (1%)
    all_to_all x1, blocking collectives, local(): packets = lax.all_to_all(packets, axes, 0, 0, tiled=True)  11.6 us
    all_to_all x1, blocking collectives, local(): weight = lax.all_to_all(weight, axes, 0, 0, tiled=True)  11.4 us
    all_to_all x1, blocking collectives, local(): copies = lax.all_to_all(copies, axes, 0, 0, tiled=True)  11.3 us
    ppermute x4, starting transfers between devices, swap(): return lax.ppermute(value, 'group', [(i, i ^ k) for i in range(groups)])  4.09 us
    pallas_call x1, Pallas kernels, local(): pl.pallas_call(functools.partial(passage_back_kernel, dims), out_shape=(s...  2.28 us
    pallas_call x1, Pallas kernels, local(): pl.pallas_call(query_kernel, out_shape=(shape((rows, depth), f32), shape(...  1.61 us
    pallas_call x1, Pallas kernels, local(): pl.pallas_call(functools.partial(far_grad_kernel, dims), out_shape=(*[sha...  1.22 us
    pallas_call x1, Pallas kernels, local(): pl.pallas_call(functools.partial(far_kernel, dims), out_shape=(shape((pas...  1.2 us
  transfers between devices with their start and end apart: 4, of which 2 were waited for; matrix products, arithmetic and copies ran while one was open for 0% of the time, Pallas kernels for 11%

profile of v10, /device:TPU:1, one launch (start us, length us, event | category | flops | bytes accessed | tf_op | source)
XLA Modules:
  0.0 51.5 jit_solution(16521642883473442183)
XLA Ops:
  0.6 0.0 copy-start
  0.6 0.0 copy-start.1
  0.7 1.6 %query_embed.1 = (f32[256,128]{1,0:T(8,128)S(1)}, bf16[272,128]{1,0:T(8,128)(2,1)S(1)}, bf16[768,128]{1,0:T(8,128)(2,1)S(1)}, bf16[256,768]{1,0:T(8,128)(2,1)S(1)}) custom-call(bf16[256,768]{1,0:T(8,128)(2,1)} %bitcast.11, bf16[768,128]{1,0:T(8,128)(2,1)} %projection_hbm.1, s32[8,32]{1,0:T(8,128)} %ids_hbm.1, s32[8]{0:T(128)} %positive_hbm.1), custom_call_target="tpu_custom_call" | custom-call | flops 20000000000 | bytes 393216 | tf_op jit(solution)/shard_map/query_embed/pallas_call | solution.py:446
  2.3 2.1 %collective-permute-start = (bf16[272,128]{1,0:T(8,128)(2,1)S(1)}, bf16[272,128]{1,0:T(8,128)(2,1)S(1)}, u32[]{:S(2)}, u32[]{:S(2)}) collective-permute-start(bf16[272,128]{1,0:T(8,128)(2,1)S(1)} %get-tuple-element.41.packed.refs_0_), channel_id=1, source_target_pairs={{0,16},{8,24},{16,0},{24,8},{1,17},{9,25},{17,1},{25,9},{2,18},{10... | collective-permute-start | bytes 208904 | tf_op jit(solution)/shard_map/ppermute | solution.py:467
  4.4 0.0 copy-done
  4.4 1.1 %passage_embed.1 = (f32[2048,128]{1,0:T(8,128)S(1)}, bf16[2064,128]{1,0:T(8,128)(2,1)S(1)}) custom-call(s32[16]{0:T(128)S(1)} %copy-done.1, bf16[2048,768]{1,0:T(8,128)(2,1)S(1)} %bitcast.6, bf16[768,128]{1,0:T(8,128)(2,1)S(1)} %get-tuple-element.39.projection), custom_call_target="tpu_custom_call" | custom-call | flops 402653184 | bytes 4718592 | tf_op jit(solution)/shard_map/passage_embed/pallas_call | solution.py:471
  5.5 1.0 %collective-permute-start.1 = (bf16[2064,128]{1,0:T(8,128)(2,1)S(1)}, bf16[2064,128]{1,0:T(8,128)(2,1)S(1)}, u32[]{:S(2)}, u32[]{:S(2)}) collective-permute-start(bf16[2064,128]{1,0:T(8,128)(2,1)S(1)} %get-tuple-element.40.embed.refs_2_), channel_id=1, source_target_pairs={{0,8},{8,0},{16,24},{24,16},{1,9},{9,1},{17,25},{25,17},{2,10},{10... | collective-permute-start | bytes 1585160 | tf_op jit(solution)/shard_map/ppermute | solution.py:467
  6.5 0.7 %forward_near.1 = (bf16[2048,256]{1,0:T(8,128)(2,1)S(1)}, f32[16,256]{1,0:T(8,128)S(1)}, bf16[128,2048]{1,0:T(8,128)(2,1)S(1)}, bf16[2048,128]{1,0:T(8,128)(2,1)...) custom-call(bf16[2064,128]{1,0:T(8,128)(2,1)S(1)} %get-tuple-element.40.embed.refs_2_, ...), custom_call_target="tpu_custom_call" | custom-call | flops 49999998976 | bytes 1000000 | tf_op jit(solution)/shard_map/forward_near/pallas_call | solution.py:489
  7.2 0.8 %collective-permute-done.1.embed.refs_3_ = bf16[2064,128]{1,0:T(8,128)(2,1)S(1)} collective-permute-done((bf16[2064,128]{1,0:T(8,128)(2,1)S(1)}, bf16[2064,128]{1,0:T(8,128)(2,1)S(1)}, u32[]{:S(2)}, u32[]{:S(2)}) %collective-permute-start.1) | collective-permute-done | bytes 528416 | tf_op jit(solution)/shard_map/ppermute | solution.py:467
  8.0 0.7 %forward_other.1 = (bf16[2048,256]{1,0:T(8,128)(2,1)S(1)}, f32[16,256]{1,0:T(8,128)S(1)}, bf16[128,2048]{1,0:T(8,128)(2,1)S(1)}, bf16[2048,128]{1,0:T(8,128)(2,1)S(1)}) custom-call(bf16[2064,128]{1,0:T(8,128)(2,1)S(1)} %collective-permute-done.1.embed.refs_3_, bf16[272,128]{1,0:T(8,128)(2,1)S(1)} %get-tuple-element.41.packed.refs_0_), custom_call_target="tpu_custom_call" | custom-call | flops 134217728 | bytes 1048576 | tf_op jit(solution)/shard_map/forward_other/pallas_call | solution.py:506
  8.7 0.0 collective-permute-done.refs_1_
  8.7 1.2 %forward_far.1 = (bf16[2048,256]{1,0:T(8,128)(2,1)S(1)}, bf16[2048,256]{1,0:T(8,128)(2,1)S(1)}, f32[32,512]{1,0:T(8,128)S(1)}, f32[96,128]{1,0:T(8,128)S(1)}, f32[32,1,128]{2,1,0:T(1,128)S(1)}) custom-call(bf16[272,128]{1,0:T(8,128)(2,1)S(1)} %get-tuple-element.41.packed.refs_0_, bf16[272,128]{1,0:T(8,128)(2,1)S(1)} %collective-permute-done.refs_1_, ...), custom_call_target="tpu_custom_call" | custom-call | flops 268435456 | bytes 2097152 | tf_op jit(solution)/shard_map/forward_far/pallas_call | solution.py:520
  9.9 11.6 %all_to_all.15.packets = f32[32,1,128]{2,1,0:T(1,128)S(1)} all-to-all(f32[32,1,128]{2,1,0:T(1,128)S(1)} %get-tuple-element.51), channel_id=1, replica_groups=mesh['group'=4,'dp'=8] {'dp','group'}, dimensions={0} | all-to-all | bytes 32768 | tf_op jit(solution)/shard_map/all_to_all | solution.py:550
  21.5 1.2 %far_grads.1 = (bf16[128,256]{1,0:T(8,128)(2,1)S(1)}, f32[32,512]{1,0:T(8,128)S(1)}, f32[8,128]{1,0:T(8,128)S(1)}, bf16[2048,128]{1,0:T(8,128)(2,1)S(1)}) custom-call(f32[32,1,128]{2,1,0:T(1,128)S(1)} %all_to_all.15.packets, f32[96,128]{1,0:T(8,128)S(1)} %get-tuple-element.52.stats, f32[32,512]{1,0:T(8,128)S(1)} %get-tuple-element.53.inverse, ...), custom_call_target="tpu_custom_call" | custom-call | flops 536870912 | bytes 4194304 | tf_op jit(solution)/shard_map/far_grads/pallas_call | solution.py:552
  22.8 0.7 %collective-permute-start.2 = (bf16[2048,128]{1,0:T(8,128)(2,1)S(1)}, bf16[2048,128]{1,0:T(8,128)(2,1)S(1)}, u32[]{:S(2)}, u32[]{:S(2)}) collective-permute-start(bf16[2048,128]{1,0:T(8,128)(2,1)S(1)} %get-tuple-element.62), channel_id=1, source_target_pairs={{0,8},{8,0},{16,24},{24,16},{1,9},{9,1},{17,25},{25,17},{2,10},{10... | collective-permute-start | bytes 1572872 | tf_op jit(solution)/shard_map/ppermute | solution.py:467
  23.5 0.3 collective-permute-start.3
  23.7 1.0 %own_grads.1 = (f32[128,256]{1,0:T(8,128)S(1)}, f32[2048,128]{1,0:T(8,128)S(1)}) custom-call(f32[32,512]{1,0:T(8,128)S(1)} %get-tuple-element.59.weights, bf16[2048,256]{1,0:T(8,128)(2,1)S(1)} %get-tuple-element.60.shares_near, bf16[2048,256]{1,0:T(8,128)(2,1)S(1)} %get-tuple-element.54.shares_far, ...), custom_call_target="tpu_custom_call" | custom-call | flops 536870912 | bytes 4194304 | tf_op jit(solution)/shard_map/own_grads/pallas_call | solution.py:583
  24.7 0.3 collective-permute-done.2.grad_other
  25.0 2.3 %passage_back.1 = (f32[768,128]{1,0:T(8,128)S(1)}, bf16[2048,768]{1,0:T(8,128)(2,1)}) custom-call(f32[2048,128]{1,0:T(8,128)S(1)} %get-tuple-element.61.grad, bf16[2048,128]{1,0:T(8,128)(2,1)S(1)} %collective-permute-done.2.grad_other, f32[2048,128]{1,0:T(8,128)S(1)} %get-tuple-element.63.pre, bf16[2048,768]{1,0:T(8,128)(2,1)S(1)} %bitcast.7, ...), custom_call_target="tpu_custom_call" | custom-call | flops 805306368 | bytes 6291456 | tf_op jit(solution)/shard_map/passage_back/pallas_call | solution.py:605
  27.3 0.0 collective-permute-done.3.refs_0_
  27.3 0.3 query_back.1
  27.6 11.4 %all_to_all.16.parts = bf16[32,24,128]{2,1,0:T(8,128)(2,1)S(1)} all-to-all(bf16[32,24,128]{2,1,0:T(8,128)(2,1)S(1)} %bitcast.9), channel_id=1, replica_groups=mesh['group'=4,'dp'=8] {'dp','group'}, dimensions={0} | all-to-all | bytes 393216 | tf_op jit(solution)/shard_map/all_to_all | solution.py:632
  39.1 11.3 %all_to_all.17 = bf16[32,24,128]{2,1,0:T(8,128)(2,1)S(1)} all-to-all(bf16[32,24,128]{2,1,0:T(8,128)(2,1)S(1)} %sum_parts.1), channel_id=1, replica_groups=mesh['group'=4,'dp'=8] {'dp','group'}, dimensions={0} | all-to-all | bytes 393216 | tf_op jit(solution)/shard_map/all_to_all | solution.py:641
  50.4 1.1 %outputs.1 = (f32[768,128]{1,0:T(8,128)}, bf16[256,768]{1,0:T(8,128)(2,1)}, f32[8]{0:T(128)}) custom-call(bf16[768,128]{1,0:T(8,128)(2,1)S(1)} %bitcast.8, bf16[128,256]{1,0:T(8,128)(2,1)S(1)} %get-tuple-element.68.back, bf16[768,128]{1,0:T(8,128)(2,1)S(1)} %get-tuple-element.39.projection, f32[8,128]{1,0:T(8,128)S(1)} %get-tuple-element.69.losses), custom_call_target="tpu_custom_call" | custom-call | flops 50331648 | bytes 786432 | tf_op jit(solution)/shard_map/outputs/pallas_call | solution.py:642
  (2 shorter events, 0.1 us)
Async XLA Ops:
  0.6 3.8 %copy-start = (bf16[16,128,768]{2,1,0:T(8,128)(2,1)S(1)}, bf16[16,128,768]{2,1,0:T(8,128)(2,1)}, u32[]{:S(2)}) copy-start(bf16[16,128,768]{2,1,0:T(8,128)(2,1)} %param.7) | copy-start | bytes 9437188
  0.6 3.7 %copy-start.1 = (s32[16]{0:T(128)S(1)}, s32[16]{0:T(128)}, u32[]{:S(2)}) copy-start(s32[16]{0:T(128)} %lens.1) | copy-start | bytes 196
  2.3 6.4 %collective-permute-start = (bf16[272,128]{1,0:T(8,128)(2,1)S(1)}, bf16[272,128]{1,0:T(8,128)(2,1)S(1)}, u32[]{:S(2)}, u32[]{:S(2)}) collective-permute-start(bf16[272,128]{1,0:T(8,128)(2,1)S(1)} %get-tuple-element.41.packed.refs_0_), channel_id=1, source_target_pairs={{0,16},{8,24},{16,0},{24,8},{1,17},{9,25},{17,1},{25,9},{2,18},{10... | collective-permute-start | bytes 208904 | tf_op jit(solution)/shard_map/ppermute | solution.py:467
  5.5 2.6 %collective-permute-start.1 = (bf16[2064,128]{1,0:T(8,128)(2,1)S(1)}, bf16[2064,128]{1,0:T(8,128)(2,1)S(1)}, u32[]{:S(2)}, u32[]{:S(2)}) collective-permute-start(bf16[2064,128]{1,0:T(8,128)(2,1)S(1)} %get-tuple-element.40.embed.refs_2_), channel_id=1, source_target_pairs={{0,8},{8,0},{16,24},{24,16},{1,9},{9,1},{17,25},{25,17},{2,10},{10... | collective-permute-start | bytes 1585160 | tf_op jit(solution)/shard_map/ppermute | solution.py:467
  22.8 2.2 %collective-permute-start.2 = (bf16[2048,128]{1,0:T(8,128)(2,1)S(1)}, bf16[2048,128]{1,0:T(8,128)(2,1)S(1)}, u32[]{:S(2)}, u32[]{:S(2)}) collective-permute-start(bf16[2048,128]{1,0:T(8,128)(2,1)S(1)} %get-tuple-element.62), channel_id=1, source_target_pairs={{0,8},{8,0},{16,24},{24,16},{1,9},{9,1},{17,25},{25,17},{2,10},{10... | collective-permute-start | bytes 1572872 | tf_op jit(solution)/shard_map/ppermute | solution.py:467
  23.5 3.8 %collective-permute-start.3 = (bf16[128,256]{1,0:T(8,128)(2,1)S(1)}, bf16[128,256]{1,0:T(8,128)(2,1)S(1)}, u32[]{:S(2)}, u32[]{:S(2)}) collective-permute-start(bf16[128,256]{1,0:T(8,128)(2,1)S(1)} %get-tuple-element.65), channel_id=1, source_target_pairs={{0,16},{8,24},{16,0},{24,8},{1,17},{9,25},{17,1},{25,9},{2,18},{10... | collective-permute-start | bytes 196616 | tf_op jit(solution)/shard_map/ppermute | solution.py:467

commit v11 on v10

--- a/solution.py
+++ b/solution.py
@@ -192,10 +192,9 @@
     gather_out[...] = token_picks(dims, gather_out.shape[1])
 
 
-def other_kernel(dims, embed, packed, shares_out, summed_out, turned_out, bias_out):
+def other_kernel(dims, embed, packed, shares_out, summed_out, bias_out):
     fill_bias(dims, embed, bias_out)
     forward_part(dims, embed, bias_out, [packed], shares_out, summed_out, 0)
-    turned_out[...] = embed[: turned_out.shape[1], :].T
 
 
 def far_kernel(dims, *refs):
@@ -215,7 +214,6 @@
     summed[passages:, :rows] = summed_other[...]
     summed[:, rows:] = summed_far[...]
     total = summed[...]
-    inverse_out[...] = 1.0 / total
     width = marks.shape[0]
     scores = exact_dot(smooth_temp * jnp.log(total), gather[...])
     marks_t = marks[...].T
@@ -249,6 +247,7 @@
         packet = jnp.concatenate([plain, hard, kept, sums] * 2, axis=0)
     for k in range(packet_out.shape[0]):
         packet_out[k] = packet
+    inverse_out[...] = 1.0 / total
 
 
 def coefficients(dims, shares, columns, weights, first, at):
@@ -270,7 +269,7 @@
     shares_other_near,
     shares_other_far,
     embed_t,
-    embed_other_t,
+    embed_other,
     *refs,
 ):
     blocks, count, length, passages, tokens, slots, step = dims
@@ -319,7 +318,7 @@
         own = coefficients(dims, shares_far, far, weights, 0, at)
         other_near = coefficients(dims, shares_other_near, near, weights, passages, at)
         other_far = coefficients(dims, shares_other_far, far, weights, passages, at)
-        terms = dot(embed_t[:, part], own, 1, 0) + dot(embed_other_t[:, part], other_far, 1, 0)
+        terms = dot(embed_t[:, part], own, 1, 0) + dot(embed_other[part, :].T, other_far, 1, 0)
         if at == 0:
             running[...] = terms
         else:
@@ -337,7 +336,7 @@
     shares_far,
     shares_other,
     embed_t,
-    embed_other_t,
+    embed_other,
     *refs,
 ):
     blocks, count, length, passages, tokens, slots, step = dims
@@ -351,7 +350,7 @@
         part = slice(at * step * tokens, (at + 1) * step * tokens)
         near = coefficients(dims, shares_near, own, weights, 0, at)
         other = coefficients(dims, shares_other, own, weights, passages, at)
-        terms = dot(embed_t[:, part], near, 1, 0) + dot(embed_other_t[:, part], other, 1, 0)
+        terms = dot(embed_t[:, part], near, 1, 0) + dot(embed_other[part, :].T, other, 1, 0)
         if at == 0:
             part_out[...] = terms
         else:
@@ -503,16 +502,15 @@
         cost_estimate=cost(5e10, 1e6),
         name="forward_near",
     )(embed, packed, query_pre, query_rows)
-    shares_other_near, summed_other, embed_other_t, bias_other = pl.pallas_call(
+    shares_other_near, summed_other, bias_other = pl.pallas_call(
         functools.partial(other_kernel, dims),
         out_shape=(
             shape((passage_rows, rows), bf16),
             shape((passages, rows), f32),
-            shape((depth, passage_rows), bf16),
             shape((passage_rows, lanes), bf16),
         ),
         in_specs=[VMEM] * 2,
-        out_specs=(VMEM,) * 4,
+        out_specs=(VMEM,) * 3,
         compiler_params=params(16),
         cost_estimate=forward_cost(passages, rows),
         name="forward_other",
@@ -574,7 +572,7 @@
         shares_other_near,
         shares_other_far,
         embed_t,
-        embed_other_t,
+        embed_other,
         *queries,
     )
     grad_other = swap(grad_other, 1)
@@ -598,7 +596,7 @@
         shares_far,
         shares_other_near,
         embed_t,
-        embed_other_t,
+        embed_other,
         *queries,
     )
 

time: 51.7 us -> 51.6 us (level)
  no operation moved by 1% of the time
where the time goes in v11:
time: 51.6 us; the launch traced here: 51.4 us
  blocking collectives  34.3 us (66%)
  Pallas kernels  11.2 us (22%)
  starting transfers between devices  4.1 us (8%)
  waiting for transfers between devices  1.09 us (2%)
  between operations  0.74 us (1%)
    all_to_all x1, blocking collectives, local(): packets = lax.all_to_all(packets, axes, 0, 0, tiled=True)  11.6 us
    all_to_all x1, blocking collectives, local(): weight = lax.all_to_all(weight, axes, 0, 0, tiled=True)  11.3 us
    all_to_all x1, blocking collectives, local(): copies = lax.all_to_all(copies, axes, 0, 0, tiled=True)  11.3 us
    ppermute x4, starting transfers between devices, swap(): return lax.ppermute(value, 'group', [(i, i ^ k) for i in range(groups)])  4.1 us
    pallas_call x1, Pallas kernels, local(): pl.pallas_call(functools.partial(passage_back_kernel, dims), out_shape=(s...  2.29 us
    pallas_call x1, Pallas kernels, local(): pl.pallas_call(query_kernel, out_shape=(shape((rows, depth), f32), shape(...  1.61 us
    pallas_call x1, Pallas kernels, local(): pl.pallas_call(functools.partial(far_grad_kernel, dims), out_shape=(*[sha...  1.21 us
    pallas_call x1, Pallas kernels, local(): pl.pallas_call(functools.partial(far_kernel, dims), out_shape=(shape((pas...  1.19 us
  transfers between devices with their start and end apart: 4, of which 2 were waited for; matrix products, arithmetic and copies ran while one was open for 0% of the time, Pallas kernels for 11%

profile of v11, /device:TPU:1, one launch (start us, length us, event | category | flops | bytes accessed | tf_op | source)
XLA Modules:
  0.0 51.4 jit_solution(7716239168016036662)
XLA Ops:
  0.6 0.0 copy-start
  0.6 0.0 copy-start.1
  0.7 1.6 %query_embed.1 = (f32[256,128]{1,0:T(8,128)S(1)}, bf16[272,128]{1,0:T(8,128)(2,1)S(1)}, bf16[768,128]{1,0:T(8,128)(2,1)S(1)}, bf16[256,768]{1,0:T(8,128)(2,1)S(1)}) custom-call(bf16[256,768]{1,0:T(8,128)(2,1)} %bitcast.11, bf16[768,128]{1,0:T(8,128)(2,1)} %projection_hbm.1, s32[8,32]{1,0:T(8,128)} %ids_hbm.1, s32[8]{0:T(128)} %positive_hbm.1), custom_call_target="tpu_custom_call" | custom-call | flops 20000000000 | bytes 393216 | tf_op jit(solution)/shard_map/query_embed/pallas_call | solution.py:445
  2.3 2.1 %collective-permute-start = (bf16[272,128]{1,0:T(8,128)(2,1)S(1)}, bf16[272,128]{1,0:T(8,128)(2,1)S(1)}, u32[]{:S(2)}, u32[]{:S(2)}) collective-permute-start(bf16[272,128]{1,0:T(8,128)(2,1)S(1)} %get-tuple-element.40.packed.refs_0_), channel_id=1, source_target_pairs={{0,16},{8,24},{16,0},{24,8},{1,17},{9,25},{17,1},{25,9},{2,18},{10... | collective-permute-start | bytes 208904 | tf_op jit(solution)/shard_map/ppermute | solution.py:466
  4.4 0.0 copy-done
  4.4 1.1 %passage_embed.1 = (f32[2048,128]{1,0:T(8,128)S(1)}, bf16[2064,128]{1,0:T(8,128)(2,1)S(1)}) custom-call(s32[16]{0:T(128)S(1)} %copy-done.1, bf16[2048,768]{1,0:T(8,128)(2,1)S(1)} %bitcast.6, bf16[768,128]{1,0:T(8,128)(2,1)S(1)} %get-tuple-element.38.projection), custom_call_target="tpu_custom_call" | custom-call | flops 402653184 | bytes 4718592 | tf_op jit(solution)/shard_map/passage_embed/pallas_call | solution.py:470
  5.5 1.0 %collective-permute-start.1 = (bf16[2064,128]{1,0:T(8,128)(2,1)S(1)}, bf16[2064,128]{1,0:T(8,128)(2,1)S(1)}, u32[]{:S(2)}, u32[]{:S(2)}) collective-permute-start(bf16[2064,128]{1,0:T(8,128)(2,1)S(1)} %get-tuple-element.39.embed.refs_2_), channel_id=1, source_target_pairs={{0,8},{8,0},{16,24},{24,16},{1,9},{9,1},{17,25},{25,17},{2,10},{10... | collective-permute-start | bytes 1585160 | tf_op jit(solution)/shard_map/ppermute | solution.py:466
  6.5 0.7 %forward_near.1 = (bf16[2048,256]{1,0:T(8,128)(2,1)S(1)}, f32[16,256]{1,0:T(8,128)S(1)}, bf16[128,2048]{1,0:T(8,128)(2,1)S(1)}, bf16[2048,128]{1,0:T(8,128)(2,1)...) custom-call(bf16[2064,128]{1,0:T(8,128)(2,1)S(1)} %get-tuple-element.39.embed.refs_2_, ...), custom_call_target="tpu_custom_call" | custom-call | flops 49999998976 | bytes 1000000 | tf_op jit(solution)/shard_map/forward_near/pallas_call | solution.py:488
  7.2 0.8 %collective-permute-done.1.embed.refs_3_.embed_other = bf16[2064,128]{1,0:T(8,128)(2,1)S(1)} collective-permute-done((bf16[2064,128]{1,0:T(8,128)(2,1)S(1)}, bf16[2064,128]{1,0:T(8,128)(2,1)S(1)}, u32[]{:S(2)}, u32[]{:S(2)}) %collective-permute-start.1) | collective-permute-done | bytes 528416 | tf_op jit(solution)/shard_map/ppermute | solution.py:466
  8.0 0.6 %forward_other.1 = (bf16[2048,256]{1,0:T(8,128)(2,1)S(1)}, f32[16,256]{1,0:T(8,128)S(1)}, bf16[2048,128]{1,0:T(8,128)(2,1)S(1)}) custom-call(bf16[2064,128]{1,0:T(8,128)(2,1)S(1)} %collective-permute-done.1.embed.refs_3_.embed_other, bf16[272,128]{1,0:T(8,128)(2,1)S(1)} %get-tuple-element.40.packed.refs_0_), custom_call_target="tpu_custom_call" | custom-call | flops 134217728 | bytes 1048576 | tf_op jit(solution)/shard_map/forward_other/pallas_call | solution.py:505
  8.7 0.0 collective-permute-done.refs_1_
  8.7 1.2 %forward_far.1 = (bf16[2048,256]{1,0:T(8,128)(2,1)S(1)}, bf16[2048,256]{1,0:T(8,128)(2,1)S(1)}, f32[32,512]{1,0:T(8,128)S(1)}, f32[96,128]{1,0:T(8,128)S(1)}, f32[32,1,128]{2,1,0:T(1,128)S(1)}) custom-call(bf16[272,128]{1,0:T(8,128)(2,1)S(1)} %get-tuple-element.40.packed.refs_0_, bf16[272,128]{1,0:T(8,128)(2,1)S(1)} %collective-permute-done.refs_1_, ...), custom_call_target="tpu_custom_call" | custom-call | flops 268435456 | bytes 2097152 | tf_op jit(solution)/shard_map/forward_far/pallas_call | solution.py:518
  9.9 11.6 %all_to_all.15.packets = f32[32,1,128]{2,1,0:T(1,128)S(1)} all-to-all(f32[32,1,128]{2,1,0:T(1,128)S(1)} %get-tuple-element.50), channel_id=1, replica_groups=mesh['group'=4,'dp'=8] {'dp','group'}, dimensions={0} | all-to-all | bytes 32768 | tf_op jit(solution)/shard_map/all_to_all | solution.py:548
  21.5 1.2 %far_grads.1 = (bf16[128,256]{1,0:T(8,128)(2,1)S(1)}, f32[32,512]{1,0:T(8,128)S(1)}, f32[8,128]{1,0:T(8,128)S(1)}, bf16[2048,128]{1,0:T(8,128)(2,1)S(1)}) custom-call(f32[32,1,128]{2,1,0:T(1,128)S(1)} %all_to_all.15.packets, f32[96,128]{1,0:T(8,128)S(1)} %get-tuple-element.51.stats, f32[32,512]{1,0:T(8,128)S(1)} %get-tuple-element.52.inverse, ...), custom_call_target="tpu_custom_call" | custom-call | flops 536870912 | bytes 4194304 | tf_op jit(solution)/shard_map/far_grads/pallas_call | solution.py:550
  22.7 0.7 %collective-permute-start.2 = (bf16[2048,128]{1,0:T(8,128)(2,1)S(1)}, bf16[2048,128]{1,0:T(8,128)(2,1)S(1)}, u32[]{:S(2)}, u32[]{:S(2)}) collective-permute-start(bf16[2048,128]{1,0:T(8,128)(2,1)S(1)} %get-tuple-element.60), channel_id=1, source_target_pairs={{0,8},{8,0},{16,24},{24,16},{1,9},{9,1},{17,25},{25,17},{2,10},{10... | collective-permute-start | bytes 1572872 | tf_op jit(solution)/shard_map/ppermute | solution.py:466
  23.4 0.3 collective-permute-start.3
  23.7 1.0 %own_grads.1 = (f32[128,256]{1,0:T(8,128)S(1)}, f32[2048,128]{1,0:T(8,128)S(1)}) custom-call(f32[32,512]{1,0:T(8,128)S(1)} %get-tuple-element.57.weights, bf16[2048,256]{1,0:T(8,128)(2,1)S(1)} %get-tuple-element.58.shares_near, bf16[2048,256]{1,0:T(8,128)(2,1)S(1)} %get-tuple-element.53.shares_far, ...), custom_call_target="tpu_custom_call" | custom-call | flops 536870912 | bytes 4194304 | tf_op jit(solution)/shard_map/own_grads/pallas_call | solution.py:581
  24.7 0.3 collective-permute-done.2.grad_other
  25.0 2.3 %passage_back.1 = (f32[768,128]{1,0:T(8,128)S(1)}, bf16[2048,768]{1,0:T(8,128)(2,1)}) custom-call(f32[2048,128]{1,0:T(8,128)S(1)} %get-tuple-element.59.grad, bf16[2048,128]{1,0:T(8,128)(2,1)S(1)} %collective-permute-done.2.grad_other, f32[2048,128]{1,0:T(8,128)S(1)} %get-tuple-element.61.pre, bf16[2048,768]{1,0:T(8,128)(2,1)S(1)} %bitcast.7, ...), custom_call_target="tpu_custom_call" | custom-call | flops 805306368 | bytes 6291456 | tf_op jit(solution)/shard_map/passage_back/pallas_call | solution.py:603
  27.3 0.0 collective-permute-done.3.refs_0_
  27.3 0.3 query_back.1
  27.6 11.3 %all_to_all.16.parts = bf16[32,24,128]{2,1,0:T(8,128)(2,1)S(1)} all-to-all(bf16[32,24,128]{2,1,0:T(8,128)(2,1)S(1)} %bitcast.9), channel_id=1, replica_groups=mesh['group'=4,'dp'=8] {'dp','group'}, dimensions={0} | all-to-all | bytes 393216 | tf_op jit(solution)/shard_map/all_to_all | solution.py:630
  39.0 11.3 %all_to_all.17 = bf16[32,24,128]{2,1,0:T(8,128)(2,1)S(1)} all-to-all(bf16[32,24,128]{2,1,0:T(8,128)(2,1)S(1)} %sum_parts.1), channel_id=1, replica_groups=mesh['group'=4,'dp'=8] {'dp','group'}, dimensions={0} | all-to-all | bytes 393216 | tf_op jit(solution)/shard_map/all_to_all | solution.py:639
  50.3 1.1 %outputs.1 = (f32[768,128]{1,0:T(8,128)}, bf16[256,768]{1,0:T(8,128)(2,1)}, f32[8]{0:T(128)}) custom-call(bf16[768,128]{1,0:T(8,128)(2,1)S(1)} %bitcast.8, bf16[128,256]{1,0:T(8,128)(2,1)S(1)} %get-tuple-element.66.back, bf16[768,128]{1,0:T(8,128)(2,1)S(1)} %get-tuple-element.38.projection, f32[8,128]{1,0:T(8,128)S(1)} %get-tuple-element.67.losses), custom_call_target="tpu_custom_call" | custom-call | flops 50331648 | bytes 786432 | tf_op jit(solution)/shard_map/outputs/pallas_call | solution.py:640
  (2 shorter events, 0.1 us)
Async XLA Ops:
  0.6 3.8 %copy-start = (bf16[16,128,768]{2,1,0:T(8,128)(2,1)S(1)}, bf16[16,128,768]{2,1,0:T(8,128)(2,1)}, u32[]{:S(2)}) copy-start(bf16[16,128,768]{2,1,0:T(8,128)(2,1)} %param.7) | copy-start | bytes 9437188
  0.6 3.7 %copy-start.1 = (s32[16]{0:T(128)S(1)}, s32[16]{0:T(128)}, u32[]{:S(2)}) copy-start(s32[16]{0:T(128)} %lens.1) | copy-start | bytes 196
  2.3 6.4 %collective-permute-start = (bf16[272,128]{1,0:T(8,128)(2,1)S(1)}, bf16[272,128]{1,0:T(8,128)(2,1)S(1)}, u32[]{:S(2)}, u32[]{:S(2)}) collective-permute-start(bf16[272,128]{1,0:T(8,128)(2,1)S(1)} %get-tuple-element.40.packed.refs_0_), channel_id=1, source_target_pairs={{0,16},{8,24},{16,0},{24,8},{1,17},{9,25},{17,1},{25,9},{2,18},{10... | collective-permute-start | bytes 208904 | tf_op jit(solution)/shard_map/ppermute | solution.py:466
  5.5 2.6 %collective-permute-start.1 = (bf16[2064,128]{1,0:T(8,128)(2,1)S(1)}, bf16[2064,128]{1,0:T(8,128)(2,1)S(1)}, u32[]{:S(2)}, u32[]{:S(2)}) collective-permute-start(bf16[2064,128]{1,0:T(8,128)(2,1)S(1)} %get-tuple-element.39.embed.refs_2_), channel_id=1, source_target_pairs={{0,8},{8,0},{16,24},{24,16},{1,9},{9,1},{17,25},{25,17},{2,10},{10... | collective-permute-start | bytes 1585160 | tf_op jit(solution)/shard_map/ppermute | solution.py:466
  22.7 2.2 %collective-permute-start.2 = (bf16[2048,128]{1,0:T(8,128)(2,1)S(1)}, bf16[2048,128]{1,0:T(8,128)(2,1)S(1)}, u32[]{:S(2)}, u32[]{:S(2)}) collective-permute-start(bf16[2048,128]{1,0:T(8,128)(2,1)S(1)} %get-tuple-element.60), channel_id=1, source_target_pairs={{0,8},{8,0},{16,24},{24,16},{1,9},{9,1},{17,25},{25,17},{2,10},{10... | collective-permute-start | bytes 1572872 | tf_op jit(solution)/shard_map/ppermute | solution.py:466
  23.4 3.8 %collective-permute-start.3 = (bf16[128,256]{1,0:T(8,128)(2,1)S(1)}, bf16[128,256]{1,0:T(8,128)(2,1)S(1)}, u32[]{:S(2)}, u32[]{:S(2)}) collective-permute-start(bf16[128,256]{1,0:T(8,128)(2,1)S(1)} %get-tuple-element.63), channel_id=1, source_target_pairs={{0,16},{8,24},{16,0},{24,8},{1,17},{9,25},{17,1},{25,9},{2,18},{10... | collective-permute-start | bytes 196616 | tf_op jit(solution)/shard_map/ppermute | solution.py:466
